TPU v7x, 32 devices: a whole 2x2x4 slice. The times are simulated.
32 devices in a mesh: fsdp: 4 (over z), ctx: 8 (over y, x, core).
Axes of the slice: x: 2, y: 2, z: 4, core: 2. Of those that a mesh axis runs over, the one named last changes fastest.
Arguments:
- tokens: bfloat16 [8, 1024, 1088], P('fsdp', 'ctx'), may hold values from -6 to 6
- lengths: int32 [8], P('fsdp'), may hold values from 256 to 1024, as said below
- cotangent: bfloat16 [8, 1024, 1088], P('fsdp', 'ctx'), may hold values from -6 to 6
- ln_gain: bfloat16 [2, 2, 1088], P(None, None, 'fsdp'), may hold values from 0.25 to 1.75
- ln_bias: bfloat16 [2, 2, 1088], P(None, None, 'fsdp'), may hold values from -1.5 to 1.5
- w_qkv: bfloat16 [2, 1088, 3264], P(None, 'fsdp'), may hold values from -0.1875 to 0.1875
- b_qv: bfloat16 [2, 2, 1088], P(None, None, 'fsdp'), may hold values from -2.5 to 2.5
- w_out: bfloat16 [2, 1088, 1088], P(None, 'fsdp'), may hold values from -3 to 3
- b_out: bfloat16 [2, 1088], P(None, 'fsdp'), may hold values from -1.5 to 1.5
- w_up: bfloat16 [2, 1088, 4352], P(None, 'fsdp'), may hold values from -0.1875 to 0.1875
- b_up: bfloat16 [2, 4352], P(None, 'fsdp'), may hold values from -2.5 to 2.5
- w_down: bfloat16 [2, 4352, 1088], P(None, 'fsdp'), may hold values from -0.09375 to 0.09375
- b_down: bfloat16 [2, 1088], P(None, 'fsdp'), may hold values from -1.5 to 1.5
Outputs:
- activations: bfloat16 [8, 1024, 1088], P('fsdp', 'ctx')
- input_grad: float32 [8, 1024, 1088], P('fsdp', 'ctx')
- ln_gain_grad: float32 [2, 2, 1088], P(None, None, 'fsdp')
- ln_bias_grad: float32 [2, 2, 1088], P(None, None, 'fsdp')
- w_qkv_grad: float32 [2, 1088, 3264], P(None, 'fsdp')
- b_qv_grad: float32 [2, 2, 1088], P(None, None, 'fsdp')
- w_out_grad: float32 [2, 1088, 1088], P(None, 'fsdp')
- b_out_grad: float32 [2, 1088], P(None, 'fsdp')
- w_up_grad: float32 [2, 1088, 4352], P(None, 'fsdp')
- b_up_grad: float32 [2, 4352], P(None, 'fsdp')
- w_down_grad: float32 [2, 4352, 1088], P(None, 'fsdp')
- b_down_grad: float32 [2, 1088], P(None, 'fsdp')
Inputs may be any that keep to these rules, and one draw needn't show every extreme that they name: `lengths`: in each aligned group of 2 sequences (those of one index of fsdp), one sequence has all 1024 slots valid.
All inputs are finite; a program needn't handle non-finite values.
Results may differ from a plain program's by a relative error of at most 0.022.
Values may be sent and summed in bfloat16 or wider, within the bound.
A program may use at most 320 MiB of HBM per device.

v0:
```python
import jax
import jax.numpy as jnp
from jax import lax
from jax.sharding import PartitionSpec as P

HEAD_DIM = 64


def from_behind(block, axis, distance):
    devices = range(lax.axis_size(axis))
    route = [(i - distance, i) for i in devices if i - distance in devices]
    return lax.ppermute(block, axis, route)


def shifted(array, axis, by):
    devices = lax.axis_size(axis)
    return lax.ppermute(array, axis, [(i, (i + by) % devices) for i in range(devices)])


def normalize(values, scales, shifts):
    average = jnp.mean(values, axis=-1, keepdims=True)
    centred = values - average
    variance = jnp.mean(centred * centred, axis=-1, keepdims=True)
    return centred * lax.rsqrt(variance + 1e-05) * scales + shifts


def outer_sum(left_rows, right_rows):
    return lax.dot_general(
        left_rows, right_rows, (((0,), (0,)), ((), ())), preferred_element_type=jnp.float32
    )


def times_transpose(left_rows, weight_rows):
    return lax.dot_general(
        left_rows, weight_rows, (((1,), (1,)), ((), ())), preferred_element_type=jnp.float32
    )


def allowed_mask(positions, key_places, lengths):
    causal = (key_places[None, :] <= positions[:, None]) & (key_places[None, :] >= 0)
    inside = key_places[None, :] < lengths[:, None]
    return causal[None, None, :, :] & inside[:, None, None, :]


def attend_forward(queries, key_rows, value_rows, positions, lengths, score_scale):
    seq_count, row_count, head_count, head_width = queries.shape
    lowest = jnp.full((seq_count, head_count, row_count), -1e30, jnp.float32)
    key_part = lax.all_gather(key_rows, "ctx", axis=1, tiled=True)
    value_part = lax.all_gather(value_rows, "ctx", axis=1, tiled=True)
    key_places = jnp.arange(key_part.shape[1], dtype=jnp.int32)
    allowed = allowed_mask(positions, key_places, lengths)
    scores = (
        jnp.einsum("sqhe,skhe->shqk", queries, key_part, preferred_element_type=jnp.float32)
        * score_scale
    )
    scores = jnp.where(allowed, scores, -1e30)
    new_top = jnp.maximum(lowest, jnp.max(scores, axis=-1))
    exp_weights = jnp.where(allowed, jnp.exp(scores - new_top[..., None]), 0.0)
    running_total = jnp.sum(exp_weights, axis=-1)
    running_sum = jnp.einsum(
        "shqk,skhe->shqe",
        exp_weights.astype(jnp.bfloat16),
        value_part,
        preferred_element_type=jnp.float32,
    )
    output = jnp.transpose(running_sum / running_total[..., None], (0, 2, 1, 3))
    return (output, new_top + jnp.log(running_total))


def block_terms(
    queries,
    grad_out,
    log_total,
    delta_row,
    key_part,
    value_part,
    first_key,
    positions,
    lengths,
    score_scale,
):
    key_places = first_key + jnp.arange(key_part.shape[1], dtype=jnp.int32)
    allowed = allowed_mask(positions, key_places, lengths)
    scores = (
        jnp.einsum("sqhe,skhe->shqk", queries, key_part, preferred_element_type=jnp.float32)
        * score_scale
    )
    scores = jnp.where(allowed, scores, -1e30)
    probability = jnp.where(allowed, jnp.exp(scores - log_total[..., None]), 0.0)
    grad_probs = jnp.einsum(
        "sqhe,skhe->shqk", grad_out, value_part, preferred_element_type=jnp.float32
    )
    grad_scores = (probability * (grad_probs - delta_row[..., None])).astype(jnp.bfloat16)
    query_add = (
        jnp.einsum("shqk,skhe->sqhe", grad_scores, key_part, preferred_element_type=jnp.float32)
        * score_scale
    )
    key_add = (
        jnp.einsum("shqk,sqhe->skhe", grad_scores, queries, preferred_element_type=jnp.float32)
        * score_scale
    )
    value_add = jnp.einsum(
        "shqk,sqhe->skhe",
        probability.astype(jnp.bfloat16),
        grad_out,
        preferred_element_type=jnp.float32,
    )
    return (query_add, key_add, value_add)


def shards(
    tokens,
    lengths,
    cotangent,
    ln_gain,
    ln_bias,
    w_qkv,
    b_qv,
    w_out,
    b_out,
    w_up,
    b_up,
    w_down,
    b_down,
):
    seq_count, row_count, model_width = tokens.shape
    head_width = HEAD_DIM
    head_count = model_width // head_width
    score_scale = head_width ** (-0.5)
    ctx_count = lax.axis_size("ctx")
    ctx_index = lax.axis_index("ctx")
    positions = ctx_index * row_count + jnp.arange(row_count, dtype=jnp.int32)
    valid_rows = (positions[None, :] < lengths[:, None]).astype(jnp.float32)[..., None]
    flat_rows = seq_count * row_count
    split_shape = (seq_count, row_count, head_count, head_width)
    layer_total = ln_gain.shape[0]
    member_total = 10
    hidden = tokens.astype(jnp.float32).reshape(flat_rows, model_width)
    kept_layers = []
    for layer_index in range(layer_total):
        params = (
            lax.all_gather(ln_gain[layer_index], "fsdp", axis=1, tiled=True),
            lax.all_gather(ln_bias[layer_index], "fsdp", axis=1, tiled=True),
            lax.all_gather(w_qkv[layer_index], "fsdp", axis=0, tiled=True),
            lax.all_gather(b_qv[layer_index], "fsdp", axis=1, tiled=True),
            lax.all_gather(w_out[layer_index], "fsdp", axis=0, tiled=True),
            lax.all_gather(b_out[layer_index], "fsdp", axis=0, tiled=True),
            lax.all_gather(w_up[layer_index], "fsdp", axis=0, tiled=True),
            lax.all_gather(b_up[layer_index], "fsdp", axis=0, tiled=True),
            lax.all_gather(w_down[layer_index], "fsdp", axis=0, tiled=True),
            lax.all_gather(b_down[layer_index], "fsdp", axis=0, tiled=True),
        )
        (
            gain_rows,
            shift_rows,
            mix_weight,
            mix_bias,
            out_weight,
            out_bias,
            up_weight,
            up_bias,
            down_weight,
            down_bias,
        ) = params
        gain_rows = gain_rows.astype(jnp.float32)
        shift_rows = shift_rows.astype(jnp.float32)
        mix_bias = mix_bias.astype(jnp.float32)
        normed_first = normalize(hidden, gain_rows[0], shift_rows[0]).astype(jnp.bfloat16)
        mixed_rows = jnp.dot(normed_first, mix_weight, preferred_element_type=jnp.float32)
        queries = (
            (mixed_rows[:, :model_width] + mix_bias[0]).astype(jnp.bfloat16).reshape(split_shape)
        )
        key_rows = (
            mixed_rows[:, model_width : 2 * model_width].astype(jnp.bfloat16).reshape(split_shape)
        )
        value_rows = (
            (mixed_rows[:, 2 * model_width :] + mix_bias[1])
            .astype(jnp.bfloat16)
            .reshape(split_shape)
        )
        output, log_total = attend_forward(
            queries, key_rows, value_rows, positions, lengths, score_scale
        )
        output = output.reshape(flat_rows, model_width)
        attended = output.astype(jnp.bfloat16)
        middle = (
            hidden
            + jnp.dot(attended, out_weight, preferred_element_type=jnp.float32)
            + out_bias.astype(jnp.float32)
        )
        normed_second = normalize(middle, gain_rows[1], shift_rows[1]).astype(jnp.bfloat16)
        upper_pre = jnp.dot(
            normed_second, up_weight, preferred_element_type=jnp.float32
        ) + up_bias.astype(jnp.float32)
        active = jax.nn.gelu(upper_pre).astype(jnp.bfloat16)
        kept_layers.append(
            (
                hidden,
                normed_first,
                queries,
                key_rows,
                value_rows,
                output,
                log_total,
                attended,
                middle,
                normed_second,
                upper_pre,
                active,
            )
        )
        hidden = (
            middle
            + jnp.dot(active, down_weight, preferred_element_type=jnp.float32)
            + down_bias.astype(jnp.float32)
        )
    activations = (valid_rows * hidden.reshape(seq_count, row_count, model_width)).astype(
        jnp.bfloat16
    )
    grad_hidden = (cotangent.astype(jnp.float32) * valid_rows).reshape(flat_rows, model_width)
    grads_by_layer = [None] * layer_total
    for layer_index in reversed(range(layer_total)):
        (
            hidden_in,
            normed_first,
            queries,
            key_rows,
            value_rows,
            output,
            log_total,
            attended,
            middle,
            normed_second,
            upper_pre,
            active,
        ) = kept_layers[layer_index]
        params = (
            lax.all_gather(ln_gain[layer_index], "fsdp", axis=1, tiled=True),
            lax.all_gather(ln_bias[layer_index], "fsdp", axis=1, tiled=True),
            lax.all_gather(w_qkv[layer_index], "fsdp", axis=0, tiled=True),
            lax.all_gather(b_qv[layer_index], "fsdp", axis=1, tiled=True),
            lax.all_gather(w_out[layer_index], "fsdp", axis=0, tiled=True),
            lax.all_gather(b_out[layer_index], "fsdp", axis=0, tiled=True),
            lax.all_gather(w_up[layer_index], "fsdp", axis=0, tiled=True),
            lax.all_gather(b_up[layer_index], "fsdp", axis=0, tiled=True),
            lax.all_gather(w_down[layer_index], "fsdp", axis=0, tiled=True),
            lax.all_gather(b_down[layer_index], "fsdp", axis=0, tiled=True),
        )
        (
            gain_rows,
            shift_rows,
            mix_weight,
            mix_bias,
            out_weight,
            out_bias,
            up_weight,
            up_bias,
            down_weight,
            down_bias,
        ) = params
        gain_rows = gain_rows.astype(jnp.float32)
        shift_rows = shift_rows.astype(jnp.float32)
        grad_branch = grad_hidden.astype(jnp.bfloat16)
        down_bias_grad = jnp.sum(grad_branch.astype(jnp.float32), axis=0)
        down_grad = outer_sum(active, grad_branch)
        grad_active = times_transpose(grad_branch, down_weight)
        unused_gelu, gelu_pull = jax.vjp(jax.nn.gelu, upper_pre)
        grad_upper = gelu_pull(grad_active)[0].astype(jnp.bfloat16)
        up_bias_grad = jnp.sum(grad_upper.astype(jnp.float32), axis=0)
        up_grad = outer_sum(normed_second, grad_upper)
        grad_normed = times_transpose(grad_upper, up_weight)
        unused_norm, norm_pull = jax.vjp(normalize, middle, gain_rows[1], shift_rows[1])
        grad_middle, gain_second, shift_second = norm_pull(grad_normed)
        grad_middle = grad_middle + grad_hidden
        grad_attn = grad_middle.astype(jnp.bfloat16)
        out_bias_grad = jnp.sum(grad_attn.astype(jnp.float32), axis=0)
        out_grad = outer_sum(attended, grad_attn)
        grad_output = times_transpose(grad_attn, out_weight).astype(jnp.bfloat16)
        delta_row = jnp.transpose(
            jnp.sum((grad_output.astype(jnp.float32) * output).reshape(split_shape), axis=-1),
            (0, 2, 1),
        )
        grad_heads = grad_output.reshape(split_shape)
        zero_block = jnp.zeros(split_shape, jnp.float32)

        def pass_step(turn_index, state_now):
            key_part, value_part, key_grad, value_grad, query_grad = state_now
            source = ctx_index - turn_index
            query_add, key_add, value_add = block_terms(
                queries,
                grad_heads,
                log_total,
                delta_row,
                key_part,
                value_part,
                source * row_count,
                positions,
                lengths,
                score_scale,
            )
            key_part, value_part = from_behind((key_part, value_part), "ctx", 1)
            key_grad, value_grad = (
                shifted((key_grad + key_add).astype(jnp.bfloat16), "ctx", 1).astype(jnp.float32),
                shifted((value_grad + value_add).astype(jnp.bfloat16), "ctx", 1).astype(
                    jnp.float32
                ),
            )
            return (key_part, value_part, key_grad, value_grad, query_grad + query_add)

        final_state = lax.fori_loop(
            0, ctx_count, pass_step, (key_rows, value_rows, zero_block, zero_block, zero_block)
        )
        key_grad, value_grad, query_grad = (final_state[2], final_state[3], final_state[4])
        query_low = query_grad.reshape(flat_rows, model_width).astype(jnp.bfloat16)
        key_low = key_grad.reshape(flat_rows, model_width).astype(jnp.bfloat16)
        value_low = value_grad.reshape(flat_rows, model_width).astype(jnp.bfloat16)
        grad_mixed = jnp.concatenate([query_low, key_low, value_low], axis=1)
        mix_bias_grad = jnp.stack(
            [
                jnp.sum(query_low.astype(jnp.float32), axis=0),
                jnp.sum(value_low.astype(jnp.float32), axis=0),
            ]
        )
        mix_grad = outer_sum(normed_first, grad_mixed)
        grad_normed_first = times_transpose(grad_mixed, mix_weight)
        unused_first, first_pull = jax.vjp(normalize, hidden_in, gain_rows[0], shift_rows[0])
        grad_input, gain_first, shift_first = first_pull(grad_normed_first)
        grad_hidden = grad_input + grad_middle
        gain_grads = jnp.stack([gain_first, gain_second])
        shift_grads = jnp.stack([shift_first, shift_second])
        scattered = (
            lax.psum_scatter(
                gain_grads.astype(jnp.bfloat16), "fsdp", scatter_dimension=1, tiled=True
            ).astype(jnp.float32),
            lax.psum_scatter(
                shift_grads.astype(jnp.bfloat16), "fsdp", scatter_dimension=1, tiled=True
            ).astype(jnp.float32),
            lax.psum_scatter(
                mix_grad.astype(jnp.bfloat16), "fsdp", scatter_dimension=0, tiled=True
            ).astype(jnp.float32),
            lax.psum_scatter(
                mix_bias_grad.astype(jnp.bfloat16), "fsdp", scatter_dimension=1, tiled=True
            ).astype(jnp.float32),
            lax.psum_scatter(
                out_grad.astype(jnp.bfloat16), "fsdp", scatter_dimension=0, tiled=True
            ).astype(jnp.float32),
            lax.psum_scatter(
                out_bias_grad.astype(jnp.bfloat16), "fsdp", scatter_dimension=0, tiled=True
            ).astype(jnp.float32),
            lax.psum_scatter(
                up_grad.astype(jnp.bfloat16), "fsdp", scatter_dimension=0, tiled=True
            ).astype(jnp.float32),
            lax.psum_scatter(
                up_bias_grad.astype(jnp.bfloat16), "fsdp", scatter_dimension=0, tiled=True
            ).astype(jnp.float32),
            lax.psum_scatter(
                down_grad.astype(jnp.bfloat16), "fsdp", scatter_dimension=0, tiled=True
            ).astype(jnp.float32),
            lax.psum_scatter(
                down_bias_grad.astype(jnp.bfloat16), "fsdp", scatter_dimension=0, tiled=True
            ).astype(jnp.float32),
        )
        grads_by_layer[layer_index] = (
            lax.psum(scattered[0].astype(jnp.bfloat16), "ctx").astype(jnp.float32),
            lax.psum(scattered[1].astype(jnp.bfloat16), "ctx").astype(jnp.float32),
            lax.psum(scattered[2].astype(jnp.bfloat16), "ctx").astype(jnp.float32),
            lax.psum(scattered[3].astype(jnp.bfloat16), "ctx").astype(jnp.float32),
            lax.psum(scattered[4].astype(jnp.bfloat16), "ctx").astype(jnp.float32),
            lax.psum(scattered[5].astype(jnp.bfloat16), "ctx").astype(jnp.float32),
            lax.psum(scattered[6].astype(jnp.bfloat16), "ctx").astype(jnp.float32),
            lax.psum(scattered[7].astype(jnp.bfloat16), "ctx").astype(jnp.float32),
            lax.psum(scattered[8].astype(jnp.bfloat16), "ctx").astype(jnp.float32),
            lax.psum(scattered[9].astype(jnp.bfloat16), "ctx").astype(jnp.float32),
        )
    input_grad = grad_hidden.reshape(seq_count, row_count, model_width)
    stacked = tuple(
        (
            jnp.stack([grads_by_layer[layer_index][member] for layer_index in range(layer_total)])
            for member in range(member_total)
        )
    )
    return (activations, input_grad) + stacked


def solution(mesh):
    placed = (
        P("fsdp", "ctx", None),
        P("fsdp"),
        P("fsdp", "ctx", None),
        P(None, None, "fsdp"),
        P(None, None, "fsdp"),
        P(None, "fsdp", None),
        P(None, None, "fsdp"),
        P(None, "fsdp", None),
        P(None, "fsdp"),
        P(None, "fsdp", None),
        P(None, "fsdp"),
        P(None, "fsdp", None),
        P(None, "fsdp"),
    )
    return jax.shard_map(
        shards,
        mesh=mesh,
        in_specs=placed,
        out_specs=(
            P("fsdp", "ctx", None),
            P("fsdp", "ctx", None),
            P(None, None, "fsdp"),
            P(None, None, "fsdp"),
            P(None, "fsdp", None),
            P(None, None, "fsdp"),
            P(None, "fsdp", None),
            P(None, "fsdp"),
            P(None, "fsdp", None),
            P(None, "fsdp"),
            P(None, "fsdp", None),
            P(None, "fsdp"),
        ),
        check_vma=False,
    )
```

profile of v0, /device:TPU:9, one launch (start us, length us, event | category | flops | bytes accessed | tf_op | source)
XLA Modules:
  0.0 3048.3 jit_solution(10345598930125150074)
XLA Ops:
  28.4 22.0 all-gather.1
  69.8 18.0 slice_reduce_fusion.6
  87.9 64.7 %all-gather.41.cloned.1.call-done = bf16[1,1088,3264]{2,1,0:T(8,128)(2,1)} async-done(((bf16[1,272,3264]{2,1,0:T(8,128)(2,1)}), bf16[1,1088,3264]{2,1,0:T(8,128)(2,1)}) %all-gather.41.cloned.1.call-update) | async-done | bytes 7102480 | tf_op jit(solution)/shard_map/all_gather | solution.py:144
  273.3 17.8 slice_reduce_fusion
  325.3 141.2 %all-gather.45.cloned.1.call-done = bf16[1,1088,4352]{2,1,0:T(8,128)(2,1)} async-done(((bf16[1,272,4352]{2,1,0:T(8,128)(2,1)}), bf16[1,1088,4352]{2,1,0:T(8,128)(2,1)}) %all-gather.45.cloned.1.call-update) | async-done | bytes 9469968 | tf_op jit(solution)/shard_map/all_gather | solution.py:148
  475.5 167.6 %all-gather.47.cloned.1.call-done = bf16[1,4352,1088]{2,1,0:T(8,128)(2,1)} async-done(((bf16[1,1088,1088]{2,1,0:T(8,128)(2,1)}), bf16[1,4352,1088]{2,1,0:T(8,128)(2,1)}) %all-gather.47.cloned.1.call-update) | async-done | bytes 9469968 | tf_op jit(solution)/shard_map/all_gather | solution.py:150
  652.8 121.0 %all-gather.49.cloned.1.call-done = bf16[1,1088,3264]{2,1,0:T(8,128)(2,1)} async-done(((bf16[1,272,3264]{2,1,0:T(8,128)(2,1)}), bf16[1,1088,3264]{2,1,0:T(8,128)(2,1)}) %all-gather.49.cloned.1.call-update) | async-done | bytes 7102480 | tf_op jit(solution)/shard_map/all_gather | solution.py:144
  840.9 23.4 all-gather.39.cloned.1.call-done
  876.0 40.3 %all-gather.51.cloned.1.call-done = bf16[1,1088,1088]{2,1,0:T(8,128)(2,1)} async-done(((bf16[1,272,1088]{2,1,0:T(8,128)(2,1)}), bf16[1,1088,1088]{2,1,0:T(8,128)(2,1)}) %all-gather.51.cloned.1.call-update) | async-done | bytes 2367504 | tf_op jit(solution)/shard_map/all_gather | solution.py:146
  919.9 163.9 %all-gather.53.cloned.1.call-done = bf16[1,1088,4352]{2,1,0:T(8,128)(2,1)} async-done(((bf16[1,272,4352]{2,1,0:T(8,128)(2,1)}), bf16[1,1088,4352]{2,1,0:T(8,128)(2,1)}) %all-gather.53.cloned.1.call-update) | async-done | bytes 9469968 | tf_op jit(solution)/shard_map/all_gather | solution.py:148
  1092.8 167.6 %all-gather.55.cloned.1.call-done = bf16[1,4352,1088]{2,1,0:T(8,128)(2,1)} async-done(((bf16[1,1088,1088]{2,1,0:T(8,128)(2,1)}), bf16[1,4352,1088]{2,1,0:T(8,128)(2,1)}) %all-gather.55.cloned.1.call-update) | async-done | bytes 9469968 | tf_op jit(solution)/shard_map/all_gather | solution.py:150
  1284.9 267.4 %while.44 = (s32[]{:T(128)}, bf16[2,128,17,64]{1,3,2,0:T(8,128)(2,1)S(1)}, bf16[2,128,17,64]{1,3,2,0:T(8,128)(2,1)}, f32[2,128,17,64]{1,3,2,0:T(8,128)}, f32[2,1...) while((s32[]{:T(128)}, ...), condition=%wide.region_16.17_spmd.clone, body=%wide.region_15.16_spmd.clone.sunk | while | flops 364380928 | bytes 47486680 | solution.py:310
  1597.1 275.0 %while.45 = (s32[]{:T(128)}, bf16[2,128,17,64]{1,3,2,0:T(8,128)(2,1)S(1)}, bf16[2,128,17,64]{1,3,2,0:T(8,128)(2,1)}, f32[2,128,17,64]{1,3,2,0:T(8,128)}, f32[2,1...) while((s32[]{:T(128)}, ...), condition=%wide.region_23.24_spmd.clone, body=%wide.region_22.23_spmd.clone.sunk | while | flops 364380928 | bytes 47486680 | solution.py:310
  1935.9 82.5 %reduce-scatter.27.cloned.1.call-done = bf16[272,3264]{1,0:T(8,128)(2,1)} async-done(((bf16[1088,3264]{1,0:T(8,128)(2,1)}), bf16[272,3264]{1,0:T(8,128)(2,1)}) %reduce-scatter.27.cloned.1.call-update) | async-done | bytes 1775632 | tf_op jit(solution)/shard_map/reduce_scatter | solution.py:338
  2018.4 164.7 %reduce-scatter.35.cloned.1.call-done = bf16[272,4352]{1,0:T(8,128)(2,1)} async-done(((bf16[1088,4352]{1,0:T(8,128)(2,1)}), bf16[272,4352]{1,0:T(8,128)(2,1)}) %reduce-scatter.35.cloned.1.call-update) | async-done | bytes 2367504 | tf_op jit(solution)/shard_map/reduce_scatter | solution.py:350
  2183.1 173.9 %reduce-scatter.39.cloned.1.call-done = bf16[1088,1088]{1,0:T(8,128)(2,1)} async-done(((bf16[4352,1088]{1,0:T(8,128)(2,1)}), bf16[1088,1088]{1,0:T(8,128)(2,1)}) %reduce-scatter.39.cloned.1.call-update) | async-done | bytes 2367504 | tf_op jit(solution)/shard_map/reduce_scatter | solution.py:356
  2356.9 166.0 %reduce-scatter.37.cloned.1.call-done = bf16[272,4352]{1,0:T(8,128)(2,1)} async-done(((bf16[1088,4352]{1,0:T(8,128)(2,1)}), bf16[272,4352]{1,0:T(8,128)(2,1)}) %reduce-scatter.37.cloned.1.call-update) | async-done | bytes 2367504 | tf_op jit(solution)/shard_map/reduce_scatter | solution.py:350
  2522.9 174.4 %reduce-scatter.41.cloned.1.call-done = bf16[1088,1088]{1,0:T(8,128)(2,1)} async-done(((bf16[4352,1088]{1,0:T(8,128)(2,1)}), bf16[1088,1088]{1,0:T(8,128)(2,1)}) %reduce-scatter.41.cloned.1.call-update) | async-done | bytes 2367504 | tf_op jit(solution)/shard_map/reduce_scatter | solution.py:356
  2737.9 19.5 reduce-scatter.47.cloned.1.call-done
  2758.3 19.3 reduce-scatter.49.cloned.1.call-done
  2778.6 19.4 reduce-scatter.43.cloned.1.call-done
  2799.0 19.3 reduce-scatter.45.cloned.1.call-done
  2819.3 21.9 all-reduce.12
  2844.8 178.3 %all-reduce.18.cloned.1.call-done = (bf16[1,272,3264]{2,1,0:T(8,128)(2,1)}, bf16[1,272,3264]{2,1,0:T(8,128)(2,1)}, bf16[1,272,1088]{2,1,0:T(8,128)(2,1)}, bf16[1...) async-done(((bf16[1,272,3264]{2,1,0:T(8,128)(2,1)}, ...) | async-done | bytes 14204944 | tf_op jit(solution)/shard_map/psum | solution.py:366
  (970 shorter events, 1041.0 us)
Async XLA Ops:
  7.2 145.4 %all-gather.41.cloned.1.call-start = ((), (), s32[]{:S(2)}) async-start(), calls=%async_computation.26 | async-start | bytes 9052160 | tf_op jit(solution)/shard_map/all_gather | solution.py:144
  11.3 280.1 %all-gather.33.cloned.1.call-start = ((), (), s32[]{:S(2)}) async-start(), calls=%async_computation.14 | async-start | bytes 5013504 | tf_op jit(solution)/shard_map/all_gather | solution.py:48
  162.2 146.1 %all-gather.35.cloned.1.call-start = ((), (), s32[]{:S(2)}) async-start(), calls=%async_computation.15 | async-start | bytes 5013504 | tf_op jit(solution)/shard_map/all_gather | solution.py:49
  199.5 267.0 %all-gather.45.cloned.1.call-start = ((), (), s32[]{:S(2)}) async-start(), calls=%async_computation.28 | async-start | bytes 11837440 | tf_op jit(solution)/shard_map/all_gather | solution.py:148
  204.4 438.7 %all-gather.47.cloned.1.call-start = ((), (), s32[]{:S(2)}) async-start(), calls=%async_computation.29 | async-start | bytes 12533760 | tf_op jit(solution)/shard_map/all_gather | solution.py:150
  209.7 564.1 %all-gather.49.cloned.1.call-start = ((), (), s32[]{:S(2)}) async-start(), calls=%async_computation.30 | async-start | bytes 9052160 | tf_op jit(solution)/shard_map/all_gather | solution.py:144
  210.4 613.4 %all-gather.37.cloned.1.call-start = ((), (), s32[]{:S(2)}) async-start(), calls=%async_computation.16 | async-start | bytes 5013504 | tf_op jit(solution)/shard_map/all_gather | solution.py:48
  820.4 263.3 %all-gather.53.cloned.1.call-start = ((), (), s32[]{:S(2)}) async-start(), calls=%async_computation.32 | async-start | bytes 11837440 | tf_op jit(solution)/shard_map/all_gather | solution.py:148
  821.1 439.2 %all-gather.55.cloned.1.call-start = ((), (), s32[]{:S(2)}) async-start(), calls=%async_computation.33 | async-start | bytes 12533760 | tf_op jit(solution)/shard_map/all_gather | solution.py:150
  821.7 1114.1 %reduce-scatter.33.cloned.1.call-start = ((), (), s32[]{:S(2)}) async-start(), calls=%async_computation.21 | async-start | bytes 3133440 | tf_op jit(solution)/shard_map/reduce_scatter | solution.py:344
  1558.2 377.7 %reduce-scatter.31.cloned.1.call-start = ((), (), s32[]{:S(2)}) async-start(), calls=%async_computation.20 | async-start | bytes 3133440 | tf_op jit(solution)/shard_map/reduce_scatter | solution.py:344
  1581.6 354.2 %reduce-scatter.29.cloned.1.call-start = ((), (), s32[]{:S(2)}) async-start(), calls=%async_computation.19 | async-start | bytes 9052160 | tf_op jit(solution)/shard_map/reduce_scatter | solution.py:338
  1596.1 422.3 %reduce-scatter.27.cloned.1.call-start = ((), (), s32[]{:S(2)}) async-start(), calls=%async_computation.18 | async-start | bytes 9052160 | tf_op jit(solution)/shard_map/reduce_scatter | solution.py:338
  1883.2 299.8 %reduce-scatter.35.cloned.1.call-start = ((), (), s32[]{:S(2)}) async-start(), calls=%async_computation.22 | async-start | bytes 11837440 | tf_op jit(solution)/shard_map/reduce_scatter | solution.py:350
  1892.0 464.9 %reduce-scatter.39.cloned.1.call-start = ((), (), s32[]{:S(2)}) async-start(), calls=%async_computation.24 | async-start | bytes 12533760 | tf_op jit(solution)/shard_map/reduce_scatter | solution.py:356
  1903.2 619.7 %reduce-scatter.37.cloned.1.call-start = ((), (), s32[]{:S(2)}) async-start(), calls=%async_computation.23 | async-start | bytes 11837440 | tf_op jit(solution)/shard_map/reduce_scatter | solution.py:350
  1911.6 785.7 %reduce-scatter.41.cloned.1.call-start = ((), (), s32[]{:S(2)}) async-start(), calls=%async_computation.25 | async-start | bytes 12533760 | tf_op jit(solution)/shard_map/reduce_scatter | solution.py:356
  1922.9 801.6 %reduce-scatter.51.cloned.1.call-start = ((), (), s32[]{:S(2)}) async-start(), calls=%async_computation.38 | async-start | bytes 348160
  1924.4 812.6 %reduce-scatter.53.cloned.1.call-start = ((), (), s32[]{:S(2)}) async-start(), calls=%async_computation.39 | async-start | bytes 348160
  1931.1 826.3 %reduce-scatter.47.cloned.1.call-start = ((), (), s32[]{:S(2)}) async-start(), calls=%async_computation.36 | async-start | bytes 348160
  1932.1 845.5 %reduce-scatter.49.cloned.1.call-start = ((), (), s32[]{:S(2)}) async-start(), calls=%async_computation.37 | async-start | bytes 348160
  1933.7 864.3 %reduce-scatter.43.cloned.1.call-start = ((), (), s32[]{:S(2)}) async-start(), calls=%async_computation.34 | async-start | bytes 348160
  1934.8 883.6 %reduce-scatter.45.cloned.1.call-start = ((), (), s32[]{:S(2)}) async-start(), calls=%async_computation.35 | async-start | bytes 348160
  1935.8 1087.4 %all-reduce.18.cloned.1.call-start = ((), (), s32[]{:S(2)}) async-start(), calls=%async_computation.40 | async-start | bytes 29245440 | tf_op jit(solution)/shard_map/psum | solution.py:366
  (223 other events, 6822.1 us)
Sparse Core Ops, SparseCore 0:
  11.5 141.0 all-gather.40
  162.3 39.4 all-gather.32
  203.6 38.5 all-gather.34
  244.3 55.2 all-gather.42
  301.5 164.9 all-gather.44
  468.5 174.6 all-gather.46
  644.7 129.0 all-gather.48
  783.7 40.0 all-gather.36
  825.7 38.5 all-gather.38
  865.7 50.5 all-gather.50
  918.5 165.2 all-gather.52
  1085.7 174.6 all-gather.54
  1558.3 56.2 reduce-scatter.32
  1616.8 50.0 reduce-scatter.30
  1669.7 128.1 reduce-scatter.28
  1883.4 134.9 reduce-scatter.26
  2020.6 162.4 reduce-scatter.34
  2185.3 171.6 reduce-scatter.38
  2359.8 163.0 reduce-scatter.36
  2525.7 171.6 reduce-scatter.40
  2739.3 18.0 reduce-scatter.46
  2759.5 18.1 reduce-scatter.48
  2779.9 18.0 reduce-scatter.42
  2822.9 200.1 all-reduce.17
  (3 shorter events, 52.9 us)
where the time goes:
time: 3060 us; the launch traced here: 3050 us
  waiting for transfers between devices  2010 us (66%)
  matrix products  326 us (11%)
  starting transfers between devices  213 us (7%)
  local copies, waits for them, and re-layouts  209 us (7%)
  blocking collectives  139 us (5%)
  other arithmetic  127 us (4%)
    reduce_scatter x2, waiting for transfers between devices, shards(): lax.psum_scatter(down_grad.astype(jnp.bfloat16), 'fsdp', scatter_dimensio...  348 us
    all_gather x2, waiting for transfers between devices, shards(): lax.all_gather(w_down[layer_index], 'fsdp', axis=0, tiled=True)  335 us
    reduce_scatter x2, waiting for transfers between devices, shards(): lax.psum_scatter(up_grad.astype(jnp.bfloat16), 'fsdp', scatter_dimension=...  331 us
    all_gather x2, waiting for transfers between devices, shards(): lax.all_gather(w_up[layer_index], 'fsdp', axis=0, tiled=True)  305 us
    all_gather x2, waiting for transfers between devices, shards(): lax.all_gather(w_qkv[layer_index], 'fsdp', axis=0, tiled=True)  186 us
    psum x1, waiting for transfers between devices, shards(): lax.psum(scattered[2].astype(jnp.bfloat16), 'ctx').astype(jnp.float32)  178 us
    ppermute x32, starting transfers between devices, from_behind(): return lax.ppermute(block, axis, route)  114 us
    ppermute x32, starting transfers between devices, shifted(): lax.ppermute(array, axis, [(i, (i + by) % devices) for i in range(devices)])  98.1 us
  transfers between devices with their start and end apart: 91, of which 42 were waited for; matrix products, arithmetic and copies ran while one was open for 17% of the time, Pallas kernels for 0%

commit v1 on v0

v1 whole, which is shorter than its diff:
```python
import functools

import jax
import jax.numpy as jnp
from jax import lax
from jax.experimental import pallas as pl
from jax.experimental.pallas import tpu as pltpu
from jax.sharding import PartitionSpec as P

MESH = pl.DeviceIdType.MESH


class Place:
    def __init__(self):
        self.depth = lax.axis_size("fsdp")
        self.z = lax.axis_index("fsdp")
        self.c8 = lax.axis_index("ctx")
        self.core = lax.rem(self.c8, 2)
        self.p = self.c8 // 2
        self.px = lax.rem(self.p, 2)
        self.py = self.p // 2
        self.sib = {"ctx": self.c8 + 1 - 2 * self.core}
        self.x_dev = {"ctx": self.c8 + 2 - 4 * self.px}
        self.y_dev = {"ctx": self.c8 + 4 - 8 * self.py}
        self.p_x = self.p + 1 - 2 * self.px
        self.p_y = self.p + 2 - 4 * self.py
        self.p_d = 3 - self.p
        self.relay_from = self.p + (1 - self.core) * (1 - 2 * self.px) + self.core * (2 - 4 * self.py)
        self.relay_dev = {
            "ctx": self.c8 + (1 - self.core) * (4 - 8 * self.py) + self.core * (2 - 4 * self.px)
        }

    def up(self):
        return {"fsdp": self.z + 1}

    def down(self):
        return {"fsdp": self.z - 1}

    def greet(self):
        barrier = pltpu.get_barrier_semaphore()
        for device in (self.sib, self.x_dev, self.y_dev):
            pl.semaphore_signal(barrier, inc=1, device_id=device, device_id_type=MESH)

        @pl.when(self.z > 0)
        def _():
            pl.semaphore_signal(barrier, inc=1, device_id=self.down(), device_id_type=MESH)

        @pl.when(self.z < self.depth - 1)
        def _():
            pl.semaphore_signal(barrier, inc=1, device_id=self.up(), device_id_type=MESH)

        below = jnp.where(self.z > 0, 1, 0)
        above = jnp.where(self.z < self.depth - 1, 1, 0)
        pl.semaphore_wait(barrier, 3 + below + above)


def remote(src, dst, send_sem, recv_sem, device):
    return pltpu.make_async_remote_copy(
        src_ref=src, dst_ref=dst, send_sem=send_sem, recv_sem=recv_sem, device_id=device, device_id_type=MESH
    )


class Gather:
    def __init__(self, at, own, whole, left_core, send, recv):
        self.at, self.own, self.whole = at, own, whole
        self.send, self.recv = send, recv
        rows = own.shape[0]
        unit = rows // 17
        self.t1 = 2 * unit
        self.block = 8 * unit
        self.rest = pl.ds(16 * unit, unit)
        self.has_rest = at.core == left_core

    def t1_rows(self, p, core=None):
        core = self.at.core if core is None else core
        return pl.ds(pl.multiple_of(core * self.block + p * self.t1, 16), self.t1)

    def block_rows(self, core):
        return pl.ds(pl.multiple_of(core * self.block, 16), self.block)

    def copy(self, kind, shard, rows, device, src=None, second=False):
        depth = self.at.depth
        slot = kind * depth + shard
        src = self.whole.at[shard, rows] if src is None else src
        send = self.send.at[(8 * depth + kind) if second else slot]
        return remote(src, self.whole.at[shard, rows], send, self.recv.at[slot], device)

    def start(self):
        at = self.at
        mine = self.t1_rows(at.p)

        @pl.when(at.z < at.depth - 1)
        def _():
            self.copy(0, at.z, mine, at.up(), self.own.at[mine]).start()

            @pl.when(self.has_rest)
            def _():
                self.copy(1, at.z, self.rest, at.up(), self.own.at[self.rest]).start()

        @pl.when(at.z > 0)
        def _():
            self.copy(0, at.z, mine, at.down(), self.own.at[mine], True).start()

            @pl.when(self.has_rest)
            def _():
                self.copy(1, at.z, self.rest, at.down(), self.own.at[self.rest], True).start()

    def cases(self, step, do):
        at = self.at

        @pl.when(at.z - 1 - step >= 0)
        def _():
            do(at.z - 1 - step, at.z < at.depth - 1, at.up())

        @pl.when(at.z + 1 + step < at.depth)
        def _():
            do(at.z + 1 + step, at.z > 0, at.down())

    def arrive(self, step):
        at = self.at
        mine = self.t1_rows(at.p)

        def do(shard, onward, device):
            self.copy(0, shard, mine, at.sib).wait_recv()

            @pl.when(onward)
            def _():
                self.copy(0, shard, mine, device).start()

            self.copy(2, shard, mine, at.x_dev).start()
            self.copy(3, shard, mine, at.y_dev).start()

            @pl.when(self.has_rest)
            def _():
                self.copy(1, shard, self.rest, at.sib).wait_recv()

                @pl.when(onward)
                def _():
                    self.copy(1, shard, self.rest, device).start()

                self.copy(5, shard, self.rest, at.sib).start()

        self.cases(step, do)

    def plane(self, step):
        at = self.at

        def do(shard, onward, device):
            self.copy(2, shard, self.t1_rows(at.p_x), at.sib).wait_recv()
            self.copy(3, shard, self.t1_rows(at.p_y), at.sib).wait_recv()
            self.copy(4, shard, self.t1_rows(at.relay_from), at.relay_dev).start()

        self.cases(step, do)

    def share(self, step):
        at = self.at

        def do(shard, onward, device):
            self.copy(4, shard, self.t1_rows(at.p_d), at.sib).wait_recv()
            self.copy(6, shard, self.block_rows(at.core), at.sib).start()

        self.cases(step, do)

    def finish(self):
        at = self.at
        mine = self.t1_rows(at.p)

        def do(shard, onward, device):
            self.copy(6, shard, self.block_rows(1 - at.core), at.sib).wait_recv()

            @pl.when(jnp.logical_not(self.has_rest))
            def _():
                self.copy(5, shard, self.rest, at.sib).wait_recv()

        for step in range(at.depth - 1):
            self.cases(step, do)

    def drain(self):
        at = self.at
        mine = self.t1_rows(at.p)

        @pl.when(at.z < at.depth - 1)
        def _():
            self.copy(0, at.z, mine, at.up(), self.own.at[mine]).wait_send()

            @pl.when(self.has_rest)
            def _():
                self.copy(1, at.z, self.rest, at.up(), self.own.at[self.rest]).wait_send()

        @pl.when(at.z > 0)
        def _():
            self.copy(0, at.z, mine, at.down(), self.own.at[mine], True).wait_send()

            @pl.when(self.has_rest)
            def _():
                self.copy(1, at.z, self.rest, at.down(), self.own.at[self.rest], True).wait_send()

        def do(shard, onward, device):
            @pl.when(onward)
            def _():
                self.copy(0, shard, mine, device).wait_send()

                @pl.when(self.has_rest)
                def _():
                    self.copy(1, shard, self.rest, device).wait_send()

            self.copy(2, shard, mine, at.x_dev).wait_send()
            self.copy(3, shard, mine, at.y_dev).wait_send()
            self.copy(4, shard, self.t1_rows(at.relay_from), at.relay_dev).wait_send()
            self.copy(6, shard, self.block_rows(at.core), at.sib).wait_send()

            @pl.when(self.has_rest)
            def _():
                self.copy(5, shard, self.rest, at.sib).wait_send()

        for step in range(at.depth - 1):
            self.cases(step, do)


def gather_kernel(count, *refs):
    owns, small = refs[:count], refs[count]
    wholes, small_all = refs[count + 1 : 2 * count + 1], refs[2 * count + 1]
    send, recv, own_sem, small_send, small_recv = refs[2 * count + 2 : 2 * count + 7]
    stages = refs[2 * count + 7 :]
    at = Place()
    depth = at.depth
    at.greet()
    items = [
        Gather(at, owns[k], wholes[k], k % 2, send.at[k], recv.at[k]) for k in range(count)
    ]
    loads = [pltpu.make_async_copy(owns[k], stages[k], own_sem.at[0, k]) for k in range(count)]
    loads.append(pltpu.make_async_copy(small, stages[count], own_sem.at[0, count]))
    stores = [
        pltpu.make_async_copy(stages[k], wholes[k].at[at.z], own_sem.at[1, k]) for k in range(count)
    ]
    stores.append(pltpu.make_async_copy(stages[count], small_all.at[at.z], own_sem.at[1, count]))

    def small_copy(shard, device, src=None, second=False):
        return remote(
            small_all.at[shard] if src is None else src,
            small_all.at[shard],
            small_send.at[depth if second else shard],
            small_recv.at[shard],
            device,
        )

    @pl.when(at.z < depth - 1)
    def _():
        small_copy(at.z, at.up(), small).start()

    @pl.when(at.z > 0)
    def _():
        small_copy(at.z, at.down(), small, True).start()

    steps = depth - 1
    items[0].start()
    for copy in loads:
        copy.start()

    def small_do(shard, onward, device):
        small_copy(shard, at.sib).wait_recv()

        @pl.when(onward)
        def _():
            small_copy(shard, device).start()

    for k in range(count):
        if k == 0:
            for step in range(steps):
                items[0].arrive(step)
            for load, store in zip(loads, stores):
                load.wait()
                store.start()
        if k == 0:
            for step in range(steps):
                items[0].cases(step, small_do)
        if k + 1 < count:
            items[k + 1].start()
        for step in range(steps):
            items[k].plane(step)
            if k + 1 < count:
                items[k + 1].arrive(step)
            items[k].share(step)
    for item in items:
        item.finish()
    for copy in stores:
        copy.wait()
    for item in items:
        item.drain()

    @pl.when(at.z < depth - 1)
    def _():
        small_copy(at.z, at.up(), small).wait_send()

    @pl.when(at.z > 0)
    def _():
        small_copy(at.z, at.down(), small, True).wait_send()

    def small_end(shard, onward, device):
        @pl.when(onward)
        def _():
            small_copy(shard, device).wait_send()

    for step in range(steps):
        items[0].cases(step, small_end)


def gather_weights(owns, small):
    depth = lax.axis_size("fsdp")
    count = len(owns)
    any_spec = pl.BlockSpec(memory_space=pl.ANY)
    shapes = [jax.ShapeDtypeStruct((depth,) + item.shape, item.dtype) for item in list(owns) + [small]]
    return pl.pallas_call(
        functools.partial(gather_kernel, count),
        out_shape=shapes,
        in_specs=[any_spec] * (count + 1),
        out_specs=[any_spec] * (count + 1),
        scratch_shapes=[
            pltpu.SemaphoreType.DMA((count, 8 * depth + 8)),
            pltpu.SemaphoreType.DMA((count, 8 * depth)),
            pltpu.SemaphoreType.DMA((2, count + 1)),
            pltpu.SemaphoreType.DMA((depth + 1,)),
            pltpu.SemaphoreType.DMA((depth,)),
        ]
        + [pltpu.VMEM(item.shape, item.dtype) for item in list(owns) + [small]],
        compiler_params=pltpu.CompilerParams(
            collective_id=0, has_side_effects=True, vmem_limit_bytes=40 * 1024 * 1024
        ),
    )(*owns, small)


def both(*conds):
    conds = [c for c in conds if c is not None]
    if not conds:
        return None
    total = conds[0]
    for c in conds[1:]:
        total = jnp.logical_and(total, c)
    return total


def under(cond, do):
    if cond is None:
        do()
    else:
        pl.when(cond)(do)


def add_rows(acc, extra, rows):
    def step(i, carry):
        piece = pl.ds(pl.multiple_of(i * 16, 16), 16)
        acc[piece, :] = acc[piece, :] + extra[piece, :]
        return carry

    lax.fori_loop(0, rows // 16, step, 0)


def add_rows_two(acc, one, two, rows):
    def step(i, carry):
        piece = pl.ds(pl.multiple_of(i * 16, 16), 16)
        total = acc[piece, :].astype(jnp.float32) + one[piece, :].astype(jnp.float32)
        acc[piece, :] = (total + two[piece, :].astype(jnp.float32)).astype(jnp.bfloat16)
        return carry

    lax.fori_loop(0, rows // 16, step, 0)


class Geometry:
    def __init__(self, rows, cols, line_part):
        self.rows, self.cols = rows, cols
        unit = rows // 17
        self.unit = unit
        self.block = 8 * unit
        self.t2 = line_part
        self.t1 = 2 * unit - line_part

    def scratch(self, depth):
        cols = self.cols
        vm = lambda *shape: pltpu.VMEM(shape + (cols,), jnp.bfloat16)
        out = [
            vm(depth, self.block),
            vm(depth, self.block),
            vm(3, depth, self.t1),
            vm(depth + 1, self.t1),
            vm(depth, self.unit),
            vm(depth + 1, self.unit),
            vm(depth, self.unit),
            vm(2, self.unit),
        ]
        if self.t2:
            out += [vm(depth + 1, 4 * self.t2), vm(3, self.t2)]
        return out


SLOTS = 48


class Reduce:
    def __init__(self, at, geo, part, out, left_core, bufs, send, recv, local):
        self.at, self.geo, self.part, self.out = at, geo, part, out
        self.acc, self.sib_in, self.plane_in, self.z_in, self.racc, self.rz_in, self.rsib_in, self.rplane_in = bufs[:8]
        if geo.t2:
            self.z2_in, self.plane2_in = bufs[8:]
        self.send, self.recv, self.local = send, recv, local
        self.has_rest = at.core == left_core
        self.no_rest = at.core != left_core
        self.rest = pl.ds(16 * geo.unit, geo.unit)
        self.names, self.posts = {}, []
        core, p = at.core, at.p
        self.direct_p = p + (1 - core) * (2 - 4 * at.py) + core * (1 - 2 * at.px)
        self.owner_dev = {
            "ctx": at.c8 + (1 - core) * (2 - 4 * at.px) + core * (4 - 8 * at.py)
        }

    def slot(self, name):
        return self.names.setdefault(name, len(self.names))

    def make(self, name, src, dst, device):
        i = self.slot(name)
        return remote(src, dst, self.send.at[i], self.recv.at[i], device)

    def post(self, name, src, dst, device, cond=None):
        under(cond, lambda: self.make(name, src, dst, device).start())
        self.posts.append((name, src, dst, device, cond))

    def take(self, name, dst, cond=None):
        under(cond, lambda: self.make(name, dst, dst, self.at.sib).wait_recv())

    def c1(self, p):
        return pl.ds(pl.multiple_of(p * self.geo.t1, 16), self.geo.t1)

    def c2(self, p):
        return pl.ds(pl.multiple_of(4 * self.geo.t1 + p * self.geo.t2, 16), self.geo.t2)

    def o1(self, p, core):
        return pl.ds(pl.multiple_of(core * self.geo.block + p * self.geo.t1, 16), self.geo.t1)

    def o2(self, p, core):
        return pl.ds(
            pl.multiple_of(core * self.geo.block + 4 * self.geo.t1 + p * self.geo.t2, 16), self.geo.t2
        )

    def begin(self):
        at, geo = self.at, self.geo
        mine = pl.ds(pl.multiple_of(at.core * geo.block, 16), geo.block)
        other = pl.ds(pl.multiple_of((1 - at.core) * geo.block, 16), geo.block)
        self.post("sib", self.part.at[:, other], self.sib_in, at.sib)
        self.post("rsib", self.part.at[:, self.rest], self.rsib_in, at.sib, self.no_rest)
        self.load = pltpu.make_async_copy(self.part.at[:, mine], self.acc, self.local.at[0])
        self.load.start()
        self.rload = pltpu.make_async_copy(self.part.at[:, self.rest], self.racc, self.local.at[1])
        pl.when(self.has_rest)(lambda: self.rload.start())

    def cores(self):
        at, geo = self.at, self.geo
        self.load.wait()
        self.take("sib", self.sib_in)
        for t in range(at.depth):
            add_rows(self.acc.at[t], self.sib_in.at[t], geo.block)
        self.post("diag", self.acc.at[:, self.c1(at.p_d)], self.plane_in.at[0], at.relay_dev)
        self.post("near", self.acc.at[:, self.c1(self.direct_p)], self.plane_in.at[1], at.relay_dev)

        def rest():
            self.rload.wait()
            self.make("rsib", self.rsib_in, self.rsib_in, at.sib).wait_recv()
            for t in range(at.depth):
                add_rows(self.racc.at[t], self.rsib_in.at[t], geo.unit)

        pl.when(self.has_rest)(rest)

    def line(self, step, name, acc, landing, rows, cond=None):
        at = self.at
        last = at.depth - 1
        right, left = last - step, step

        def go_right():
            @pl.when(at.z > 0)
            def _():
                self.make(f"{name}{right}", landing.at[right], landing.at[right], at.sib).wait_recv()
                add_rows(acc(right), landing.at[right], rows)

        def go_left():
            @pl.when(at.z < last)
            def _():
                self.make(f"{name}{left}", landing.at[left], landing.at[left], at.sib).wait_recv()
                add_rows(acc(left), landing.at[left], rows)

        is_right, is_left = both(at.z < right, cond), both(at.z > left, cond)
        under(is_right, go_right)
        self.post(f"{name}{right}", acc(right), landing.at[right], at.up(), is_right)
        under(is_left, go_left)
        self.post(f"{name}{left}", acc(left), landing.at[left], at.down(), both(at.z > left + 1, cond))
        self.post(f"{name}end{left}", acc(left), landing.at[at.depth], at.down(), both(at.z == left + 1, cond))

    def line_end(self, name, acc, landing, rows, cond=None):
        at = self.at
        last = at.depth - 1
        for t in range(at.depth):
            def from_below():
                self.make(f"{name}{t}", landing.at[t], landing.at[t], at.sib).wait_recv()
                add_rows(acc(t), landing.at[t], rows)

            def from_above():
                self.make(f"{name}end{t}", landing.at[at.depth], landing.at[at.depth], at.sib).wait_recv()
                add_rows(acc(t), landing.at[at.depth], rows)

            if t > 0:
                under(both(at.z == t, cond), from_below)
            if t < last:
                under(both(at.z == t, cond), from_above)

    def relay(self):
        at, geo = self.at, self.geo
        self.take("diag", self.plane_in.at[0])
        mine = self.c1(at.relay_from)
        for t in range(at.depth):
            add_rows(self.acc.at[t, mine], self.plane_in.at[0, t], geo.t1)
        self.post("relay", self.acc.at[:, mine], self.plane_in.at[2], self.owner_dev)

    def combine(self):
        at, geo = self.at, self.geo
        self.take("near", self.plane_in.at[1])
        self.take("relay", self.plane_in.at[2])
        mine = self.c1(at.p)
        for t in range(at.depth):
            add_rows_two(self.acc.at[t, mine], self.plane_in.at[1, t], self.plane_in.at[2, t], geo.t1)

    def line1(self, step):
        mine = self.c1(self.at.p)
        self.line(step, "z", lambda t: self.acc.at[t, mine], self.z_in, self.geo.t1)

    def line1_end(self):
        at, geo = self.at, self.geo
        mine = self.c1(at.p)
        self.line_end("z", lambda t: self.acc.at[t, mine], self.z_in, geo.t1)
        self.spread("a", self.acc.at[at.z, mine], self.o1)

    def line2(self, step):
        at, geo = self.at, self.geo
        if geo.t2:
            span = pl.ds(4 * geo.t1, 4 * geo.t2)
            self.line(step, "w", lambda t: self.acc.at[t, span], self.z2_in, 4 * geo.t2)
        self.line(step, "r", lambda t: self.racc.at[t], self.rz_in, geo.unit, self.has_rest)

    def line2_end(self):
        at, geo = self.at, self.geo
        self.line_end("r", lambda t: self.racc.at[t], self.rz_in, geo.unit, self.has_rest)
        self.post("rx", self.racc.at[at.z], self.rplane_in.at[0], at.x_dev, self.has_rest)
        if geo.t2:
            span = pl.ds(4 * geo.t1, 4 * geo.t2)
            self.line_end("w", lambda t: self.acc.at[t, span], self.z2_in, 4 * geo.t2)
            self.post("diag2", self.acc.at[at.z, self.c2(at.p_d)], self.plane2_in.at[0], at.relay_dev)
            self.post("near2", self.acc.at[at.z, self.c2(self.direct_p)], self.plane2_in.at[1], at.relay_dev)

    def relay2(self):
        at, geo = self.at, self.geo
        if geo.t2:
            self.take("diag2", self.plane2_in.at[0])
            mine = self.c2(at.relay_from)
            add_rows(self.acc.at[at.z, mine], self.plane2_in.at[0], geo.t2)
            self.post("relay2", self.acc.at[at.z, mine], self.plane2_in.at[2], self.owner_dev)

    def rest_x(self):
        at, geo = self.at, self.geo

        def rest():
            self.make("rx", self.rplane_in.at[0], self.rplane_in.at[0], at.sib).wait_recv()
            self.make("rx", self.racc.at[at.z], self.rplane_in.at[0], at.x_dev).wait_send()
            add_rows(self.racc.at[at.z], self.rplane_in.at[0], geo.unit)

        pl.when(self.has_rest)(rest)
        self.posts = [item for item in self.posts if item[0] != "rx"]
        self.post("ry", self.racc.at[at.z], self.rplane_in.at[1], at.y_dev, self.has_rest)

    def rest_y(self):
        at, geo = self.at, self.geo

        def rest():
            self.make("ry", self.rplane_in.at[1], self.rplane_in.at[1], at.sib).wait_recv()
            self.make("ry", self.racc.at[at.z], self.rplane_in.at[1], at.y_dev).wait_send()
            add_rows(self.racc.at[at.z], self.rplane_in.at[1], geo.unit)
            pltpu.make_async_copy(self.racc.at[at.z], self.out.at[self.rest], self.local.at[2]).start()

        pl.when(self.has_rest)(rest)
        self.posts = [item for item in self.posts if item[0] != "ry"]
        self.post("rout", self.racc.at[at.z], self.out.at[self.rest], at.sib, self.has_rest)

    def combine2(self):
        at, geo = self.at, self.geo
        if geo.t2:
            self.take("near2", self.plane2_in.at[1])
            self.take("relay2", self.plane2_in.at[2])
            mine = self.c2(at.p)
            add_rows_two(self.acc.at[at.z, mine], self.plane2_in.at[1], self.plane2_in.at[2], geo.t2)
            self.spread("b", self.acc.at[at.z, mine], self.o2)

    def spread(self, name, src, rows):
        at = self.at
        mine = rows(at.p, at.core)
        index = 3 if name == "a" else 4
        pltpu.make_async_copy(src, self.out.at[mine], self.local.at[index]).start()
        self.post(name + "x", src, self.out.at[mine], at.x_dev)
        self.post(name + "y", src, self.out.at[mine], at.y_dev)
        self.post(name + "s", src, self.out.at[mine], at.sib)

    def spread_relay(self, name, rows):
        at = self.at
        for far, place in ((name + "x", at.p_x), (name + "y", at.p_y)):
            here = self.out.at[rows(place, at.core)]
            self.take(far, here)
            self.post(far + "s", here, here, at.sib)
        here = self.out.at[rows(at.relay_from, at.core)]
        self.post(name + "d", here, here, at.relay_dev)

    def spread_last(self, name, rows):
        at = self.at
        here = self.out.at[rows(at.p_d, at.core)]
        self.take(name + "d", here)
        self.post(name + "ds", here, here, at.sib)

    def spread_end(self, name, src, rows):
        at = self.at
        for suffix, place in (("s", at.p), ("xs", at.p_x), ("ys", at.p_y), ("ds", at.p_d)):
            self.take(name + suffix, self.out.at[rows(place, 1 - at.core)])
        index = 3 if name == "a" else 4
        pltpu.make_async_copy(src, self.out.at[rows(at.p, at.core)], self.local.at[index]).wait()

    def finish(self):
        at = self.at
        self.spread_end("a", self.acc.at[at.z, self.c1(at.p)], self.o1)
        if self.geo.t2:
            self.spread_end("b", self.acc.at[at.z, self.c2(at.p)], self.o2)
        pl.when(self.has_rest)(
            lambda: pltpu.make_async_copy(self.racc.at[at.z], self.out.at[self.rest], self.local.at[2]).wait()
        )
        self.take("rout", self.out.at[self.rest], self.no_rest)

    def drain(self):
        for name, src, dst, device, cond in self.posts:
            under(cond, lambda: self.make(name, src, dst, device).wait_send())

    def stages(self):
        steps = range(self.at.depth - 1)
        has2 = bool(self.geo.t2)
        return [
            [self.cores],
            [functools.partial(self.line2, i) for i in steps[:1]] + [self.relay],
            [functools.partial(self.line2, i) for i in steps[1:]] + [self.combine],
            [self.line2_end] + [functools.partial(self.line1, i) for i in steps[:1]],
            [self.relay2, self.rest_x] + [functools.partial(self.line1, i) for i in steps[1:2]],
            [self.combine2, self.rest_y] + [functools.partial(self.line1, i) for i in steps[2:]],
            [self.line1_end] + ([functools.partial(self.spread_relay, "b", self.o2)] if has2 else []),
            [functools.partial(self.spread_relay, "a", self.o1)]
            + ([functools.partial(self.spread_last, "b", self.o2)] if has2 else []),
            [functools.partial(self.spread_last, "a", self.o1)],
            [self.finish],
        ]


def reduce_kernel(geos, lag, *refs):
    count = len(geos)
    parts, outs = refs[:count], refs[count : 2 * count]
    send, recv, local = refs[2 * count : 2 * count + 3]
    rest = list(refs[2 * count + 3 :])
    at = Place()
    at.greet()
    items = []
    for k, geo in enumerate(geos):
        size = 10 if geo.t2 else 8
        bufs, rest = rest[:size], rest[size:]
        items.append(
            Reduce(at, geo, parts[k], outs[k], k % 2, bufs, send.at[k], recv.at[k], local.at[k])
        )
    for item in items:
        item.begin()
    plan = []
    for k, item in enumerate(items):
        for s, todo in enumerate(item.stages()):
            plan.append((s + lag * k, k, todo))
    for _, _, todo in sorted(plan, key=lambda entry: entry[:2]):
        for do in todo:
            do()
    for item in items:
        item.drain()


def reduce_grads(parts, line_parts, collective_id, lag=2):
    depth = lax.axis_size("fsdp")
    geos = [Geometry(item.shape[1], item.shape[2], b) for item, b in zip(parts, line_parts)]
    any_spec = pl.BlockSpec(memory_space=pl.ANY)
    count = len(parts)
    scratch = [
        pltpu.SemaphoreType.DMA((count, SLOTS)),
        pltpu.SemaphoreType.DMA((count, SLOTS)),
        pltpu.SemaphoreType.DMA((count, 5)),
    ]
    for geo in geos:
        scratch += geo.scratch(depth)
    return pl.pallas_call(
        functools.partial(reduce_kernel, geos, lag),
        out_shape=[jax.ShapeDtypeStruct(item.shape[1:], item.dtype) for item in parts],
        in_specs=[any_spec] * count,
        out_specs=[any_spec] * count,
        scratch_shapes=scratch,
        compiler_params=pltpu.CompilerParams(
            collective_id=collective_id, has_side_effects=True, vmem_limit_bytes=60 * 1024 * 1024
        ),
    )(*parts)
HEAD_DIM = 64


def normalize(values, scales, shifts):
    average = jnp.mean(values, axis=-1, keepdims=True)
    centred = values - average
    variance = jnp.mean(centred * centred, axis=-1, keepdims=True)
    return centred * lax.rsqrt(variance + 1e-05) * scales + shifts


def outer_sum(left_rows, right_rows):
    return lax.dot_general(
        left_rows, right_rows, (((0,), (0,)), ((), ())), preferred_element_type=jnp.float32
    )


def times_transpose(left_rows, weight_rows):
    return lax.dot_general(
        left_rows, weight_rows, (((1,), (1,)), ((), ())), preferred_element_type=jnp.float32
    )


def allowed_mask(positions, key_places, lengths):
    causal = (key_places[None, :] <= positions[:, None]) & (key_places[None, :] >= 0)
    inside = key_places[None, :] < lengths[:, None]
    return causal[None, None, :, :] & inside[:, None, None, :]


def attend_forward(queries, key_part, value_part, positions, lengths, score_scale):
    seq_count, row_count, head_count, head_width = queries.shape
    lowest = jnp.full((seq_count, head_count, row_count), -1e30, jnp.float32)
    key_places = jnp.arange(key_part.shape[1], dtype=jnp.int32)
    allowed = allowed_mask(positions, key_places, lengths)
    scores = (
        jnp.einsum("sqhe,skhe->shqk", queries, key_part, preferred_element_type=jnp.float32)
        * score_scale
    )
    scores = jnp.where(allowed, scores, -1e30)
    new_top = jnp.maximum(lowest, jnp.max(scores, axis=-1))
    exp_weights = jnp.where(allowed, jnp.exp(scores - new_top[..., None]), 0.0)
    running_total = jnp.sum(exp_weights, axis=-1)
    running_sum = jnp.einsum(
        "shqk,skhe->shqe",
        exp_weights.astype(jnp.bfloat16),
        value_part,
        preferred_element_type=jnp.float32,
    )
    output = jnp.transpose(running_sum / running_total[..., None], (0, 2, 1, 3))
    return (output, new_top + jnp.log(running_total))


def block_terms(
    queries,
    grad_out,
    log_total,
    delta_row,
    key_part,
    value_part,
    first_key,
    positions,
    lengths,
    score_scale,
):
    key_places = first_key + jnp.arange(key_part.shape[1], dtype=jnp.int32)
    allowed = allowed_mask(positions, key_places, lengths)
    scores = (
        jnp.einsum("sqhe,skhe->shqk", queries, key_part, preferred_element_type=jnp.float32)
        * score_scale
    )
    scores = jnp.where(allowed, scores, -1e30)
    probability = jnp.where(allowed, jnp.exp(scores - log_total[..., None]), 0.0)
    grad_probs = jnp.einsum(
        "sqhe,skhe->shqk", grad_out, value_part, preferred_element_type=jnp.float32
    )
    grad_scores = (probability * (grad_probs - delta_row[..., None])).astype(jnp.bfloat16)
    query_add = (
        jnp.einsum("shqk,skhe->sqhe", grad_scores, key_part, preferred_element_type=jnp.float32)
        * score_scale
    )
    key_add = (
        jnp.einsum("shqk,sqhe->skhe", grad_scores, queries, preferred_element_type=jnp.float32)
        * score_scale
    )
    value_add = jnp.einsum(
        "shqk,sqhe->skhe",
        probability.astype(jnp.bfloat16),
        grad_out,
        preferred_element_type=jnp.float32,
    )
    return (query_add, key_add, value_add)


def pack_small(ln_gain, ln_bias, b_qv, b_out, b_up, b_down):
    layers, _, part = ln_gain.shape
    return jnp.concatenate(
        [
            ln_gain.reshape(layers, 2, part),
            ln_bias.reshape(layers, 2, part),
            b_qv.reshape(layers, 2, part),
            b_out.reshape(layers, 1, part),
            b_down.reshape(layers, 1, part),
            b_up.reshape(layers, 4, part),
        ],
        axis=1,
    )


def unpack_small(whole):
    depth, _, part = whole.shape
    flat = jnp.transpose(whole[:, :8], (1, 0, 2)).reshape(8, depth * part)
    up_bias = whole[:, 8:].reshape(depth * 4 * part)
    return flat[0:2], flat[2:4], flat[4:6], flat[6], flat[7], up_bias


def small_rows(gains, shifts, mix_bias, out_bias, down_bias, up_bias, depth):
    width = gains.shape[-1]
    flat = jnp.concatenate([gains, shifts, mix_bias, out_bias[None], down_bias[None]], axis=0)
    flat = jnp.transpose(flat.reshape(8, depth, width // depth), (1, 0, 2))
    return jnp.concatenate([flat, up_bias.reshape(depth, 4, width // depth)], axis=1)


def fast_mesh(rows):
    return lax.axis_size("ctx") == 8 and rows % 272 == 0


def gather_all(weights, small):
    flat = [item for layer in weights for item in layer]
    layers = len(weights)
    if fast_mesh(flat[0].shape[0]):
        packed = small.reshape(layers * small.shape[1], small.shape[2])
        *wholes, small_all = gather_weights(flat, packed)
        small_all = small_all.reshape(-1, layers, small.shape[1], small.shape[2])
        wholes = [item.reshape(-1, item.shape[2]) for item in wholes]
    else:
        wholes = [lax.all_gather(item, "fsdp", axis=0, tiled=True) for item in flat]
        small_all = lax.all_gather(small, "fsdp", axis=0)
    return [wholes[4 * i : 4 * i + 4] for i in range(layers)], [small_all[:, i] for i in range(layers)]


def reduce_layer(grads, collective_id):
    depth = lax.axis_size("fsdp")
    if fast_mesh(grads[0].shape[0] // depth):
        parts = [item.reshape(depth, item.shape[0] // depth, item.shape[1]) for item in grads]
        return reduce_grads(parts, [0] * len(parts), collective_id, lag=1)
    shards_now = [
        lax.psum_scatter(item, "fsdp", scatter_dimension=0, tiled=True) for item in grads
    ]
    return [lax.psum(item, "ctx") for item in shards_now]


def shards(
    tokens,
    lengths,
    cotangent,
    ln_gain,
    ln_bias,
    w_qkv,
    b_qv,
    w_out,
    b_out,
    w_up,
    b_up,
    w_down,
    b_down,
):
    seq_count, row_count, model_width = tokens.shape
    head_width = HEAD_DIM
    head_count = model_width // head_width
    score_scale = head_width ** (-0.5)
    ctx_index = lax.axis_index("ctx")
    depth = lax.axis_size("fsdp")
    positions = ctx_index * row_count + jnp.arange(row_count, dtype=jnp.int32)
    valid_rows = (positions[None, :] < lengths[:, None]).astype(jnp.float32)[..., None]
    flat_rows = seq_count * row_count
    split_shape = (seq_count, row_count, head_count, head_width)
    layer_total = ln_gain.shape[0]
    hidden = tokens.astype(jnp.float32).reshape(flat_rows, model_width)
    small = pack_small(ln_gain, ln_bias, b_qv, b_out, b_up, b_down)
    weights, smalls = gather_all(
        [(w_qkv[i], w_out[i], w_up[i], w_down[i]) for i in range(layer_total)], small
    )
    kept_layers = []
    for layer_index in range(layer_total):
        mix_weight, out_weight, up_weight, down_weight = weights[layer_index]
        gain_rows, shift_rows, mix_bias, out_bias, down_bias, up_bias = unpack_small(
            smalls[layer_index].astype(jnp.float32)
        )
        normed_first = normalize(hidden, gain_rows[0], shift_rows[0]).astype(jnp.bfloat16)
        mixed_rows = jnp.dot(normed_first, mix_weight, preferred_element_type=jnp.float32)
        queries = (
            (mixed_rows[:, :model_width] + mix_bias[0]).astype(jnp.bfloat16).reshape(split_shape)
        )
        key_rows = (
            mixed_rows[:, model_width : 2 * model_width].astype(jnp.bfloat16).reshape(split_shape)
        )
        value_rows = (
            (mixed_rows[:, 2 * model_width :] + mix_bias[1])
            .astype(jnp.bfloat16)
            .reshape(split_shape)
        )
        key_part = lax.all_gather(key_rows, "ctx", axis=1, tiled=True)
        value_part = lax.all_gather(value_rows, "ctx", axis=1, tiled=True)
        output, log_total = attend_forward(
            queries, key_part, value_part, positions, lengths, score_scale
        )
        output = output.reshape(flat_rows, model_width)
        attended = output.astype(jnp.bfloat16)
        middle = (
            hidden + jnp.dot(attended, out_weight, preferred_element_type=jnp.float32) + out_bias
        )
        normed_second = normalize(middle, gain_rows[1], shift_rows[1]).astype(jnp.bfloat16)
        upper_pre = (
            jnp.dot(normed_second, up_weight, preferred_element_type=jnp.float32) + up_bias
        )
        active = jax.nn.gelu(upper_pre).astype(jnp.bfloat16)
        kept_layers.append(
            (
                hidden,
                normed_first,
                queries,
                key_part,
                value_part,
                output,
                log_total,
                attended,
                middle,
                normed_second,
                upper_pre,
                active,
                gain_rows,
                shift_rows,
            )
        )
        hidden = (
            middle + jnp.dot(active, down_weight, preferred_element_type=jnp.float32) + down_bias
        )
    activations = (valid_rows * hidden.reshape(seq_count, row_count, model_width)).astype(
        jnp.bfloat16
    )
    grad_hidden = (cotangent.astype(jnp.float32) * valid_rows).reshape(flat_rows, model_width)
    big_grads = [None] * layer_total
    small_grads = [None] * layer_total
    for layer_index in reversed(range(layer_total)):
        (
            hidden_in,
            normed_first,
            queries,
            key_part,
            value_part,
            output,
            log_total,
            attended,
            middle,
            normed_second,
            upper_pre,
            active,
            gain_rows,
            shift_rows,
        ) = kept_layers[layer_index]
        mix_weight, out_weight, up_weight, down_weight = weights[layer_index]
        grad_branch = grad_hidden.astype(jnp.bfloat16)
        down_bias_grad = jnp.sum(grad_branch.astype(jnp.float32), axis=0)
        down_grad = outer_sum(active, grad_branch)
        grad_active = times_transpose(grad_branch, down_weight)
        unused_gelu, gelu_pull = jax.vjp(jax.nn.gelu, upper_pre)
        grad_upper = gelu_pull(grad_active)[0].astype(jnp.bfloat16)
        up_bias_grad = jnp.sum(grad_upper.astype(jnp.float32), axis=0)
        up_grad = outer_sum(normed_second, grad_upper)
        grad_normed = times_transpose(grad_upper, up_weight)
        unused_norm, norm_pull = jax.vjp(normalize, middle, gain_rows[1], shift_rows[1])
        grad_middle, gain_second, shift_second = norm_pull(grad_normed)
        grad_middle = grad_middle + grad_hidden
        grad_attn = grad_middle.astype(jnp.bfloat16)
        out_bias_grad = jnp.sum(grad_attn.astype(jnp.float32), axis=0)
        out_grad = outer_sum(attended, grad_attn)
        grad_output = times_transpose(grad_attn, out_weight).astype(jnp.bfloat16)
        delta_row = jnp.transpose(
            jnp.sum((grad_output.astype(jnp.float32) * output).reshape(split_shape), axis=-1),
            (0, 2, 1),
        )
        grad_heads = grad_output.reshape(split_shape)
        query_grad, key_add, value_add = block_terms(
            queries,
            grad_heads,
            log_total,
            delta_row,
            key_part,
            value_part,
            0,
            positions,
            lengths,
            score_scale,
        )
        key_low = lax.psum_scatter(
            key_add.astype(jnp.bfloat16), "ctx", scatter_dimension=1, tiled=True
        ).reshape(flat_rows, model_width)
        value_low = lax.psum_scatter(
            value_add.astype(jnp.bfloat16), "ctx", scatter_dimension=1, tiled=True
        ).reshape(flat_rows, model_width)
        query_low = query_grad.reshape(flat_rows, model_width).astype(jnp.bfloat16)
        grad_mixed = jnp.concatenate([query_low, key_low, value_low], axis=1)
        mix_bias_grad = jnp.stack(
            [
                jnp.sum(query_low.astype(jnp.float32), axis=0),
                jnp.sum(value_low.astype(jnp.float32), axis=0),
            ]
        )
        mix_grad = outer_sum(normed_first, grad_mixed)
        grad_normed_first = times_transpose(grad_mixed, mix_weight)
        unused_first, first_pull = jax.vjp(normalize, hidden_in, gain_rows[0], shift_rows[0])
        grad_input, gain_first, shift_first = first_pull(grad_normed_first)
        grad_hidden = grad_input + grad_middle
        big_grads[layer_index] = reduce_layer(
            [item.astype(jnp.bfloat16) for item in (up_grad, down_grad, mix_grad, out_grad)],
            1 + layer_index,
        )
        small_grads[layer_index] = small_rows(
            jnp.stack([gain_first, gain_second]),
            jnp.stack([shift_first, shift_second]),
            mix_bias_grad,
            out_bias_grad,
            down_bias_grad,
            up_bias_grad,
            depth,
        )
    input_grad = grad_hidden.reshape(seq_count, row_count, model_width)
    packed = jnp.stack(small_grads).astype(jnp.bfloat16)
    total = lax.psum(packed, ("fsdp", "ctx"))
    own = lax.dynamic_index_in_dim(total, lax.axis_index("fsdp"), 1, keepdims=False)
    own = own.astype(jnp.float32)

    def whole(member):
        return jnp.stack([big_grads[i][member].astype(jnp.float32) for i in range(layer_total)])

    return (
        activations,
        input_grad,
        own[:, 0:2],
        own[:, 2:4],
        whole(2),
        own[:, 4:6],
        whole(3),
        own[:, 6],
        whole(0),
        own[:, 8:].reshape(layer_total, -1),
        whole(1),
        own[:, 7],
    )


def solution(mesh):
    placed = (
        P("fsdp", "ctx", None),
        P("fsdp"),
        P("fsdp", "ctx", None),
        P(None, None, "fsdp"),
        P(None, None, "fsdp"),
        P(None, "fsdp", None),
        P(None, None, "fsdp"),
        P(None, "fsdp", None),
        P(None, "fsdp"),
        P(None, "fsdp", None),
        P(None, "fsdp"),
        P(None, "fsdp", None),
        P(None, "fsdp"),
    )
    return jax.shard_map(
        shards,
        mesh=mesh,
        in_specs=placed,
        out_specs=(
            P("fsdp", "ctx", None),
            P("fsdp", "ctx", None),
            P(None, None, "fsdp"),
            P(None, None, "fsdp"),
            P(None, "fsdp", None),
            P(None, None, "fsdp"),
            P(None, "fsdp", None),
            P(None, "fsdp"),
            P(None, "fsdp", None),
            P(None, "fsdp"),
            P(None, "fsdp", None),
            P(None, "fsdp"),
        ),
        check_vma=False,
    )
```

time: 3060 us -> 1380 us (0.45)
  waiting for transfers between devices: 2010 us -> 153 us
  Pallas kernels: 0 us -> 613 us
  starting transfers between devices: 213 us -> 0.54 us
  blocking collectives: 139 us -> 37.2 us
  matrix products: 326 us -> 244 us
  other arithmetic: 127 us -> 51.4 us
  local copies, waits for them, and re-layouts: 209 us -> 253 us
    all_gather x12 -> x4, waiting for transfers between devices: 891 us -> 106 us  [the longest x2 53.2 us: shards(): key_part = lax.all_gather(key_rows, 'ctx', axis=1, tiled=True)]
    reduce_scatter x8 -> x0, waiting for transfers between devices: 761 us -> none  [the longest x2 348 us: shards(): lax.psum_scatter(down_grad.astype(jnp.bfloat16), 'fsdp', scatter_dimensio...]
    pallas_call x0 -> x3, Pallas kernels: none -> 613 us  [the longest x2 407 us: reduce_grads(): pl.pallas_call(functools.partial(reduce_kernel, geos, lag), out_shape=[ja...]
    ppermute x64 -> x0, starting transfers between devices: 212 us -> none  [the longest x32 114 us: from_behind(): return lax.ppermute(block, axis, route)]
    psum x1 -> x0, waiting for transfers between devices: 178 us -> none  [shards(): lax.psum(scattered[2].astype(jnp.bfloat16), 'ctx').astype(jnp.float32)]
    unnamed x229 -> x273, local copies, waits for them, and re-layouts: 48.3 us -> 162 us
    all_gather x6 -> x0, blocking collectives: 92.5 us -> none  [the longest x2 36.2 us: shards(): lax.all_gather(ln_bias[layer_index], 'fsdp', axis=1, tiled=True)]
    ppermute x64 -> x0, waiting for transfers between devices: 89.4 us -> none  [the longest x32 87.3 us: from_behind(): return lax.ppermute(block, axis, route)]
  transfers between devices with their start and end apart: 91 -> 8, of which waited for: 42 -> 5; matrix products, arithmetic and copies ran while one was open for 17% -> 18% of each run, Pallas kernels for 0% -> 15%
where the time goes in v1:
time: 1380 us; the launch traced here: 1370 us
  Pallas kernels  613 us (44%)
  local copies, waits for them, and re-layouts  253 us (18%)
  matrix products  244 us (18%)
  waiting for transfers between devices  153 us (11%)
  other arithmetic  51.4 us (4%)
  blocking collectives  37.2 us (3%)
  between operations  16 us (1%)
    pallas_call x2, Pallas kernels, reduce_grads(): pl.pallas_call(functools.partial(reduce_kernel, geos, lag), out_shape=[ja...  407 us
    pallas_call x1, Pallas kernels, gather_weights(): pl.pallas_call(functools.partial(gather_kernel, count), out_shape=shapes,...  207 us
    unnamed x273, local copies, waits for them, and re-layouts  162 us
    all_gather x2, waiting for transfers between devices, shards(): key_part = lax.all_gather(key_rows, 'ctx', axis=1, tiled=True)  53.2 us
    all_gather x2, waiting for transfers between devices, shards(): value_part = lax.all_gather(value_rows, 'ctx', axis=1, tiled=True)  52.5 us
    dot_general x8, matrix products, outer_sum(): lax.dot_general(left_rows, right_rows, (((0,), (0,)), ((), ())), preferre...  49.5 us
    unnamed x12, waiting for transfers between devices  46.9 us
    dot_general x8, matrix products, times_transpose(): lax.dot_general(left_rows, weight_rows, (((1,), (1,)), ((), ())), preferr...  41 us
  transfers between devices with their start and end apart: 8, of which 5 were waited for; matrix products, arithmetic and copies ran while one was open for 18% of the time, Pallas kernels for 15%

profile of v1, /device:TPU:9, one launch (start us, length us, event | category | flops | bytes accessed | tf_op | source)
XLA Modules:
  0.0 1368.6 jit_solution(1491396507969036759)
XLA Ops:
  21.3 206.5 %shard_map.220 = (bf16[4,272,3264]{2,1,0:T(8,128)(2,1)}, bf16[4,272,1088]{2,1,0:T(8,128)(2,1)S(1)}, bf16[4,272,4352]{2,1,0:T(8,128)(2,1)}, bf16[4,1088,1088]{2,1...) custom-call(bf16[272,3264]{1,0:T(8,128)(2,1)S(1)} %get-tuple-element, ...), custom_call_target="tpu_custom_call" | custom-call | tf_op jit(solution)/shard_map/pallas_call | solution.py:313
  257.9 32.9 %all-gather.5.cloned.1.call-done = bf16[2,1024,17,64]{1,3,2,0:T(8,128)(2,1)} async-done(((bf16[2,128,17,64]{1,3,2,0:T(8,128)(2,1)}), bf16[2,1024,17,64]{1,3,2,0:T(8,128)(2,1)}) %all-gather.5.cloned.1.call-update) | async-done | bytes 4456464 | tf_op jit(solution)/shard_map/all_gather | solution.py:909
  308.2 23.7 %all-gather.7.cloned.1.call-done = bf16[2,1024,17,64]{1,3,2,0:T(8,128)(2,1)} async-done(((bf16[2,128,17,64]{1,3,2,0:T(8,128)(2,1)}), bf16[2,1024,17,64]{1,3,2,0:T(8,128)(2,1)}) %all-gather.7.cloned.1.call-update) | async-done | bytes 4456464 | tf_op jit(solution)/shard_map/all_gather | solution.py:910
  331.9 10.7 fusion.141
  376.7 11.3 fusion.149
  388.1 20.3 %all-gather.9.cloned.1.call-done = bf16[2,1024,17,64]{1,3,2,0:T(8,128)(2,1)} async-done(((bf16[2,128,17,64]{1,3,2,0:T(8,128)(2,1)}), bf16[2,1024,17,64]{1,3,2,0:T(8,128)(2,1)}) %all-gather.9.cloned.1.call-update) | async-done | bytes 4456464 | tf_op jit(solution)/shard_map/all_gather | solution.py:909
  420.5 28.8 %all-gather.11.cloned.1.call-done = bf16[2,1024,17,64]{1,3,2,0:T(8,128)(2,1)} async-done(((bf16[2,128,17,64]{1,3,2,0:T(8,128)(2,1)}), bf16[2,1024,17,64]{1,3,2,0:T(8,128)(2,1)}) %all-gather.11.cloned.1.call-update) | async-done | bytes 4456464 | tf_op jit(solution)/shard_map/all_gather | solution.py:910
  462.2 12.6 fusion.135
  498.5 11.8 multiply_convert_fusion.1
  518.5 14.9 %copy.212 = bf16[2,1024,17,64]{3,2,0,1:T(8,128)(2,1)} copy(bf16[2,1024,17,64]{1,3,2,0:T(8,128)(2,1)} %fusion.42) | data formatting | bytes 8912896
  533.4 15.3 %reshape.580 = bf16[1024,2176]{1,0:T(8,128)(2,1)} reshape(bf16[1024,2,17,64]{3,2,1,0:T(8,128)(2,1)} %bitcast.293) | data formatting | bytes 8912896
  560.3 15.1 %copy.214 = bf16[2,1024,17,64]{3,2,0,1:T(8,128)(2,1)} copy(bf16[2,1024,17,64]{1,3,2,0:T(8,128)(2,1)} %convert_bitcast_fusion.1) | data formatting | bytes 8912896
  575.4 15.4 %reshape.582 = bf16[1024,2176]{1,0:T(8,128)(2,1)} reshape(bf16[1024,2,17,64]{3,2,1,0:T(8,128)(2,1)} %bitcast.294) | data formatting | bytes 8912896
  610.8 46.8 %reduce-scatter.15.cloned.1.call-done = bf16[128,2176]{1,0:T(8,128)(2,1)} async-done(((bf16[1024,2176]{1,0:T(8,128)(2,1)}), bf16[128,2176]{1,0:T(8,128)(2,1)}) %reduce-scatter.15.cloned.1.call-update) | async-done | bytes 557072
  693.3 11.8 multiply_convert_fusion
  712.0 14.9 %copy.216 = bf16[2,1024,17,64]{3,2,0,1:T(8,128)(2,1)} copy(bf16[2,1024,17,64]{1,3,2,0:T(8,128)(2,1)} %fusion.43) | data formatting | bytes 8912896
  726.9 15.3 %reshape.584 = bf16[1024,2176]{1,0:T(8,128)(2,1)} reshape(bf16[1024,2,17,64]{3,2,1,0:T(8,128)(2,1)} %bitcast.295) | data formatting | bytes 8912896
  753.4 14.9 %copy.218 = bf16[2,1024,17,64]{3,2,0,1:T(8,128)(2,1)} copy(bf16[2,1024,17,64]{1,3,2,0:T(8,128)(2,1)} %convert_bitcast_fusion) | data formatting | bytes 8912896
  768.3 15.4 %reshape.586 = bf16[1024,2176]{1,0:T(8,128)(2,1)} reshape(bf16[1024,2,17,64]{3,2,1,0:T(8,128)(2,1)} %bitcast.296) | data formatting | bytes 8912896
  794.6 14.0 %copy.206 = bf16[4352,1088]{1,0:T(8,128)(2,1)} copy(bf16[4352,1088]{0,1:T(8,128)(2,1)} %convolution_convert_fusion) | data formatting | bytes 18939904 | tf_op jit(solution)/shard_map/convert_element_type | solution.py:1022
  839.6 14.0 %copy.205 = bf16[4352,1088]{1,0:T(8,128)(2,1)} copy(bf16[4352,1088]{0,1:T(8,128)(2,1)} %convolution_convert_fusion.1) | data formatting | bytes 18939904 | tf_op jit(solution)/shard_map/convert_element_type | solution.py:1022
  860.3 201.4 %shard_map.222 = (bf16[272,4352]{1,0:T(8,128)(2,1)}, bf16[1088,1088]{1,0:T(8,128)(2,1)}, bf16[272,3264]{1,0:T(8,128)(2,1)}, bf16[272,1088]{1,0:T(8,128)(2,1)}) custom-call(bf16[4,272,4352]{2,1,0:T(8,128)(2,1)} %bitcast.298, bf16[4,1088,1088]{2,1,0:T(8,128)(2,1)} %bitcast.302, bf16[4,272,3264]{2,1,0:T(8,128)(2,1)} %bitcast.299, bf16[4,272,1088]{2,1,0:T(8,128)(2,1)} %bitcast.318), custom_call_target="tpu_custom_call" | custom-call | tf_op jit(solution)/shard_map/pallas_call | solution.py:699
  1090.8 37.2 %psum.7 = bf16[2,4,12,272]{3,0,2,1:T(2,128)(2,1)S(1)} all-reduce(bf16[2,4,12,272]{3,0,2,1:T(2,128)(2,1)S(1)} %pad_maximum_fusion), channel_id=1, replica_groups=mesh['fsdp'=4,'ctx'=8] {'fsdp','ctx'}, use_global_device_ids=true, to_apply=%region_44.45 | all-reduce | flops 26112 | bytes 104448 | tf_op jit(solution)/shard_map/psum | solution.py:1036
  1139.2 205.4 %shard_map.221 = (bf16[272,4352]{1,0:T(8,128)(2,1)}, bf16[1088,1088]{1,0:T(8,128)(2,1)}, bf16[272,3264]{1,0:T(8,128)(2,1)}, bf16[272,1088]{1,0:T(8,128)(2,1)}) custom-call(bf16[4,272,4352]{2,1,0:T(8,128)(2,1)} %bitcast.297, bf16[4,1088,1088]{2,1,0:T(8,128)(2,1)} %bitcast.301, bf16[4,272,3264]{2,1,0:T(8,128)(2,1)} %bitcast.300, bf16[4,272,1088]{2,1,0:T(8,128)(2,1)} %bitcast.317), custom_call_target="tpu_custom_call" | custom-call | tf_op jit(solution)/shard_map/pallas_call | solution.py:699
  (475 shorter events, 342.3 us)
Async XLA Ops:
  7.2 283.6 %all-gather.5.cloned.1.call-start = ((), (), s32[]{:S(2)}) async-start(), calls=%async_computation.4 | async-start | bytes 5013504 | tf_op jit(solution)/shard_map/all_gather | solution.py:909
  21.3 206.8 %copy-start.11 = (bf16[2,128,1088]{1,2,0:T(8,128)(2,1)S(1)}, bf16[2,128,1088]{1,2,0:T(8,128)(2,1)}, u32[]{:S(2)}) copy-start(bf16[2,128,1088]{1,2,0:T(8,128)(2,1)} %param.13) | copy-start | bytes 1671172
  227.9 115.3 %copy-start = (bf16[4,272,1088]{2,1,0:T(8,128)(2,1)}, bf16[4,272,1088]{2,1,0:T(8,128)(2,1)S(1)}, u32[]{:S(2)}) copy-start(bf16[4,272,1088]{2,1,0:T(8,128)(2,1)S(1)} %get-tuple-element.31) | copy-start | bytes 7102468
  245.3 86.6 %all-gather.7.cloned.1.call-start = ((), (), s32[]{:S(2)}) async-start(), calls=%async_computation.5 | async-start | bytes 5013504 | tf_op jit(solution)/shard_map/all_gather | solution.py:910
  252.9 155.5 %all-gather.9.cloned.1.call-start = ((), (), s32[]{:S(2)}) async-start(), calls=%async_computation.6 | async-start | bytes 5013504 | tf_op jit(solution)/shard_map/all_gather | solution.py:909
  254.7 105.2 %copy-start.64 = (f32[1088]{0:T(1024)}, f32[1088]{0:T(1024)S(1)}, u32[]{:S(2)}) copy-start(f32[1088]{0:T(1024)S(1)} %add.307) | copy-start | bytes 13060
  254.8 89.9 %copy-start.48 = (f32[1088]{0:T(1024)}, f32[1088]{0:T(1024)S(1)}, u32[]{:S(2)}) copy-start(f32[1088]{0:T(1024)S(1)} %mul.402) | copy-start | bytes 13060
  254.8 89.8 %copy-start.54 = (f32[1088]{0:T(1024)}, f32[1088]{0:T(1024)S(1)}, u32[]{:S(2)}) copy-start(f32[1088]{0:T(1024)S(1)} %add.294) | copy-start | bytes 13060
  257.5 38.8 %copy-start.103 = (s32[128]{0:T(128)}, s32[128]{0:T(128)S(1)}, u32[]{:S(2)}) copy-start(s32[128]{0:T(128)S(1)} %iota_add_fusion) | copy-start | bytes 1540
  308.2 34.4 %copy-start.61 = (f32[2,17,128]{2,1,0:T(8,128)}, f32[2,17,128]{2,1,0:T(8,128)S(1)}, u32[]{:S(2)}) copy-start(f32[2,17,128]{2,1,0:T(8,128)S(1)} %fusion) | copy-start | bytes 52228
  359.6 314.2 %copy-start.13 = (f32[256,1088]{0,1:T(8,128)}, f32[256,1088]{0,1:T(8,128)S(1)}, u32[]{:S(2)}) copy-start(f32[256,1088]{0,1:T(8,128)S(1)} %get-tuple-element.183) | copy-start | bytes 3342340
  369.6 79.7 %all-gather.11.cloned.1.call-start = ((), (), s32[]{:S(2)}) async-start(), calls=%async_computation.7 | async-start | bytes 5013504 | tf_op jit(solution)/shard_map/all_gather | solution.py:910
  374.9 229.4 %reduce-scatter.13.cloned.1.call-start = ((), (), s32[]{:S(2)}) async-start(), calls=%async_computation.8 | async-start | bytes 5013504
  376.4 113.6 %copy-start.56 = (f32[1088]{0:T(1024)}, f32[1088]{0:T(1024)S(1)}, u32[]{:S(2)}) copy-start(f32[1088]{0:T(1024)S(1)} %mul.419) | copy-start | bytes 13060
  376.5 85.7 %copy-start.66 = (f32[1088]{0:T(1024)}, f32[1088]{0:T(1024)S(1)}, u32[]{:S(2)}) copy-start(f32[1088]{0:T(1024)S(1)} %add.321) | copy-start | bytes 13060
  462.2 29.0 %copy-start.22 = (f32[2,128,17,64]{1,0,3,2:T(2,128)}, f32[2,128,17,64]{1,0,3,2:T(2,128)S(1)}, u32[]{:S(2)}) copy-start(f32[2,128,17,64]{1,0,3,2:T(2,128)S(1)} %copy.186) | copy-start | bytes 3342340
  491.1 195.4 %copy-start.10 = (f32[256,1088]{0,1:T(8,128)}, f32[256,1088]{0,1:T(8,128)S(1)}, u32[]{:S(2)}) copy-start(f32[256,1088]{0,1:T(8,128)S(1)} %get-tuple-element.130) | copy-start | bytes 3342340
  548.7 108.8 %reduce-scatter.15.cloned.1.call-start = ((), (), s32[]{:S(2)}) async-start(), calls=%async_computation.9 | async-start | bytes 5013504
  590.7 479.8 %reduce-scatter.17.cloned.1.call-start = ((), (), s32[]{:S(2)}) async-start(), calls=%async_computation.10 | async-start | bytes 5013504
  742.2 332.9 %reduce-scatter.19.cloned.1.call-start = ((), (), s32[]{:S(2)}) async-start(), calls=%async_computation.11 | async-start | bytes 5013504
  860.3 201.4 %copy-start.17 = (f32[256,1088]{0,1:T(8,128)S(1)}, f32[256,1088]{0,1:T(8,128)}, u32[]{:S(2)}) copy-start(f32[256,1088]{0,1:T(8,128)} %copy-done.16) | copy-start | bytes 3342340
  860.3 201.4 %copy-start.21 = (f32[2,128,17,64]{1,0,3,2:T(2,128)S(1)}, f32[2,128,17,64]{1,0,3,2:T(2,128)}, u32[]{:S(2)}) copy-start(f32[2,128,17,64]{1,0,3,2:T(2,128)} %copy.194) | copy-start | bytes 3342340
  1083.9 44.7 %copy-start.60 = (f32[1088]{0:T(1024)S(1)}, f32[1088]{0:T(1024)}, u32[]{:S(2)}) copy-start(f32[1088]{0:T(1024)} %copy-done.59) | copy-start | bytes 13060
  1139.2 205.4 %copy-start.44 = (bf16[272,1088]{1,0:T(8,128)(2,1)S(1)}, bf16[272,1088]{1,0:T(8,128)(2,1)}, u32[]{:S(2)}) copy-start(bf16[272,1088]{1,0:T(8,128)(2,1)} %get-tuple-element.41) | copy-start | bytes 1775620
  (105 other events, 716.7 us)
Sparse Core Ops, SparseCore 0:
  245.4 45.3 all-gather.4
  293.2 38.5 all-gather.6
  369.8 38.5 all-gather.8
  410.7 38.5 all-gather.10
  548.9 52.2 reduce-scatter.12
  604.9 52.6 reduce-scatter.14
  742.3 52.6 reduce-scatter.16
  798.9 52.6 reduce-scatter.18

commit v2 on v1

--- a/solution.py
+++ b/solution.py
@@ -65,6 +65,7 @@
         self.at, self.own, self.whole = at, own, whole
         self.send, self.recv = send, recv
         rows = own.shape[0]
+        self.rows = rows
         unit = rows // 17
         self.t1 = 2 * unit
         self.block = 8 * unit
@@ -81,9 +82,14 @@
     def copy(self, kind, shard, rows, device, src=None, second=False):
         depth = self.at.depth
         slot = kind * depth + shard
-        src = self.whole.at[shard, rows] if src is None else src
+        place = self.place(shard, rows)
+        src = place if src is None else src
         send = self.send.at[(8 * depth + kind) if second else slot]
-        return remote(src, self.whole.at[shard, rows], send, self.recv.at[slot], device)
+        return remote(src, place, send, self.recv.at[slot], device)
+
+    def place(self, shard, rows):
+        first = pl.multiple_of(shard * self.rows + rows.start, 16)
+        return self.whole.at[pl.ds(first, rows.size)]
 
     def start(self):
         at = self.at
@@ -215,118 +221,6 @@
 
         for step in range(at.depth - 1):
             self.cases(step, do)
-
-
-def gather_kernel(count, *refs):
-    owns, small = refs[:count], refs[count]
-    wholes, small_all = refs[count + 1 : 2 * count + 1], refs[2 * count + 1]
-    send, recv, own_sem, small_send, small_recv = refs[2 * count + 2 : 2 * count + 7]
-    stages = refs[2 * count + 7 :]
-    at = Place()
-    depth = at.depth
-    at.greet()
-    items = [
-        Gather(at, owns[k], wholes[k], k % 2, send.at[k], recv.at[k]) for k in range(count)
-    ]
-    loads = [pltpu.make_async_copy(owns[k], stages[k], own_sem.at[0, k]) for k in range(count)]
-    loads.append(pltpu.make_async_copy(small, stages[count], own_sem.at[0, count]))
-    stores = [
-        pltpu.make_async_copy(stages[k], wholes[k].at[at.z], own_sem.at[1, k]) for k in range(count)
-    ]
-    stores.append(pltpu.make_async_copy(stages[count], small_all.at[at.z], own_sem.at[1, count]))
-
-    def small_copy(shard, device, src=None, second=False):
-        return remote(
-            small_all.at[shard] if src is None else src,
-            small_all.at[shard],
-            small_send.at[depth if second else shard],
-            small_recv.at[shard],
-            device,
-        )
-
-    @pl.when(at.z < depth - 1)
-    def _():
-        small_copy(at.z, at.up(), small).start()
-
-    @pl.when(at.z > 0)
-    def _():
-        small_copy(at.z, at.down(), small, True).start()
-
-    steps = depth - 1
-    items[0].start()
-    for copy in loads:
-        copy.start()
-
-    def small_do(shard, onward, device):
-        small_copy(shard, at.sib).wait_recv()
-
-        @pl.when(onward)
-        def _():
-            small_copy(shard, device).start()
-
-    for k in range(count):
-        if k == 0:
-            for step in range(steps):
-                items[0].arrive(step)
-            for load, store in zip(loads, stores):
-                load.wait()
-                store.start()
-        if k == 0:
-            for step in range(steps):
-                items[0].cases(step, small_do)
-        if k + 1 < count:
-            items[k + 1].start()
-        for step in range(steps):
-            items[k].plane(step)
-            if k + 1 < count:
-                items[k + 1].arrive(step)
-            items[k].share(step)
-    for item in items:
-        item.finish()
-    for copy in stores:
-        copy.wait()
-    for item in items:
-        item.drain()
-
-    @pl.when(at.z < depth - 1)
-    def _():
-        small_copy(at.z, at.up(), small).wait_send()
-
-    @pl.when(at.z > 0)
-    def _():
-        small_copy(at.z, at.down(), small, True).wait_send()
-
-    def small_end(shard, onward, device):
-        @pl.when(onward)
-        def _():
-            small_copy(shard, device).wait_send()
-
-    for step in range(steps):
-        items[0].cases(step, small_end)
-
-
-def gather_weights(owns, small):
-    depth = lax.axis_size("fsdp")
-    count = len(owns)
-    any_spec = pl.BlockSpec(memory_space=pl.ANY)
-    shapes = [jax.ShapeDtypeStruct((depth,) + item.shape, item.dtype) for item in list(owns) + [small]]
-    return pl.pallas_call(
-        functools.partial(gather_kernel, count),
-        out_shape=shapes,
-        in_specs=[any_spec] * (count + 1),
-        out_specs=[any_spec] * (count + 1),
-        scratch_shapes=[
-            pltpu.SemaphoreType.DMA((count, 8 * depth + 8)),
-            pltpu.SemaphoreType.DMA((count, 8 * depth)),
-            pltpu.SemaphoreType.DMA((2, count + 1)),
-            pltpu.SemaphoreType.DMA((depth + 1,)),
-            pltpu.SemaphoreType.DMA((depth,)),
-        ]
-        + [pltpu.VMEM(item.shape, item.dtype) for item in list(owns) + [small]],
-        compiler_params=pltpu.CompilerParams(
-            collective_id=0, has_side_effects=True, vmem_limit_bytes=40 * 1024 * 1024
-        ),
-    )(*owns, small)
 
 
 def both(*conds):
@@ -706,7 +600,557 @@
             collective_id=collective_id, has_side_effects=True, vmem_limit_bytes=60 * 1024 * 1024
         ),
     )(*parts)
+
+
 HEAD_DIM = 64
+
+LANES = 128
+F32, BF16 = jnp.float32, jnp.bfloat16
+
+
+def pad_lanes(n):
+    return (n + LANES - 1) // LANES * LANES
+
+
+def by_tiles(total, tile, do):
+    count = total // tile
+
+    def step(i, carry):
+        do(pl.multiple_of(i * tile, tile), tile)
+        return carry
+
+    if count:
+        lax.fori_loop(0, count, step, 0)
+    if total % tile:
+        do(count * tile, total % tile)
+
+
+def row_norm(values):
+    average = jnp.mean(values, axis=-1, keepdims=True)
+    centred = values - average
+    variance = jnp.mean(centred * centred, axis=-1, keepdims=True)
+    scale = lax.rsqrt(variance + 1e-05)
+    return centred * scale, scale
+
+
+GELU_A = 0.7978845608028654
+GELU_B = 0.044715
+
+
+def gelu_of(u):
+    return 0.5 * u * (1.0 + jnp.tanh(GELU_A * (u + GELU_B * u * u * u)))
+
+
+class Context:
+    def __init__(self, at, own, whole, rows, send, recv, local):
+        self.at, self.own, self.whole, self.rows = at, own, whole, rows
+        self.send, self.recv, self.local = send, recv, local
+        core, p = at.core, at.p
+        self.names, self.posts = {}, []
+
+    def place(self, p, core):
+        return self.whole.at[:, pl.ds(pl.multiple_of((2 * p + core) * self.rows, 16), self.rows)]
+
+    def make(self, name, src, dst, device):
+        i = self.names.setdefault(name, len(self.names))
+        return remote(src, dst, self.send.at[i], self.recv.at[i], device)
+
+    def post(self, name, src, dst, device):
+        self.make(name, src, dst, device).start()
+        self.posts.append((name, src, dst, device))
+
+    def take(self, name, dst):
+        self.make(name, dst, dst, self.at.sib).wait_recv()
+
+    def start(self):
+        at = self.at
+        here = self.place(at.p, at.core)
+        self.post("x", self.own, here, at.x_dev)
+        self.post("y", self.own, here, at.y_dev)
+        self.post("s", self.own, here, at.sib)
+        self.keep = pltpu.make_async_copy(self.own, here, self.local)
+        self.keep.start()
+
+    def relay(self):
+        at = self.at
+        for name, p in (("x", at.p_x), ("y", at.p_y)):
+            self.take(name, self.place(p, at.core))
+        here = self.place(at.relay_from, at.core)
+        self.post("d", here, here, at.relay_dev)
+        for name, p in (("x", at.p_x), ("y", at.p_y)):
+            here = self.place(p, at.core)
+            self.post(name + "s", here, here, at.sib)
+
+    def last(self):
+        at = self.at
+        here = self.place(at.p_d, at.core)
+        self.take("d", here)
+        self.post("ds", here, here, at.sib)
+
+    def finish(self):
+        at = self.at
+        for name, p in (("s", at.p), ("xs", at.p_x), ("ys", at.p_y), ("ds", at.p_d)):
+            self.take(name, self.place(p, 1 - at.core))
+        self.keep.wait()
+
+    def drain(self, own):
+        for name, src, dst, device in self.posts:
+            if (name in ("x", "y", "s")) == own:
+                self.make(name, src, dst, device).wait_send()
+
+
+KEPT = ("h", "a", "q", "kv", "o", "lse", "h1", "c", "u")
+
+
+def kept_shapes(seqs, slots, rows, width, ff):
+    wide = pad_lanes(width)
+    flat = seqs * rows
+    return {
+        "h": ((flat, width), F32),
+        "a": ((flat, width), BF16),
+        "q": ((flat, wide), BF16),
+        "kv": ((seqs, slots, 2 * wide), BF16),
+        "o": ((flat, wide), BF16),
+        "lse": ((flat * 2, LANES), F32),
+        "h1": ((flat, width), F32),
+        "c": ((flat, width), BF16),
+        "u": ((flat, ff), F32),
+    }
+
+
+def key_bias(out, seqs, rows, slots, lengths, ctx):
+    for s in range(seqs):
+        key = lax.broadcasted_iota(jnp.int32, (rows, slots), 1)
+        row = ctx * rows + lax.broadcasted_iota(jnp.int32, (rows, slots), 0)
+        seen = jnp.logical_and(key <= row, key < lengths[s])
+        out[s] = jnp.where(seen, 0.0, -1e30)
+
+
+def two_heads(block):
+    lane = lax.broadcasted_iota(jnp.int32, block.shape, 1)
+    zero = jnp.zeros_like(block)
+    return jnp.concatenate(
+        [jnp.where(lane < HEAD_DIM, block, zero), jnp.where(lane < HEAD_DIM, zero, block)], axis=0
+    )
+
+
+def one_pair(stacked, rows):
+    lane = lax.broadcasted_iota(jnp.int32, (rows, LANES), 1)
+    return jnp.where(lane < HEAD_DIM, stacked[:rows], stacked[rows:])
+
+
+def across(a, b):
+    return lax.dot_general(a, b, (((1,), (1,)), ((), ())), preferred_element_type=F32)
+
+
+def attend(s, first, count, q_ref, kv_ref, bias_ref, o_ref, lse_ref, rows, pairs, wide):
+    def step(i, carry):
+        j = first + i
+        col = pl.ds(pl.multiple_of(j * LANES, LANES), LANES)
+        q2 = two_heads(q_ref[pl.ds(s * rows, rows), col])
+        keys = kv_ref[s, :, col]
+        values = kv_ref[s, :, pl.ds(pl.multiple_of(wide + j * LANES, LANES), LANES)]
+        bias = bias_ref[s]
+        scores = across(q2, keys) * (HEAD_DIM ** (-0.5))
+        scores = scores + jnp.concatenate([bias, bias], axis=0)
+        top = jnp.max(scores, axis=-1, keepdims=True)
+        weights = jnp.exp(scores - top)
+        total = jnp.sum(weights, axis=-1, keepdims=True)
+        out = jnp.dot(weights.astype(BF16), values, preferred_element_type=F32) / total
+        o_ref[pl.ds(s * rows, rows), col] = one_pair(out, rows).astype(BF16)
+        mine = s * pairs + j
+        here = pl.ds(s * 2 * rows, 2 * rows)
+        lane = lax.broadcasted_iota(jnp.int32, (2 * rows, LANES), 1)
+        lse_ref[here, :] = jnp.where(lane == mine, top + jnp.log(total), lse_ref[here, :])
+        return carry
+
+    lax.fori_loop(0, count, step, 0)
+
+
+def forward_kernel(dims, *refs):
+    layers, seqs, rows, slots, width, ff, depth = dims
+    flat, wide = seqs * rows, pad_lanes(width)
+    pairs = wide // LANES
+    refs = list(refs)
+
+    def grab(n):
+        out = refs[:n]
+        del refs[:n]
+        return out
+
+    tokens, lengths, w_qkv, w_out, w_up, w_down, small = grab(7)
+    acts, vecs = grab(2)
+    wholes = grab(4 * layers)
+    kept = [dict(zip(KEPT, grab(len(KEPT)))) for _ in range(layers)]
+    (send, recv, small_send, small_recv, kv_send, kv_recv, load_sem, keep_sem, stage_sem) = grab(9)
+    (small_all, vec, up_bias, h, a, q, own_kv, kv, bias, o, lse, h1, c, u, z) = grab(15)
+    w_bufs = grab(4)
+    at = Place()
+    at.greet()
+
+    owns = [ref.at[l] for l in range(layers) for ref in (w_qkv, w_out, w_up, w_down)]
+    items = [Gather(at, owns[k], wholes[k], k % 2, send.at[k], recv.at[k]) for k in range(4 * layers)]
+    contexts = [
+        Context(at, own_kv, kept[l]["kv"], rows, kv_send.at[l], kv_recv.at[l], keep_sem.at[l, len(KEPT)])
+        for l in range(layers)
+    ]
+    pending = {}
+
+    def keep(l, name, src):
+        copy = pltpu.make_async_copy(src, kept[l][name], keep_sem.at[l, KEPT.index(name)])
+        copy.start()
+        pending[(l, name)] = copy
+
+    def free(l, name):
+        copy = pending.pop((l, name), None)
+        if copy is not None:
+            copy.wait()
+
+    def buffer(k):
+        return w_bufs[k % 4]
+
+    def own_copy(k, load):
+        r = owns[k].shape[0]
+        shard = lax.rem(at.z + k // 4, depth)
+        place = buffer(k).at[pl.ds(pl.multiple_of(shard * r, 16), r)]
+        if load:
+            return pltpu.make_async_copy(owns[k], place, stage_sem.at[0, k])
+        return pltpu.make_async_copy(place, items[k].place(at.z, pl.ds(0, r)), stage_sem.at[1, k])
+
+    def own_load(k):
+        own_copy(k, True).start()
+
+    def own_store(k):
+        own_copy(k, True).wait()
+        own_copy(k, False).start()
+
+    def own_done(k):
+        own_copy(k, False).wait()
+
+    def fetch(k):
+        pltpu.make_async_copy(wholes[k], buffer(k), load_sem.at[k]).start()
+
+    def ready(k):
+        pltpu.make_async_copy(wholes[k], buffer(k), load_sem.at[k]).wait()
+
+    def small_copy(shard, device, src=None, second=False):
+        return remote(
+            small_all.at[shard] if src is None else src,
+            small_all.at[shard],
+            small_send.at[depth if second else shard],
+            small_recv.at[shard],
+            device,
+        )
+
+    def small_start():
+        @pl.when(at.z < depth - 1)
+        def _():
+            small_copy(at.z, at.up(), small).start()
+
+        @pl.when(at.z > 0)
+        def _():
+            small_copy(at.z, at.down(), small, True).start()
+
+        pltpu.make_async_copy(small, small_all.at[at.z], stage_sem.at[2, 0]).start()
+
+    def small_take():
+        def do(shard, onward, device):
+            small_copy(shard, at.sib).wait_recv()
+            pl.when(onward)(lambda: small_copy(shard, device).start())
+
+        for step in range(depth - 1):
+            items[0].cases(step, do)
+        pltpu.make_async_copy(small, small_all.at[at.z], stage_sem.at[2, 0]).wait()
+
+    def small_drain():
+        @pl.when(at.z < depth - 1)
+        def _():
+            small_copy(at.z, at.up(), small).wait_send()
+
+        @pl.when(at.z > 0)
+        def _():
+            small_copy(at.z, at.down(), small, True).wait_send()
+
+        def do(shard, onward, device):
+            pl.when(onward)(lambda: small_copy(shard, device).wait_send())
+
+        for step in range(depth - 1):
+            items[0].cases(step, do)
+
+    def small_spread():
+        part = width // depth
+        per_layer = small_all.shape[1] // layers
+        total = jnp.zeros((small_all.shape[1], wide), F32)
+        room = jnp.zeros((small_all.shape[1], wide - small_all.shape[2]), F32)
+        pieces = [small_all[i].astype(F32) for i in range(depth)]
+        for i in range(depth):
+            piece = jnp.concatenate([pieces[i], room], axis=1)
+            total = total + (pltpu.roll(piece, i * part, 1) if i else piece)
+        for l in range(layers):
+            vec[l] = total[l * per_layer : l * per_layer + 8]
+            vecs[l] = total[l * per_layer : l * per_layer + 8]
+            wide_up = jnp.zeros((1, ff), F32)
+            up_room = jnp.zeros((1, ff - small_all.shape[2]), F32)
+            for i in range(depth):
+                for r in range(4):
+                    at_row = l * per_layer + 8 + r
+                    piece = jnp.concatenate([pieces[i][at_row : at_row + 1], up_room], axis=1)
+                    shift = (i * 4 + r) * part
+                    wide_up = wide_up + (pltpu.roll(piece, shift, 1) if shift else piece)
+            up_bias[l] = jnp.broadcast_to(wide_up, (8, ff))
+
+    def row(l, i):
+        return vec[l, pl.ds(i, 1), pl.ds(0, width)]
+
+    def norm(l, i, src, dst):
+        def do(first, size):
+            here = pl.ds(first, size)
+            unit, _ = row_norm(src[here, :])
+            dst[here, :] = (unit * row(l, i) + row(l, 2 + i)).astype(BF16)
+
+        by_tiles(flat, 32, do)
+
+    def load_tokens():
+        def do(first, size):
+            here = pl.ds(first, size)
+            h[here, :] = tokens[here, :].astype(F32)
+
+        by_tiles(flat, 32, do)
+
+    def mix(l):
+        def do(first, size):
+            cols = pl.ds(first, size)
+            u[:, cols] = jnp.dot(a[...], w_bufs[0][:, cols], preferred_element_type=F32)
+
+        by_tiles(3 * width, 256, do)
+
+        for s in range(seqs):
+
+            def split(first, size):
+                here, there = pl.ds(s * rows + first, size), pl.ds(first, size)
+                queries = u[here, pl.ds(0, width)] + row(l, 4)
+                keys = u[here, pl.ds(width, width)]
+                values = u[here, pl.ds(2 * width, width)] + row(l, 5)
+                q[here, pl.ds(0, width)] = queries.astype(BF16)
+                own_kv[s, there, pl.ds(0, width)] = keys.astype(BF16)
+                own_kv[s, there, pl.ds(wide, width)] = values.astype(BF16)
+
+            by_tiles(rows, 32, split)
+
+    def project(l):
+        def do(first, size):
+            cols = pl.ds(first, size)
+            bias_row = vec[l, pl.ds(6, 1), cols]
+            h1[:, cols] = (
+                h[:, cols]
+                + jnp.dot(o[:, pl.ds(0, width)], w_bufs[1][:, cols], preferred_element_type=F32)
+                + bias_row
+            )
+
+        by_tiles(width, 256, do)
+
+    def rise(l):
+        def do(first, size):
+            cols = pl.ds(first, size)
+            pre = jnp.dot(c[...], w_bufs[2][:, cols], preferred_element_type=F32) + up_bias[l, pl.ds(0, 1), cols]
+            u[:, cols] = pre
+            z[:, cols] = gelu_of(pre).astype(BF16)
+
+        by_tiles(ff, 256, do)
+
+    def fall(l):
+        def do(first, size):
+            cols = pl.ds(first, size)
+            h[:, cols] = (
+                h1[:, cols]
+                + jnp.dot(z[...], w_bufs[3][:, cols], preferred_element_type=F32)
+                + vec[l, pl.ds(7, 1), cols]
+            )
+
+        by_tiles(width, 256, do)
+
+    def finish_tokens():
+        for s in range(seqs):
+            def do(first, size):
+                here = pl.ds(s * rows + first, size)
+                place = at.c8 * rows + first + lax.broadcasted_iota(jnp.int32, (size, width), 0)
+                acts[here, :] = jnp.where(place < lengths[s], h[here, :], 0.0).astype(BF16)
+
+            by_tiles(rows, 32, do)
+
+    steps = depth - 1
+    ticks = []
+    for k in range(4 * layers):
+        if k == 0:
+            ticks += [functools.partial(items[0].arrive, i) for i in range(steps)]
+        if k + 2 < 4 * layers:
+            ticks.append(items[k + 2].start)
+        for i in range(steps):
+            ticks.append(functools.partial(items[k].plane, i))
+            if k + 1 < 4 * layers:
+                ticks.append(functools.partial(items[k + 1].arrive, i))
+            ticks.append(functools.partial(items[k].share, i))
+        ticks.append(("end", k))
+
+    def tick(n):
+        for _ in range(n):
+            if not ticks:
+                return
+            item = ticks.pop(0)
+            if isinstance(item, tuple) and item[0] == "end":
+                items[item[1]].finish()
+            else:
+                item()
+
+    def reach(k):
+        while ("end", k) in ticks:
+            tick(1)
+
+    small_start()
+    items[0].start()
+    items[1].start()
+    for k in range(4 * layers):
+        own_load(k)
+    load_tokens()
+    q[...] = jnp.zeros_like(q)
+    o[...] = jnp.zeros_like(o)
+    own_kv[...] = jnp.zeros_like(own_kv)
+    lse[...] = jnp.zeros_like(lse)
+    key_bias(bias, seqs, rows, slots, lengths, at.c8)
+    for k in range(4 * layers):
+        own_store(k)
+    tick(steps)
+    small_take()
+    small_spread()
+    for k in range(4 * layers):
+        own_done(k)
+    for l in range(layers):
+        k = 4 * l
+        free(l - 1, "a")
+        norm(l, 0, h, a)
+        keep(l, "h", h)
+        keep(l, "a", a)
+        reach(k)
+        fetch(k)
+        free(l - 1, "u")
+        free(l - 1, "q")
+        if l:
+            contexts[l - 1].drain(True)
+        ready(k)
+        mix(l)
+        contexts[l].start()
+        keep(l, "q", q)
+        tick(8)
+        contexts[l].relay()
+        reach(k + 1)
+        fetch(k + 1)
+        tick(4)
+        contexts[l].last()
+        tick(3)
+        contexts[l].finish()
+        seen = pltpu.make_async_copy(kept[l]["kv"], kv, load_sem.at[4 * layers])
+        seen.start()
+        free(l - 1, "o")
+        free(l - 1, "lse")
+        seen.wait()
+        half = pairs // 2
+        for s in range(seqs):
+            attend(s, 0, half, q, kv, bias, o, lse, rows, pairs, wide)
+            tick(2)
+            attend(s, half, pairs - half, q, kv, bias, o, lse, rows, pairs, wide)
+            tick(2)
+        keep(l, "o", o)
+        keep(l, "lse", lse)
+        ready(k + 1)
+        free(l - 1, "h1")
+        project(l)
+        keep(l, "h1", h1)
+        free(l - 1, "c")
+        norm(l, 1, h1, c)
+        keep(l, "c", c)
+        reach(k + 2)
+        fetch(k + 2)
+        ready(k + 2)
+        rise(l)
+        keep(l, "u", u)
+        reach(k + 3)
+        fetch(k + 3)
+        free(l, "h")
+        ready(k + 3)
+        fall(l)
+    tick(len(ticks))
+    finish_tokens()
+    for key in list(pending):
+        free(*key)
+    small_drain()
+    for item in items:
+        item.drain()
+    contexts[-1].drain(True)
+    for context in contexts:
+        context.drain(False)
+
+
+def forward(tokens, lengths, w_qkv, w_out, w_up, w_down, small):
+    seqs, rows, width = tokens.shape
+    layers, part, _ = w_qkv.shape
+    depth = lax.axis_size("fsdp")
+    slots = rows * lax.axis_size("ctx")
+    ff = w_up.shape[2]
+    flat, wide = seqs * rows, pad_lanes(width)
+    dims = (layers, seqs, rows, slots, width, ff, depth)
+    any_spec = pl.BlockSpec(memory_space=pl.ANY)
+    vmem = pl.BlockSpec(memory_space=pltpu.VMEM)
+    struct = lambda shape, kind: jax.ShapeDtypeStruct(shape, kind)
+    shapes = kept_shapes(seqs, slots, rows, width, ff)
+    out_shape = [struct((flat, width), BF16), struct((layers, 8, wide), F32)]
+    for l in range(layers):
+        for ref in (w_qkv, w_out, w_up, w_down):
+            out_shape.append(struct((depth * ref.shape[1], ref.shape[2]), BF16))
+    for l in range(layers):
+        out_shape += [struct(*shapes[name]) for name in KEPT]
+    count = 4 * layers
+    dma = pltpu.SemaphoreType.DMA
+    scratch = [
+        dma((count, 8 * depth + 8)),
+        dma((count, 8 * depth)),
+        dma((depth + 1,)),
+        dma((depth,)),
+        dma((layers, 8)),
+        dma((layers, 8)),
+        dma((count + 1,)),
+        dma((layers, len(KEPT) + 1)),
+        dma((3, count)),
+        pltpu.VMEM((depth,) + small.shape, BF16),
+        pltpu.VMEM((layers, 8, wide), F32),
+        pltpu.VMEM((layers, 8, ff), F32),
+        pltpu.VMEM((flat, width), F32),
+        pltpu.VMEM((flat, width), BF16),
+        pltpu.VMEM((flat, wide), BF16),
+        pltpu.VMEM((seqs, rows, 2 * wide), BF16),
+        pltpu.VMEM((seqs, slots, 2 * wide), BF16),
+        pltpu.VMEM((seqs, rows, slots), F32),
+        pltpu.VMEM((flat, wide), BF16),
+        pltpu.VMEM((2 * flat, LANES), F32),
+        pltpu.VMEM((flat, width), F32),
+        pltpu.VMEM((flat, width), BF16),
+        pltpu.VMEM((flat, ff), F32),
+        pltpu.VMEM((flat, ff), BF16),
+    ] + [pltpu.VMEM((depth * ref.shape[1], ref.shape[2]), BF16) for ref in (w_qkv, w_out, w_up, w_down)]
+    outs = pl.pallas_call(
+        functools.partial(forward_kernel, dims),
+        out_shape=out_shape,
+        in_specs=[vmem, pl.BlockSpec(memory_space=pltpu.SMEM)] + [any_spec] * 5,
+        out_specs=[vmem, vmem] + [any_spec] * (len(out_shape) - 2),
+        scratch_shapes=scratch,
+        compiler_params=pltpu.CompilerParams(
+            collective_id=0, has_side_effects=True, vmem_limit_bytes=63 * 1024 * 1024
+        ),
+    )(tokens.reshape(flat, width), lengths, w_qkv, w_out, w_up, w_down, small)
+    acts, vecs = outs[:2]
+    wholes = outs[2 : 2 + count]
+    rest = outs[2 + count :]
+    kept = [dict(zip(KEPT, rest[l * len(KEPT) : (l + 1) * len(KEPT)])) for l in range(layers)]
+    return acts, vecs, [wholes[4 * l : 4 * l + 4] for l in range(layers)], kept
 
 
 def normalize(values, scales, shifts):
@@ -801,14 +1245,7 @@
 def pack_small(ln_gain, ln_bias, b_qv, b_out, b_up, b_down):
     layers, _, part = ln_gain.shape
     return jnp.concatenate(
-        [
-            ln_gain.reshape(layers, 2, part),
-            ln_bias.reshape(layers, 2, part),
-            b_qv.reshape(layers, 2, part),
-            b_out.reshape(layers, 1, part),
-            b_down.reshape(layers, 1, part),
-            b_up.reshape(layers, 4, part),
-        ],
+        [ln_gain, ln_bias, b_qv, b_out[:, None], b_down[:, None], b_up.reshape(layers, 4, part)],
         axis=1,
     )
 
@@ -834,14 +1271,8 @@
 def gather_all(weights, small):
     flat = [item for layer in weights for item in layer]
     layers = len(weights)
-    if fast_mesh(flat[0].shape[0]):
-        packed = small.reshape(layers * small.shape[1], small.shape[2])
-        *wholes, small_all = gather_weights(flat, packed)
-        small_all = small_all.reshape(-1, layers, small.shape[1], small.shape[2])
-        wholes = [item.reshape(-1, item.shape[2]) for item in wholes]
-    else:
-        wholes = [lax.all_gather(item, "fsdp", axis=0, tiled=True) for item in flat]
-        small_all = lax.all_gather(small, "fsdp", axis=0)
+    wholes = [lax.all_gather(item, "fsdp", axis=0, tiled=True) for item in flat]
+    small_all = lax.all_gather(small, "fsdp", axis=0)
     return [wholes[4 * i : 4 * i + 4] for i in range(layers)], [small_all[:, i] for i in range(layers)]
 
 
@@ -884,67 +1315,109 @@
     layer_total = ln_gain.shape[0]
     hidden = tokens.astype(jnp.float32).reshape(flat_rows, model_width)
     small = pack_small(ln_gain, ln_bias, b_qv, b_out, b_up, b_down)
-    weights, smalls = gather_all(
-        [(w_qkv[i], w_out[i], w_up[i], w_down[i]) for i in range(layer_total)], small
-    )
-    kept_layers = []
-    for layer_index in range(layer_total):
-        mix_weight, out_weight, up_weight, down_weight = weights[layer_index]
-        gain_rows, shift_rows, mix_bias, out_bias, down_bias, up_bias = unpack_small(
-            smalls[layer_index].astype(jnp.float32)
+    if fast_mesh(w_qkv.shape[1]):
+        part = small.shape[2]
+        padded = jnp.pad(small, ((0, 0), (0, 4), (0, pad_lanes(part) - part)))
+        activations, vectors, weights, kept = forward(
+            tokens, lengths, w_qkv, w_out, w_up, w_down, padded.reshape(layer_total * 16, -1)
         )
-        normed_first = normalize(hidden, gain_rows[0], shift_rows[0]).astype(jnp.bfloat16)
-        mixed_rows = jnp.dot(normed_first, mix_weight, preferred_element_type=jnp.float32)
-        queries = (
-            (mixed_rows[:, :model_width] + mix_bias[0]).astype(jnp.bfloat16).reshape(split_shape)
+        activations = activations.reshape(tokens.shape)
+        kept_layers = []
+        for layer_index in range(layer_total):
+            one = kept[layer_index]
+            wide = one["q"].shape[1]
+            cut = lambda array: array[..., :model_width]
+            heads = cut(one["q"]).reshape(split_shape)
+            kv_shape = (seq_count, -1, head_count, head_width)
+            attended = cut(one["o"])
+            lse = one["lse"].reshape(seq_count, 2, row_count, -1)
+            pairs = wide // LANES
+            log_total = jnp.stack(
+                [
+                    jnp.stack([lse[s, n % 2, :, s * pairs + n // 2] for n in range(head_count)])
+                    for s in range(seq_count)
+                ]
+            )
+            kept_layers.append(
+                (
+                    one["h"],
+                    one["a"],
+                    heads,
+                    cut(one["kv"]).reshape(kv_shape),
+                    cut(one["kv"][..., wide:]).reshape(kv_shape),
+                    attended.astype(jnp.float32),
+                    log_total,
+                    attended,
+                    one["h1"],
+                    one["c"],
+                    one["u"],
+                    jax.nn.gelu(one["u"]).astype(jnp.bfloat16),
+                    cut(vectors[layer_index, 0:2]),
+                    cut(vectors[layer_index, 2:4]),
+                )
+            )
+    else:
+        weights, smalls = gather_all(
+            [(w_qkv[i], w_out[i], w_up[i], w_down[i]) for i in range(layer_total)], small
         )
-        key_rows = (
-            mixed_rows[:, model_width : 2 * model_width].astype(jnp.bfloat16).reshape(split_shape)
+        kept_layers = []
+        for layer_index in range(layer_total):
+            mix_weight, out_weight, up_weight, down_weight = weights[layer_index]
+            gain_rows, shift_rows, mix_bias, out_bias, down_bias, up_bias = unpack_small(
+                smalls[layer_index].astype(jnp.float32)
+            )
+            normed_first = normalize(hidden, gain_rows[0], shift_rows[0]).astype(jnp.bfloat16)
+            mixed_rows = jnp.dot(normed_first, mix_weight, preferred_element_type=jnp.float32)
+            queries = (
+                (mixed_rows[:, :model_width] + mix_bias[0]).astype(jnp.bfloat16).reshape(split_shape)
+            )
+            key_rows = (
+                mixed_rows[:, model_width : 2 * model_width].astype(jnp.bfloat16).reshape(split_shape)
+            )
+            value_rows = (
+                (mixed_rows[:, 2 * model_width :] + mix_bias[1])
+                .astype(jnp.bfloat16)
+                .reshape(split_shape)
+            )
+            key_part = lax.all_gather(key_rows, "ctx", axis=1, tiled=True)
+            value_part = lax.all_gather(value_rows, "ctx", axis=1, tiled=True)
+            output, log_total = attend_forward(
+                queries, key_part, value_part, positions, lengths, score_scale
+            )
+            output = output.reshape(flat_rows, model_width)
+            attended = output.astype(jnp.bfloat16)
+            middle = (
+                hidden + jnp.dot(attended, out_weight, preferred_element_type=jnp.float32) + out_bias
+            )
+            normed_second = normalize(middle, gain_rows[1], shift_rows[1]).astype(jnp.bfloat16)
+            upper_pre = (
+                jnp.dot(normed_second, up_weight, preferred_element_type=jnp.float32) + up_bias
+            )
+            active = jax.nn.gelu(upper_pre).astype(jnp.bfloat16)
+            kept_layers.append(
+                (
+                    hidden,
+                    normed_first,
+                    queries,
+                    key_part,
+                    value_part,
+                    output,
+                    log_total,
+                    attended,
+                    middle,
+                    normed_second,
+                    upper_pre,
+                    active,
+                    gain_rows,
+                    shift_rows,
+                )
+            )
+            hidden = (
+                middle + jnp.dot(active, down_weight, preferred_element_type=jnp.float32) + down_bias
+            )
+        activations = (valid_rows * hidden.reshape(seq_count, row_count, model_width)).astype(
+            jnp.bfloat16
         )
-        value_rows = (
-            (mixed_rows[:, 2 * model_width :] + mix_bias[1])
-            .astype(jnp.bfloat16)
-            .reshape(split_shape)
-        )
-        key_part = lax.all_gather(key_rows, "ctx", axis=1, tiled=True)
-        value_part = lax.all_gather(value_rows, "ctx", axis=1, tiled=True)
-        output, log_total = attend_forward(
-            queries, key_part, value_part, positions, lengths, score_scale
-        )
-        output = output.reshape(flat_rows, model_width)
-        attended = output.astype(jnp.bfloat16)
-        middle = (
-            hidden + jnp.dot(attended, out_weight, preferred_element_type=jnp.float32) + out_bias
-        )
-        normed_second = normalize(middle, gain_rows[1], shift_rows[1]).astype(jnp.bfloat16)
-        upper_pre = (
-            jnp.dot(normed_second, up_weight, preferred_element_type=jnp.float32) + up_bias
-        )
-        active = jax.nn.gelu(upper_pre).astype(jnp.bfloat16)
-        kept_layers.append(
-            (
-                hidden,
-                normed_first,
-                queries,
-                key_part,
-                value_part,
-                output,
-                log_total,
-                attended,
-                middle,
-                normed_second,
-                upper_pre,
-                active,
-                gain_rows,
-                shift_rows,
-            )
-        )
-        hidden = (
-            middle + jnp.dot(active, down_weight, preferred_element_type=jnp.float32) + down_bias
-        )
-    activations = (valid_rows * hidden.reshape(seq_count, row_count, model_width)).astype(
-        jnp.bfloat16
-    )
     grad_hidden = (cotangent.astype(jnp.float32) * valid_rows).reshape(flat_rows, model_width)
     big_grads = [None] * layer_total
     small_grads = [None] * layer_total

time: 1380 us -> 1400 us (1.014)
  waiting for transfers between devices: 153 us -> 0.11 us
  Pallas kernels: 613 us -> 759 us
  local copies, waits for them, and re-layouts: 253 us -> 337 us
  matrix products: 244 us -> 181 us
    pallas_call x1, Pallas kernels: 207 us -> 355 us  [forward(): pl.pallas_call(functools.partial(forward_kernel, dims), out_shape=out_sha...]
    all_gather x4 -> x0, waiting for transfers between devices: 106 us -> none  [the longest x2 53.2 us: shards(): key_part = lax.all_gather(key_rows, 'ctx', axis=1, tiled=True)]
    dot_general x12 -> x2, matrix products: 84 us -> 21.9 us  [block_terms(): jnp.einsum('sqhe,skhe->shqk', queries, key_part, preferred_element_type=j...]
    slice x8 -> x13, local copies, waits for them, and re-layouts: 1.56 us -> 53.3 us  [the longest x7 43.9 us: shards(): cut = lambda array: array[..., :model_width]]
    unnamed x12 -> x8, waiting for transfers between devices: 46.9 us -> 0.11 us
    unnamed x273 -> x294, local copies, waits for them, and re-layouts: 162 us -> 199 us
  transfers between devices with their start and end apart: 8 -> 4, of which waited for: 5 -> 0; matrix products, arithmetic and copies ran while one was open for 18% -> 18% of each run, Pallas kernels for 15% -> 15%
where the time goes in v2:
time: 1400 us; the launch traced here: 1380 us
  Pallas kernels  759 us (54%)
  local copies, waits for them, and re-layouts  337 us (24%)
  matrix products  181 us (13%)
  other arithmetic  51.2 us (4%)
  blocking collectives  37.2 us (3%)
  between operations  15.4 us (1%)
    pallas_call x2, Pallas kernels, reduce_grads(): pl.pallas_call(functools.partial(reduce_kernel, geos, lag), out_shape=[ja...  404 us
    pallas_call x1, Pallas kernels, forward(): pl.pallas_call(functools.partial(forward_kernel, dims), out_shape=out_sha...  355 us
    unnamed x294, local copies, waits for them, and re-layouts  199 us
    dot_general x8, matrix products, outer_sum(): lax.dot_general(left_rows, right_rows, (((0,), (0,)), ((), ())), preferre...  50.7 us
    slice x7, local copies, waits for them, and re-layouts, shards(): cut = lambda array: array[..., :model_width]  43.9 us
    dot_general x8, matrix products, times_transpose(): lax.dot_general(left_rows, weight_rows, (((1,), (1,)), ((), ())), preferr...  39.2 us
    psum x1, blocking collectives, shards(): total = lax.psum(packed, ('fsdp', 'ctx'))  37.2 us
    convert_element_type x2, local copies, waits for them, and re-layouts, shards(): item.astype(jnp.bfloat16)  28.5 us
  transfers between devices with their start and end apart: 4, of which 0 were waited for; matrix products, arithmetic and copies ran while one was open for 18% of the time, Pallas kernels for 15%

profile of v2, /device:TPU:9, one launch (start us, length us, event | category | flops | bytes accessed | tf_op | source)
XLA Modules:
  0.0 1380.7 jit_solution(10817984312115233582)
XLA Ops:
  12.9 355.2 %shard_map.220 = (bf16[256,1088]{1,0:T(8,128)(2,1)}, f32[2,8,1152]{2,1,0:T(8,128)}, bf16[1088,3264]{1,0:T(8,128)(2,1)}, bf16[1088,1088]{1,0:T(8,128)(2,1)}, bf16...) custom-call(bf16[256,1088]{1,0:T(8,128)(2,1)} %bitcast.264, ...), custom_call_target="tpu_custom_call" | custom-call | tf_op jit(solution)/shard_map/pallas_call | solution.py:1139
  403.8 14.1 %fusion.91 = (bf16[2,1024,1088]{2,1,0:T(8,128)(2,1)}, bf16[2,1024,1088]{2,1,0:T(8,128)(2,1)}, bf16[2,1024,1088]{2,1,0:T(8,128)(2,1)}, bf16[2,1024,1088]{2,1,0:T(8,128)(2,1)}) fusion(bf16[2,1024,2304]{2,1,0:T(8,128)(2,1)} %get-tuple-element.49, bf16[2,1024,2304]{2,1,0:T(8,128)(2,1)} %get-tuple-element.52), kind=kLoop, calls=%fused_computation.198 | loop fusion | bytes 35651584 | tf_op jit(solution)/shard_map/slice | solution.py:1329
  457.7 11.0 fusion.53
  469.6 11.7 multiply_convert_fusion.1
  488.3 15.0 %copy.592 = bf16[2,1024,17,64]{3,2,0,1:T(8,128)(2,1)} copy(bf16[2,1024,17,64]{1,3,2,0:T(8,128)(2,1)} %fusion.30) | data formatting | bytes 8912896
  503.3 15.3 %reshape.427 = bf16[1024,2176]{1,0:T(8,128)(2,1)} reshape(bf16[1024,2,17,64]{3,2,1,0:T(8,128)(2,1)} %bitcast.231) | data formatting | bytes 8912896
  519.4 10.5 convert_bitcast_fusion.1
  529.8 15.0 %copy.594 = bf16[2,1024,17,64]{3,2,0,1:T(8,128)(2,1)} copy(bf16[2,1024,17,64]{1,3,2,0:T(8,128)(2,1)} %convert_bitcast_fusion.1) | data formatting | bytes 8912896
  544.8 15.4 %reshape.429 = bf16[1024,2176]{1,0:T(8,128)(2,1)} reshape(bf16[1024,2,17,64]{3,2,1,0:T(8,128)(2,1)} %bitcast.232) | data formatting | bytes 8912896
  560.3 8.6 fusion.100
  626.0 10.9 fusion.56
  699.1 12.1 multiply_convert_fusion
  719.2 15.0 %copy.596 = bf16[2,1024,17,64]{3,2,0,1:T(8,128)(2,1)} copy(bf16[2,1024,17,64]{1,3,2,0:T(8,128)(2,1)} %fusion.31) | data formatting | bytes 8912896
  734.1 15.3 %reshape.431 = bf16[1024,2176]{1,0:T(8,128)(2,1)} reshape(bf16[1024,2,17,64]{3,2,1,0:T(8,128)(2,1)} %bitcast.233) | data formatting | bytes 8912896
  752.7 9.2 convolution_convert_fusion
  761.9 14.4 %copy.585 = bf16[4352,1088]{1,0:T(8,128)(2,1)} copy(bf16[4352,1088]{0,1:T(8,128)(2,1)} %convolution_convert_fusion) | data formatting | bytes 18939904 | tf_op jit(solution)/shard_map/convert_element_type | solution.py:1495
  778.7 10.3 convert_bitcast_fusion
  789.0 14.9 %copy.598 = bf16[2,1024,17,64]{3,2,0,1:T(8,128)(2,1)} copy(bf16[2,1024,17,64]{1,3,2,0:T(8,128)(2,1)} %convert_bitcast_fusion) | data formatting | bytes 8912896
  803.9 15.8 %reshape.433 = bf16[1024,2176]{1,0:T(8,128)(2,1)} reshape(bf16[1024,2,17,64]{3,2,1,0:T(8,128)(2,1)} %bitcast.234) | data formatting | bytes 8912896
  839.8 8.9 convolution_convert_fusion.2
  848.6 14.1 %copy.584 = bf16[4352,1088]{1,0:T(8,128)(2,1)} copy(bf16[4352,1088]{0,1:T(8,128)(2,1)} %convolution_convert_fusion.2) | data formatting | bytes 18939904 | tf_op jit(solution)/shard_map/convert_element_type | solution.py:1495
  869.1 203.9 %shard_map.222 = (bf16[272,4352]{1,0:T(8,128)(2,1)}, bf16[1088,1088]{1,0:T(8,128)(2,1)}, bf16[272,3264]{1,0:T(8,128)(2,1)}, bf16[272,1088]{1,0:T(8,128)(2,1)}) custom-call(bf16[4,272,4352]{2,1,0:T(8,128)(2,1)} %bitcast.236, bf16[4,1088,1088]{2,1,0:T(8,128)(2,1)} %bitcast.240, bf16[4,272,3264]{2,1,0:T(8,128)(2,1)} %bitcast.238, bf16[4,272,1088]{2,1,0:T(8,128)(2,1)} %bitcast.254), custom_call_target="tpu_custom_call" | custom-call | tf_op jit(solution)/shard_map/pallas_call | solution.py:593
  1106.1 37.2 %psum.7 = bf16[2,4,12,272]{3,0,2,1:T(2,128)(2,1)S(1)} all-reduce(bf16[2,4,12,272]{3,0,2,1:T(2,128)(2,1)S(1)} %pad_maximum_fusion), channel_id=1, replica_groups=mesh['fsdp'=4,'ctx'=8] {'fsdp','ctx'}, use_global_device_ids=true, to_apply=%region_40.41 | all-reduce | flops 26112 | bytes 104448 | tf_op jit(solution)/shard_map/psum | solution.py:1509
  1156.5 200.1 %shard_map.221 = (bf16[272,4352]{1,0:T(8,128)(2,1)}, bf16[1088,1088]{1,0:T(8,128)(2,1)}, bf16[272,3264]{1,0:T(8,128)(2,1)}, bf16[272,1088]{1,0:T(8,128)(2,1)}) custom-call(bf16[4,272,4352]{2,1,0:T(8,128)(2,1)} %bitcast.235, bf16[4,1088,1088]{2,1,0:T(8,128)(2,1)} %bitcast.239, bf16[4,272,3264]{2,1,0:T(8,128)(2,1)} %bitcast.237, bf16[4,272,1088]{2,1,0:T(8,128)(2,1)} %bitcast.253), custom_call_target="tpu_custom_call" | custom-call | tf_op jit(solution)/shard_map/pallas_call | solution.py:593
  (453 shorter events, 311.5 us)
Async XLA Ops:
  7.2 629.8 %reduce-scatter.13.cloned.1.call-start = ((), (), s32[]{:S(2)}) async-start(), calls=%async_computation.4 | async-start | bytes 5013504
  428.5 21.7 %copy-start.48 = (f32[1,1,128,1]{3,2,1,0:T(8,128)S(1)}, f32[1,1,128,1]{3,2,1,0:T(8,128)}, u32[]{:S(2)}) copy-start(f32[1,1,128,1]{3,2,1,0:T(8,128)} %get-tuple-element.239) | copy-start | bytes 1540
  428.5 21.8 %copy-start.47 = (f32[1,1,128,1]{3,2,1,0:T(8,128)S(1)}, f32[1,1,128,1]{3,2,1,0:T(8,128)}, u32[]{:S(2)}) copy-start(f32[1,1,128,1]{3,2,1,0:T(8,128)} %get-tuple-element.238) | copy-start | bytes 1540
  428.5 21.8 %copy-start.46 = (f32[1,1,128,1]{3,2,1,0:T(8,128)S(1)}, f32[1,1,128,1]{3,2,1,0:T(8,128)}, u32[]{:S(2)}) copy-start(f32[1,1,128,1]{3,2,1,0:T(8,128)} %get-tuple-element.237) | copy-start | bytes 1540
  428.5 21.9 %copy-start.45 = (f32[1,1,128,1]{3,2,1,0:T(8,128)S(1)}, f32[1,1,128,1]{3,2,1,0:T(8,128)}, u32[]{:S(2)}) copy-start(f32[1,1,128,1]{3,2,1,0:T(8,128)} %get-tuple-element.236) | copy-start | bytes 1540
  428.5 22.0 %copy-start.44 = (f32[1,1,128,1]{3,2,1,0:T(8,128)S(1)}, f32[1,1,128,1]{3,2,1,0:T(8,128)}, u32[]{:S(2)}) copy-start(f32[1,1,128,1]{3,2,1,0:T(8,128)} %get-tuple-element.235) | copy-start | bytes 1540
  428.5 22.1 %copy-start.43 = (f32[1,1,128,1]{3,2,1,0:T(8,128)S(1)}, f32[1,1,128,1]{3,2,1,0:T(8,128)}, u32[]{:S(2)}) copy-start(f32[1,1,128,1]{3,2,1,0:T(8,128)} %get-tuple-element.234) | copy-start | bytes 1540
  428.5 22.1 %copy-start.42 = (f32[1,1,128,1]{3,2,1,0:T(8,128)S(1)}, f32[1,1,128,1]{3,2,1,0:T(8,128)}, u32[]{:S(2)}) copy-start(f32[1,1,128,1]{3,2,1,0:T(8,128)} %get-tuple-element.233) | copy-start | bytes 1540
  428.5 22.2 %copy-start.41 = (f32[1,1,128,1]{3,2,1,0:T(8,128)S(1)}, f32[1,1,128,1]{3,2,1,0:T(8,128)}, u32[]{:S(2)}) copy-start(f32[1,1,128,1]{3,2,1,0:T(8,128)} %get-tuple-element.232) | copy-start | bytes 1540
  429.7 20.1 %copy-start.54 = (f32[1,1,128,1]{3,2,1,0:T(8,128)S(1)}, f32[1,1,128,1]{3,2,1,0:T(8,128)}, u32[]{:S(2)}) copy-start(f32[1,1,128,1]{3,2,1,0:T(8,128)} %get-tuple-element.243) | copy-start | bytes 1540
  429.8 20.2 %copy-start.52 = (f32[1,1,128,1]{3,2,1,0:T(8,128)S(1)}, f32[1,1,128,1]{3,2,1,0:T(8,128)}, u32[]{:S(2)}) copy-start(f32[1,1,128,1]{3,2,1,0:T(8,128)} %get-tuple-element.242) | copy-start | bytes 1540
  429.8 20.2 %copy-start.50 = (f32[1,1,128,1]{3,2,1,0:T(8,128)S(1)}, f32[1,1,128,1]{3,2,1,0:T(8,128)}, u32[]{:S(2)}) copy-start(f32[1,1,128,1]{3,2,1,0:T(8,128)} %get-tuple-element.241) | copy-start | bytes 1540
  429.8 20.3 %copy-start.49 = (f32[1,1,128,1]{3,2,1,0:T(8,128)S(1)}, f32[1,1,128,1]{3,2,1,0:T(8,128)}, u32[]{:S(2)}) copy-start(f32[1,1,128,1]{3,2,1,0:T(8,128)} %get-tuple-element.240) | copy-start | bytes 1540
  429.8 21.1 %copy-start.40 = (f32[1,1,128,1]{3,2,1,0:T(8,128)S(1)}, f32[1,1,128,1]{3,2,1,0:T(8,128)}, u32[]{:S(2)}) copy-start(f32[1,1,128,1]{3,2,1,0:T(8,128)} %get-tuple-element.231) | copy-start | bytes 1540
  429.8 21.1 %copy-start.39 = (f32[1,1,128,1]{3,2,1,0:T(8,128)S(1)}, f32[1,1,128,1]{3,2,1,0:T(8,128)}, u32[]{:S(2)}) copy-start(f32[1,1,128,1]{3,2,1,0:T(8,128)} %get-tuple-element.230) | copy-start | bytes 1540
  429.8 21.2 %copy-start.38 = (f32[1,1,128,1]{3,2,1,0:T(8,128)S(1)}, f32[1,1,128,1]{3,2,1,0:T(8,128)}, u32[]{:S(2)}) copy-start(f32[1,1,128,1]{3,2,1,0:T(8,128)} %get-tuple-element.229) | copy-start | bytes 1540
  429.8 21.3 %copy-start.37 = (f32[1,1,128,1]{3,2,1,0:T(8,128)S(1)}, f32[1,1,128,1]{3,2,1,0:T(8,128)}, u32[]{:S(2)}) copy-start(f32[1,1,128,1]{3,2,1,0:T(8,128)} %get-tuple-element.212) | copy-start | bytes 1540
  469.6 49.1 %copy-start.58 = (pred[2,128,1024]{2,1,0:T(8,128)(4,1)}, pred[2,128,1024]{2,1,0:T(8,128)(4,1)S(1)}, u32[]{:S(2)}) copy-start(pred[2,128,1024]{2,1,0:T(8,128)(4,1)S(1)} %broadcast_and_fusion) | copy-start | bytes 786436
  518.6 124.5 %reduce-scatter.15.cloned.1.call-start = ((), (), s32[]{:S(2)}) async-start(), calls=%async_computation.5 | async-start | bytes 5013504
  560.3 522.6 %reduce-scatter.17.cloned.1.call-start = ((), (), s32[]{:S(2)}) async-start(), calls=%async_computation.6 | async-start | bytes 5013504
  581.6 44.4 %copy-start.9 = (bf16[2,128,17,64]{1,0,3,2:T(2,128)(2,1)}, bf16[2,128,17,64]{1,0,3,2:T(2,128)(2,1)S(1)}, u32[]{:S(2)}) copy-start(bf16[2,128,17,64]{1,0,3,2:T(2,128)(2,1)S(1)} %reshape.398) | copy-start | bytes 1671172
  749.5 337.2 %reduce-scatter.19.cloned.1.call-start = ((), (), s32[]{:S(2)}) async-start(), calls=%async_computation.7 | async-start | bytes 5013504
  869.1 204.0 %copy-start.17 = (bf16[256,1152]{1,0:T(8,128)(2,1)S(1)}, bf16[256,1152]{1,0:T(8,128)(2,1)}, u32[]{:S(2)}) copy-start(bf16[256,1152]{1,0:T(8,128)(2,1)} %get-tuple-element.69) | copy-start | bytes 1769476
  1156.5 200.1 %copy-start.26 = (bf16[272,3264]{1,0:T(8,128)(2,1)S(1)}, bf16[272,3264]{1,0:T(8,128)(2,1)}, u32[]{:S(2)}) copy-start(bf16[272,3264]{1,0:T(8,128)(2,1)} %get-tuple-element.77) | copy-start | bytes 5326852
  (76 other events, 549.2 us)
Sparse Core Ops, SparseCore 0:
  518.8 54.5 reduce-scatter.12
  577.2 52.6 reduce-scatter.14
  749.7 54.8 reduce-scatter.16
  819.9 54.7 reduce-scatter.18

commit v3 on v2

--- a/solution.py
+++ b/solution.py
@@ -259,351 +259,7 @@
     lax.fori_loop(0, rows // 16, step, 0)
 
 
-class Geometry:
-    def __init__(self, rows, cols, line_part):
-        self.rows, self.cols = rows, cols
-        unit = rows // 17
-        self.unit = unit
-        self.block = 8 * unit
-        self.t2 = line_part
-        self.t1 = 2 * unit - line_part
-
-    def scratch(self, depth):
-        cols = self.cols
-        vm = lambda *shape: pltpu.VMEM(shape + (cols,), jnp.bfloat16)
-        out = [
-            vm(depth, self.block),
-            vm(depth, self.block),
-            vm(3, depth, self.t1),
-            vm(depth + 1, self.t1),
-            vm(depth, self.unit),
-            vm(depth + 1, self.unit),
-            vm(depth, self.unit),
-            vm(2, self.unit),
-        ]
-        if self.t2:
-            out += [vm(depth + 1, 4 * self.t2), vm(3, self.t2)]
-        return out
-
-
-SLOTS = 48
-
-
-class Reduce:
-    def __init__(self, at, geo, part, out, left_core, bufs, send, recv, local):
-        self.at, self.geo, self.part, self.out = at, geo, part, out
-        self.acc, self.sib_in, self.plane_in, self.z_in, self.racc, self.rz_in, self.rsib_in, self.rplane_in = bufs[:8]
-        if geo.t2:
-            self.z2_in, self.plane2_in = bufs[8:]
-        self.send, self.recv, self.local = send, recv, local
-        self.has_rest = at.core == left_core
-        self.no_rest = at.core != left_core
-        self.rest = pl.ds(16 * geo.unit, geo.unit)
-        self.names, self.posts = {}, []
-        core, p = at.core, at.p
-        self.direct_p = p + (1 - core) * (2 - 4 * at.py) + core * (1 - 2 * at.px)
-        self.owner_dev = {
-            "ctx": at.c8 + (1 - core) * (2 - 4 * at.px) + core * (4 - 8 * at.py)
-        }
-
-    def slot(self, name):
-        return self.names.setdefault(name, len(self.names))
-
-    def make(self, name, src, dst, device):
-        i = self.slot(name)
-        return remote(src, dst, self.send.at[i], self.recv.at[i], device)
-
-    def post(self, name, src, dst, device, cond=None):
-        under(cond, lambda: self.make(name, src, dst, device).start())
-        self.posts.append((name, src, dst, device, cond))
-
-    def take(self, name, dst, cond=None):
-        under(cond, lambda: self.make(name, dst, dst, self.at.sib).wait_recv())
-
-    def c1(self, p):
-        return pl.ds(pl.multiple_of(p * self.geo.t1, 16), self.geo.t1)
-
-    def c2(self, p):
-        return pl.ds(pl.multiple_of(4 * self.geo.t1 + p * self.geo.t2, 16), self.geo.t2)
-
-    def o1(self, p, core):
-        return pl.ds(pl.multiple_of(core * self.geo.block + p * self.geo.t1, 16), self.geo.t1)
-
-    def o2(self, p, core):
-        return pl.ds(
-            pl.multiple_of(core * self.geo.block + 4 * self.geo.t1 + p * self.geo.t2, 16), self.geo.t2
-        )
-
-    def begin(self):
-        at, geo = self.at, self.geo
-        mine = pl.ds(pl.multiple_of(at.core * geo.block, 16), geo.block)
-        other = pl.ds(pl.multiple_of((1 - at.core) * geo.block, 16), geo.block)
-        self.post("sib", self.part.at[:, other], self.sib_in, at.sib)
-        self.post("rsib", self.part.at[:, self.rest], self.rsib_in, at.sib, self.no_rest)
-        self.load = pltpu.make_async_copy(self.part.at[:, mine], self.acc, self.local.at[0])
-        self.load.start()
-        self.rload = pltpu.make_async_copy(self.part.at[:, self.rest], self.racc, self.local.at[1])
-        pl.when(self.has_rest)(lambda: self.rload.start())
-
-    def cores(self):
-        at, geo = self.at, self.geo
-        self.load.wait()
-        self.take("sib", self.sib_in)
-        for t in range(at.depth):
-            add_rows(self.acc.at[t], self.sib_in.at[t], geo.block)
-        self.post("diag", self.acc.at[:, self.c1(at.p_d)], self.plane_in.at[0], at.relay_dev)
-        self.post("near", self.acc.at[:, self.c1(self.direct_p)], self.plane_in.at[1], at.relay_dev)
-
-        def rest():
-            self.rload.wait()
-            self.make("rsib", self.rsib_in, self.rsib_in, at.sib).wait_recv()
-            for t in range(at.depth):
-                add_rows(self.racc.at[t], self.rsib_in.at[t], geo.unit)
-
-        pl.when(self.has_rest)(rest)
-
-    def line(self, step, name, acc, landing, rows, cond=None):
-        at = self.at
-        last = at.depth - 1
-        right, left = last - step, step
-
-        def go_right():
-            @pl.when(at.z > 0)
-            def _():
-                self.make(f"{name}{right}", landing.at[right], landing.at[right], at.sib).wait_recv()
-                add_rows(acc(right), landing.at[right], rows)
-
-        def go_left():
-            @pl.when(at.z < last)
-            def _():
-                self.make(f"{name}{left}", landing.at[left], landing.at[left], at.sib).wait_recv()
-                add_rows(acc(left), landing.at[left], rows)
-
-        is_right, is_left = both(at.z < right, cond), both(at.z > left, cond)
-        under(is_right, go_right)
-        self.post(f"{name}{right}", acc(right), landing.at[right], at.up(), is_right)
-        under(is_left, go_left)
-        self.post(f"{name}{left}", acc(left), landing.at[left], at.down(), both(at.z > left + 1, cond))
-        self.post(f"{name}end{left}", acc(left), landing.at[at.depth], at.down(), both(at.z == left + 1, cond))
-
-    def line_end(self, name, acc, landing, rows, cond=None):
-        at = self.at
-        last = at.depth - 1
-        for t in range(at.depth):
-            def from_below():
-                self.make(f"{name}{t}", landing.at[t], landing.at[t], at.sib).wait_recv()
-                add_rows(acc(t), landing.at[t], rows)
-
-            def from_above():
-                self.make(f"{name}end{t}", landing.at[at.depth], landing.at[at.depth], at.sib).wait_recv()
-                add_rows(acc(t), landing.at[at.depth], rows)
-
-            if t > 0:
-                under(both(at.z == t, cond), from_below)
-            if t < last:
-                under(both(at.z == t, cond), from_above)
-
-    def relay(self):
-        at, geo = self.at, self.geo
-        self.take("diag", self.plane_in.at[0])
-        mine = self.c1(at.relay_from)
-        for t in range(at.depth):
-            add_rows(self.acc.at[t, mine], self.plane_in.at[0, t], geo.t1)
-        self.post("relay", self.acc.at[:, mine], self.plane_in.at[2], self.owner_dev)
-
-    def combine(self):
-        at, geo = self.at, self.geo
-        self.take("near", self.plane_in.at[1])
-        self.take("relay", self.plane_in.at[2])
-        mine = self.c1(at.p)
-        for t in range(at.depth):
-            add_rows_two(self.acc.at[t, mine], self.plane_in.at[1, t], self.plane_in.at[2, t], geo.t1)
-
-    def line1(self, step):
-        mine = self.c1(self.at.p)
-        self.line(step, "z", lambda t: self.acc.at[t, mine], self.z_in, self.geo.t1)
-
-    def line1_end(self):
-        at, geo = self.at, self.geo
-        mine = self.c1(at.p)
-        self.line_end("z", lambda t: self.acc.at[t, mine], self.z_in, geo.t1)
-        self.spread("a", self.acc.at[at.z, mine], self.o1)
-
-    def line2(self, step):
-        at, geo = self.at, self.geo
-        if geo.t2:
-            span = pl.ds(4 * geo.t1, 4 * geo.t2)
-            self.line(step, "w", lambda t: self.acc.at[t, span], self.z2_in, 4 * geo.t2)
-        self.line(step, "r", lambda t: self.racc.at[t], self.rz_in, geo.unit, self.has_rest)
-
-    def line2_end(self):
-        at, geo = self.at, self.geo
-        self.line_end("r", lambda t: self.racc.at[t], self.rz_in, geo.unit, self.has_rest)
-        self.post("rx", self.racc.at[at.z], self.rplane_in.at[0], at.x_dev, self.has_rest)
-        if geo.t2:
-            span = pl.ds(4 * geo.t1, 4 * geo.t2)
-            self.line_end("w", lambda t: self.acc.at[t, span], self.z2_in, 4 * geo.t2)
-            self.post("diag2", self.acc.at[at.z, self.c2(at.p_d)], self.plane2_in.at[0], at.relay_dev)
-            self.post("near2", self.acc.at[at.z, self.c2(self.direct_p)], self.plane2_in.at[1], at.relay_dev)
-
-    def relay2(self):
-        at, geo = self.at, self.geo
-        if geo.t2:
-            self.take("diag2", self.plane2_in.at[0])
-            mine = self.c2(at.relay_from)
-            add_rows(self.acc.at[at.z, mine], self.plane2_in.at[0], geo.t2)
-            self.post("relay2", self.acc.at[at.z, mine], self.plane2_in.at[2], self.owner_dev)
-
-    def rest_x(self):
-        at, geo = self.at, self.geo
-
-        def rest():
-            self.make("rx", self.rplane_in.at[0], self.rplane_in.at[0], at.sib).wait_recv()
-            self.make("rx", self.racc.at[at.z], self.rplane_in.at[0], at.x_dev).wait_send()
-            add_rows(self.racc.at[at.z], self.rplane_in.at[0], geo.unit)
-
-        pl.when(self.has_rest)(rest)
-        self.posts = [item for item in self.posts if item[0] != "rx"]
-        self.post("ry", self.racc.at[at.z], self.rplane_in.at[1], at.y_dev, self.has_rest)
-
-    def rest_y(self):
-        at, geo = self.at, self.geo
-
-        def rest():
-            self.make("ry", self.rplane_in.at[1], self.rplane_in.at[1], at.sib).wait_recv()
-            self.make("ry", self.racc.at[at.z], self.rplane_in.at[1], at.y_dev).wait_send()
-            add_rows(self.racc.at[at.z], self.rplane_in.at[1], geo.unit)
-            pltpu.make_async_copy(self.racc.at[at.z], self.out.at[self.rest], self.local.at[2]).start()
-
-        pl.when(self.has_rest)(rest)
-        self.posts = [item for item in self.posts if item[0] != "ry"]
-        self.post("rout", self.racc.at[at.z], self.out.at[self.rest], at.sib, self.has_rest)
-
-    def combine2(self):
-        at, geo = self.at, self.geo
-        if geo.t2:
-            self.take("near2", self.plane2_in.at[1])
-            self.take("relay2", self.plane2_in.at[2])
-            mine = self.c2(at.p)
-            add_rows_two(self.acc.at[at.z, mine], self.plane2_in.at[1], self.plane2_in.at[2], geo.t2)
-            self.spread("b", self.acc.at[at.z, mine], self.o2)
-
-    def spread(self, name, src, rows):
-        at = self.at
-        mine = rows(at.p, at.core)
-        index = 3 if name == "a" else 4
-        pltpu.make_async_copy(src, self.out.at[mine], self.local.at[index]).start()
-        self.post(name + "x", src, self.out.at[mine], at.x_dev)
-        self.post(name + "y", src, self.out.at[mine], at.y_dev)
-        self.post(name + "s", src, self.out.at[mine], at.sib)
-
-    def spread_relay(self, name, rows):
-        at = self.at
-        for far, place in ((name + "x", at.p_x), (name + "y", at.p_y)):
-            here = self.out.at[rows(place, at.core)]
-            self.take(far, here)
-            self.post(far + "s", here, here, at.sib)
-        here = self.out.at[rows(at.relay_from, at.core)]
-        self.post(name + "d", here, here, at.relay_dev)
-
-    def spread_last(self, name, rows):
-        at = self.at
-        here = self.out.at[rows(at.p_d, at.core)]
-        self.take(name + "d", here)
-        self.post(name + "ds", here, here, at.sib)
-
-    def spread_end(self, name, src, rows):
-        at = self.at
-        for suffix, place in (("s", at.p), ("xs", at.p_x), ("ys", at.p_y), ("ds", at.p_d)):
-            self.take(name + suffix, self.out.at[rows(place, 1 - at.core)])
-        index = 3 if name == "a" else 4
-        pltpu.make_async_copy(src, self.out.at[rows(at.p, at.core)], self.local.at[index]).wait()
-
-    def finish(self):
-        at = self.at
-        self.spread_end("a", self.acc.at[at.z, self.c1(at.p)], self.o1)
-        if self.geo.t2:
-            self.spread_end("b", self.acc.at[at.z, self.c2(at.p)], self.o2)
-        pl.when(self.has_rest)(
-            lambda: pltpu.make_async_copy(self.racc.at[at.z], self.out.at[self.rest], self.local.at[2]).wait()
-        )
-        self.take("rout", self.out.at[self.rest], self.no_rest)
-
-    def drain(self):
-        for name, src, dst, device, cond in self.posts:
-            under(cond, lambda: self.make(name, src, dst, device).wait_send())
-
-    def stages(self):
-        steps = range(self.at.depth - 1)
-        has2 = bool(self.geo.t2)
-        return [
-            [self.cores],
-            [functools.partial(self.line2, i) for i in steps[:1]] + [self.relay],
-            [functools.partial(self.line2, i) for i in steps[1:]] + [self.combine],
-            [self.line2_end] + [functools.partial(self.line1, i) for i in steps[:1]],
-            [self.relay2, self.rest_x] + [functools.partial(self.line1, i) for i in steps[1:2]],
-            [self.combine2, self.rest_y] + [functools.partial(self.line1, i) for i in steps[2:]],
-            [self.line1_end] + ([functools.partial(self.spread_relay, "b", self.o2)] if has2 else []),
-            [functools.partial(self.spread_relay, "a", self.o1)]
-            + ([functools.partial(self.spread_last, "b", self.o2)] if has2 else []),
-            [functools.partial(self.spread_last, "a", self.o1)],
-            [self.finish],
-        ]
-
-
-def reduce_kernel(geos, lag, *refs):
-    count = len(geos)
-    parts, outs = refs[:count], refs[count : 2 * count]
-    send, recv, local = refs[2 * count : 2 * count + 3]
-    rest = list(refs[2 * count + 3 :])
-    at = Place()
-    at.greet()
-    items = []
-    for k, geo in enumerate(geos):
-        size = 10 if geo.t2 else 8
-        bufs, rest = rest[:size], rest[size:]
-        items.append(
-            Reduce(at, geo, parts[k], outs[k], k % 2, bufs, send.at[k], recv.at[k], local.at[k])
-        )
-    for item in items:
-        item.begin()
-    plan = []
-    for k, item in enumerate(items):
-        for s, todo in enumerate(item.stages()):
-            plan.append((s + lag * k, k, todo))
-    for _, _, todo in sorted(plan, key=lambda entry: entry[:2]):
-        for do in todo:
-            do()
-    for item in items:
-        item.drain()
-
-
-def reduce_grads(parts, line_parts, collective_id, lag=2):
-    depth = lax.axis_size("fsdp")
-    geos = [Geometry(item.shape[1], item.shape[2], b) for item, b in zip(parts, line_parts)]
-    any_spec = pl.BlockSpec(memory_space=pl.ANY)
-    count = len(parts)
-    scratch = [
-        pltpu.SemaphoreType.DMA((count, SLOTS)),
-        pltpu.SemaphoreType.DMA((count, SLOTS)),
-        pltpu.SemaphoreType.DMA((count, 5)),
-    ]
-    for geo in geos:
-        scratch += geo.scratch(depth)
-    return pl.pallas_call(
-        functools.partial(reduce_kernel, geos, lag),
-        out_shape=[jax.ShapeDtypeStruct(item.shape[1:], item.dtype) for item in parts],
-        in_specs=[any_spec] * count,
-        out_specs=[any_spec] * count,
-        scratch_shapes=scratch,
-        compiler_params=pltpu.CompilerParams(
-            collective_id=collective_id, has_side_effects=True, vmem_limit_bytes=60 * 1024 * 1024
-        ),
-    )(*parts)
-
-
 HEAD_DIM = 64
-
 LANES = 128
 F32, BF16 = jnp.float32, jnp.bfloat16
 
@@ -637,8 +293,31 @@
 GELU_B = 0.044715
 
 
-def gelu_of(u):
-    return 0.5 * u * (1.0 + jnp.tanh(GELU_A * (u + GELU_B * u * u * u)))
+def gelu_both(u):
+    square = u * u
+    bent = jnp.tanh(GELU_A * (u + GELU_B * u * square))
+    half = 0.5 * (1.0 + bent)
+    slope = half + 0.5 * u * (1.0 - bent * bent) * (GELU_A * (1.0 + 3.0 * GELU_B * square))
+    return u * half, slope
+
+
+def cut_pieces(src, dst, part, first):
+    depth = 4
+
+    def do(off, size):
+        here = pl.ds(off, size)
+        left = []
+        for t in range(depth):
+            start = (first + t * (src.shape[1] // part // depth)) * part
+            block = src[here, pl.ds(start, part)]
+            for core in range(2):
+                dst[core, here, pl.ds(t * LANES, LANES)] = block[:, core * LANES : (core + 1) * LANES]
+            left.append(block[:, 2 * LANES :])
+        rest = jnp.concatenate(left + [jnp.zeros_like(left[0])] * 4, axis=1)
+        for core in range(2):
+            dst[core, here, pl.ds(depth * LANES, LANES)] = rest
+
+    by_tiles(src.shape[0], 64, do)
 
 
 class Context:
@@ -699,7 +378,8 @@
                 self.make(name, src, dst, device).wait_send()
 
 
-KEPT = ("h", "a", "q", "kv", "o", "lse", "h1", "c", "u")
+KEPT = ("h", "pa", "q", "kv", "o", "po", "lse", "h1", "pc", "pz", "dg")
+PIECE = 5 * LANES
 
 
 def kept_shapes(seqs, slots, rows, width, ff):
@@ -707,14 +387,16 @@
     flat = seqs * rows
     return {
         "h": ((flat, width), F32),
-        "a": ((flat, width), BF16),
+        "pa": ((2, flat, PIECE), BF16),
         "q": ((flat, wide), BF16),
         "kv": ((seqs, slots, 2 * wide), BF16),
         "o": ((flat, wide), BF16),
+        "po": ((2, flat, PIECE), BF16),
         "lse": ((flat * 2, LANES), F32),
         "h1": ((flat, width), F32),
-        "c": ((flat, width), BF16),
-        "u": ((flat, ff), F32),
+        "pc": ((2, flat, PIECE), BF16),
+        "pz": ((2, 4, flat, PIECE), BF16),
+        "dg": ((flat, ff), BF16),
     }
 
 
@@ -771,6 +453,7 @@
     layers, seqs, rows, slots, width, ff, depth = dims
     flat, wide = seqs * rows, pad_lanes(width)
     pairs = wide // LANES
+    part = width // depth
     refs = list(refs)
 
     def grab(n):
@@ -783,7 +466,7 @@
     wholes = grab(4 * layers)
     kept = [dict(zip(KEPT, grab(len(KEPT)))) for _ in range(layers)]
     (send, recv, small_send, small_recv, kv_send, kv_recv, load_sem, keep_sem, stage_sem) = grab(9)
-    (small_all, vec, up_bias, h, a, q, own_kv, kv, bias, o, lse, h1, c, u, z) = grab(15)
+    (small_all, vec, up_bias, h, a, q, own_kv, kv, bias, o, lse, h1, c, u, z, dg, pa, pc, po, pz) = grab(20)
     w_bufs = grab(4)
     at = Place()
     at.greet()
@@ -953,8 +636,9 @@
         def do(first, size):
             cols = pl.ds(first, size)
             pre = jnp.dot(c[...], w_bufs[2][:, cols], preferred_element_type=F32) + up_bias[l, pl.ds(0, 1), cols]
-            u[:, cols] = pre
-            z[:, cols] = gelu_of(pre).astype(BF16)
+            value, slope = gelu_both(pre)
+            z[:, cols] = value.astype(BF16)
+            dg[:, cols] = slope.astype(BF16)
 
         by_tiles(ff, 256, do)
 
@@ -1026,13 +710,13 @@
         own_done(k)
     for l in range(layers):
         k = 4 * l
-        free(l - 1, "a")
         norm(l, 0, h, a)
         keep(l, "h", h)
-        keep(l, "a", a)
+        free(l - 1, "pa")
+        cut_pieces(a, pa, part, 0)
+        keep(l, "pa", pa)
         reach(k)
         fetch(k)
-        free(l - 1, "u")
         free(l - 1, "q")
         if l:
             contexts[l - 1].drain(True)
@@ -1061,18 +745,27 @@
             tick(2)
         keep(l, "o", o)
         keep(l, "lse", lse)
+        free(l - 1, "po")
+        cut_pieces(o.at[:, pl.ds(0, wide)], po, part, 0)
+        keep(l, "po", po)
         ready(k + 1)
         free(l - 1, "h1")
         project(l)
         keep(l, "h1", h1)
-        free(l - 1, "c")
         norm(l, 1, h1, c)
-        keep(l, "c", c)
+        free(l - 1, "pc")
+        cut_pieces(c, pc, part, 0)
+        keep(l, "pc", pc)
         reach(k + 2)
         fetch(k + 2)
         ready(k + 2)
+        free(l - 1, "dg")
         rise(l)
-        keep(l, "u", u)
+        keep(l, "dg", dg)
+        free(l - 1, "pz")
+        for i in range(4):
+            cut_pieces(z, pz.at[:, i], part, i)
+        keep(l, "pz", pz)
         reach(k + 3)
         fetch(k + 3)
         free(l, "h")
@@ -1133,8 +826,13 @@
         pltpu.VMEM((2 * flat, LANES), F32),
         pltpu.VMEM((flat, width), F32),
         pltpu.VMEM((flat, width), BF16),
-        pltpu.VMEM((flat, ff), F32),
+        pltpu.VMEM((flat, 3 * width), F32),
         pltpu.VMEM((flat, ff), BF16),
+        pltpu.VMEM((flat, ff), BF16),
+        pltpu.VMEM((2, flat, PIECE), BF16),
+        pltpu.VMEM((2, flat, PIECE), BF16),
+        pltpu.VMEM((2, flat, PIECE), BF16),
+        pltpu.VMEM((2, 4, flat, PIECE), BF16),
     ] + [pltpu.VMEM((depth * ref.shape[1], ref.shape[2]), BF16) for ref in (w_qkv, w_out, w_up, w_down)]
     outs = pl.pallas_call(
         functools.partial(forward_kernel, dims),
@@ -1151,6 +849,771 @@
     rest = outs[2 + count :]
     kept = [dict(zip(KEPT, rest[l * len(KEPT) : (l + 1) * len(KEPT)])) for l in range(layers)]
     return acts, vecs, [wholes[4 * l : 4 * l + 4] for l in range(layers)], kept
+
+
+SETS = 4
+KINDS = ("down", "up", "out", "mix")
+
+
+def over_rows(a, b):
+    return lax.dot_general(a, b, (((0,), (0,)), ((), ())), preferred_element_type=F32)
+
+
+class Granule:
+    def __init__(self, at, index, acc, plane_in, z_in, fin, out, send, recv, local, credit, wait_credit, give_credit):
+        self.at, self.index, self.acc, self.plane_in, self.z_in = at, index, acc, plane_in, z_in
+        self.fin, self.out, self.send, self.recv, self.local = fin, out, send, recv, local
+        self.credit, self.wait_credit, self.give_credit = credit, wait_credit, give_credit
+        self.t1 = acc.shape[1] // 4
+        self.names, self.posts = {}, []
+        core, p = at.core, at.p
+        self.direct_p = p + (1 - core) * (2 - 4 * at.py) + core * (1 - 2 * at.px)
+        self.owner_dev = {"ctx": at.c8 + (1 - core) * (2 - 4 * at.px) + core * (4 - 8 * at.py)}
+
+    def make(self, name, src, dst, device):
+        i = self.names.setdefault(name, len(self.names))
+        return remote(src, dst, self.send.at[i], self.recv.at[i], device)
+
+    def post(self, name, src, dst, device, cond=None):
+        under(cond, lambda: self.make(name, src, dst, device).start())
+        self.posts.append((name, src, dst, device, cond))
+
+    def take(self, name, dst):
+        self.make(name, dst, dst, self.at.sib).wait_recv()
+
+    def chunk(self, p):
+        return pl.ds(pl.multiple_of(p * self.t1, 16), self.t1)
+
+    def place(self, p, core):
+        return self.out.at[pl.ds(pl.multiple_of(core * 4 * self.t1 + p * self.t1, 16), self.t1)]
+
+    def begin(self):
+        at = self.at
+        if self.wait_credit is not None:
+            below = jnp.where(at.z > 0, 1, 0)
+            above = jnp.where(at.z < at.depth - 1, 1, 0)
+            pl.semaphore_wait(self.wait_credit, 2 + below + above)
+        self.post("diag", self.acc.at[:, self.chunk(at.p_d)], self.plane_in.at[0], at.relay_dev)
+        self.post("near", self.acc.at[:, self.chunk(self.direct_p)], self.plane_in.at[1], at.relay_dev)
+
+    def relay(self):
+        at = self.at
+        self.take("diag", self.plane_in.at[0])
+        mine = self.chunk(at.relay_from)
+        for t in range(at.depth):
+            add_rows(self.acc.at[t, mine], self.plane_in.at[0, t], self.t1)
+        self.post("relay", self.acc.at[:, mine], self.plane_in.at[2], self.owner_dev)
+
+    def combine(self):
+        at = self.at
+        self.take("near", self.plane_in.at[1])
+        self.take("relay", self.plane_in.at[2])
+        mine = self.chunk(at.p)
+        for t in range(at.depth):
+            add_rows_two(self.acc.at[t, mine], self.plane_in.at[1, t], self.plane_in.at[2, t], self.t1)
+
+    def line(self, step):
+        at = self.at
+        last = at.depth - 1
+        right, left = last - step, step
+        mine = self.chunk(at.p)
+        acc = lambda t: self.acc.at[t, mine]
+
+        def go(t, here):
+            @pl.when(here)
+            def _():
+                self.take(f"z{t}", self.z_in.at[t])
+                add_rows(acc(t), self.z_in.at[t], self.t1)
+
+        is_right, is_left = at.z < right, at.z > left
+        under(is_right, lambda: go(right, at.z > 0))
+        self.post(f"z{right}", acc(right), self.z_in.at[right], at.up(), is_right)
+        under(is_left, lambda: go(left, at.z < last))
+        self.post(f"z{left}", acc(left), self.z_in.at[left], at.down(), at.z > left + 1)
+        self.post(f"e{left}", acc(left), self.z_in.at[at.depth], at.down(), at.z == left + 1)
+
+    def end(self):
+        at = self.at
+        last = at.depth - 1
+        mine = self.chunk(at.p)
+        for t in range(at.depth):
+            def below():
+                self.take(f"z{t}", self.z_in.at[t])
+                add_rows(self.acc.at[t, mine], self.z_in.at[t], self.t1)
+
+            def above():
+                self.take(f"e{t}", self.z_in.at[at.depth])
+                add_rows(self.acc.at[t, mine], self.z_in.at[at.depth], self.t1)
+
+            if t > 0:
+                under(at.z == t, below)
+            if t < last:
+                under(at.z == t, above)
+        if self.give_credit:
+            for device in (at.x_dev, at.y_dev):
+                pl.semaphore_signal(self.credit, inc=1, device_id=device, device_id_type=MESH)
+            under(
+                at.z > 0,
+                lambda: pl.semaphore_signal(self.credit, inc=1, device_id=at.down(), device_id_type=MESH),
+            )
+            under(
+                at.z < last,
+                lambda: pl.semaphore_signal(self.credit, inc=1, device_id=at.up(), device_id_type=MESH),
+            )
+        self.fin[...] = self.acc[at.z, mine]
+        here = self.place(at.p, at.core)
+        pltpu.make_async_copy(self.fin, here, self.local).start()
+        self.post("sx", self.fin, here, at.x_dev)
+        self.post("sy", self.fin, here, at.y_dev)
+        self.post("ss", self.fin, here, at.sib)
+
+    def release(self):
+        keep = []
+        for name, src, dst, device, cond in self.posts:
+            if name[0] == "s":
+                keep.append((name, src, dst, device, cond))
+            else:
+                under(cond, lambda: self.make(name, src, dst, device).wait_send())
+        self.posts = keep
+
+    def spread_relay(self):
+        at = self.at
+        for far, p in (("sx", at.p_x), ("sy", at.p_y)):
+            here = self.place(p, at.core)
+            self.take(far, here)
+            self.post(far + "s", here, here, at.sib)
+        here = self.place(at.relay_from, at.core)
+        self.post("sd", here, here, at.relay_dev)
+
+    def spread_last(self):
+        at = self.at
+        here = self.place(at.p_d, at.core)
+        self.take("sd", here)
+        self.post("sds", here, here, at.sib)
+
+    def finish(self):
+        at = self.at
+        for name, p in (("ss", at.p), ("sxs", at.p_x), ("sys", at.p_y), ("sds", at.p_d)):
+            self.take(name, self.place(p, 1 - at.core))
+        pltpu.make_async_copy(self.fin, self.place(at.p, at.core), self.local).wait()
+
+    def drain(self):
+        for name, src, dst, device, cond in self.posts:
+            under(cond, lambda: self.make(name, src, dst, device).wait_send())
+
+    def stages(self):
+        steps = range(self.at.depth - 1)
+        out = [[self.relay], [self.combine, functools.partial(self.line, 0)]]
+        out += [[functools.partial(self.line, i)] for i in steps[1:]]
+        out += [[self.end], [self.release, self.spread_relay], [self.spread_last], [self.finish]]
+        return out
+
+
+class KeyGrads:
+    def __init__(self, at, parts, sib_in, stage, plane_in, send, recv, local, credit, layer):
+        self.at, self.parts, self.sib_in, self.stage, self.plane_in = at, parts, sib_in, stage, plane_in
+        self.send, self.recv, self.local, self.credit, self.layer = send, recv, local, credit, layer
+        self.names, self.posts = {}, []
+        core, p = at.core, at.p
+        self.direct_p = p + (1 - core) * (2 - 4 * at.py) + core * (1 - 2 * at.px)
+        self.owner_dev = {"ctx": at.c8 + (1 - core) * (2 - 4 * at.px) + core * (4 - 8 * at.py)}
+        self.order = [at.p_d, self.direct_p, at.relay_from, at.p]
+
+    def make(self, name, src, dst, device):
+        i = self.names.setdefault(name, len(self.names))
+        return remote(src, dst, self.send.at[i], self.recv.at[i], device)
+
+    def post(self, name, src, dst, device):
+        self.make(name, src, dst, device).start()
+        self.posts.append((name, src, dst, device))
+
+    def take(self, name, dst):
+        self.make(name, dst, dst, self.at.sib).wait_recv()
+
+    def start(self):
+        for i, p in enumerate(self.other_order()):
+            self.post(f"s{i}", self.parts.at[1, p], self.sib_in.at[p], self.at.sib)
+
+    def other_order(self):
+        at = self.at
+        core = 1 - at.core
+        direct = at.p + (1 - core) * (2 - 4 * at.py) + core * (1 - 2 * at.px)
+        relay = at.p + (1 - core) * (1 - 2 * at.px) + core * (2 - 4 * at.py)
+        return [at.p_d, direct, relay, at.p]
+
+    def add(self, p, extra):
+        seqs, rows = self.parts.shape[2], self.parts.shape[3]
+        for s in range(seqs):
+            add_rows(self.parts.at[0, p, s], extra.at[s], rows)
+
+    def core_sum(self, i):
+        p = self.order[i]
+        self.take(f"s{i}", self.sib_in.at[p])
+        copy = pltpu.make_async_copy(self.sib_in.at[p], self.stage, self.local)
+        copy.start()
+        copy.wait()
+        self.add(p, self.stage)
+
+    def first(self):
+        at = self.at
+        self.core_sum(0)
+        if self.layer is not None:
+            pl.semaphore_wait(self.credit, 2)
+        self.post("diag", self.parts.at[0, at.p_d], self.plane_in.at[0], at.relay_dev)
+        self.core_sum(1)
+        self.post("near", self.parts.at[0, self.direct_p], self.plane_in.at[1], at.relay_dev)
+        self.core_sum(2)
+        self.core_sum(3)
+
+    def relay(self):
+        at = self.at
+        self.take("diag", self.plane_in.at[0])
+        self.add(at.relay_from, self.plane_in.at[0])
+        self.post("relay", self.parts.at[0, at.relay_from], self.plane_in.at[2], self.owner_dev)
+
+    def combine(self, give_credit):
+        at = self.at
+        seqs, rows = self.parts.shape[2], self.parts.shape[3]
+        self.take("near", self.plane_in.at[1])
+        self.take("relay", self.plane_in.at[2])
+        for s in range(seqs):
+            add_rows_two(self.parts.at[0, at.p, s], self.plane_in.at[1, s], self.plane_in.at[2, s], rows)
+        if give_credit:
+            for device in (at.x_dev, at.y_dev):
+                pl.semaphore_signal(self.credit, inc=1, device_id=device, device_id_type=MESH)
+
+    def drain(self):
+        for name, src, dst, device in self.posts:
+            self.make(name, src, dst, device).wait_send()
+        self.posts = []
+
+
+def backward_kernel(dims, *refs):
+    layers, seqs, rows, slots, width, ff, depth, per_layer = dims
+    flat, wide = seqs * rows, pad_lanes(width)
+    pairs = wide // LANES
+    total = seqs * pairs
+    refs = list(refs)
+
+    def grab(n):
+        out = refs[:n]
+        del refs[:n]
+        return out
+
+    cot, lengths, vecs = grab(3)
+    kept = [dict(zip(KEPT, grab(len(KEPT)))) for _ in range(layers)]
+    wholes = [grab(4) for _ in range(layers)]
+    grad_in, small_out = grab(2)
+    outs = grab(layers * per_layer)
+    kv_sib = grab(layers)
+    (g_send, g_recv, g_local, g_credit, kv_send, kv_recv, kv_local, kv_credit) = grab(8)
+    (pg_send, pg_recv, pg_local, pg_credit, sm_send, sm_recv, load_sem, w_sem, kvp_sem) = grab(9)
+    acc, plane_in, z_in, rest_acc, fin = grab(5)
+    g, hx, dn = grab(3)
+    gm, gu, ga, gq, gk, gv = grab(6)
+    pz, pc, po, pa = grab(4)
+    dg, q, go, o, lse, bias, kvp = grab(7)
+    parts, kv_stage, kv_plane = grab(3)
+    wt_a, wt_u, wt_q, gm3 = grab(4)
+    sm, sm_sum, sm_in, sm_z, up_row = grab(5)
+
+    at = Place()
+    core = at.core
+    barrier = pltpu.get_barrier_semaphore()
+    others = [{"fsdp": lax.rem(at.z + i, depth)} for i in range(1, depth)]
+    for device in [at.sib, at.x_dev, at.y_dev] + others:
+        pl.semaphore_signal(barrier, inc=1, device_id=device, device_id_type=MESH)
+    pl.semaphore_wait(barrier, 3 + depth - 1)
+
+    exchange = {
+        "down": [("pz", pz), ("gm", gm)],
+        "up": [("pc", pc), ("gu", gu)],
+        "out": [("po", po), ("ga", ga)],
+        "mix": [("pa", pa), ("gq", gq), ("gk", gk), ("gv", gv)],
+    }
+    slot_of = {}
+    for kind in KINDS:
+        for name, _ in exchange[kind]:
+            slot_of[name] = len(slot_of)
+    buffers = {name: buf for kind in KINDS for name, buf in exchange[kind]}
+    posted = {}
+
+    def pg_copy(name, src):
+        i = slot_of[name]
+        buf = buffers[name]
+        dst = buf.at[1]
+        return remote(src, dst, pg_send.at[i], pg_recv.at[i], at.sib)
+
+    def pg_post(name, src):
+        pg_copy(name, src).start()
+        posted[name] = src
+
+    def pg_sent(name):
+        src = posted.pop(name, None)
+        if src is not None:
+            pg_copy(name, src).wait_send()
+
+    def pg_take(name):
+        buf = buffers[name].at[1]
+        pg_copy(name, buf).wait_recv()
+
+    def piece_load(l, name):
+        return pltpu.make_async_copy(kept[l][name].at[core], buffers[name].at[0], pg_local.at[slot_of[name]])
+
+    def free_kind(kind, l):
+        if l < layers - 1:
+            pl.semaphore_wait(pg_credit.at[KINDS.index(kind)], 1)
+
+    def done_kind(kind, l):
+        if l > 0:
+            pl.semaphore_signal(
+                pg_credit.at[KINDS.index(kind)], inc=1, device_id=at.sib, device_id_type=MESH
+            )
+
+    active, items = [], []
+    line_up = layers * per_layer
+
+    def pump(times=1):
+        for _ in range(times):
+            for entry in list(active):
+                for do in entry[1].pop(0):
+                    do()
+                if not entry[1]:
+                    active.remove(entry)
+
+    def open_set():
+        index = len(items)
+        if index >= SETS:
+            old = items[index - SETS]
+            while any(entry[0] is old and len(entry[1]) > 2 for entry in active):
+                pump()
+        return index
+
+    def launch(source):
+        index = len(items)
+        s = index % SETS
+        item = Granule(
+            at, index, source, plane_in.at[s], z_in.at[s], fin.at[index], outs[index],
+            g_send.at[index], g_recv.at[index], g_local.at[index], g_credit.at[index],
+            g_credit.at[index - SETS] if index >= SETS else None, index + SETS < line_up,
+        )
+        item.begin()
+        items.append(item)
+        active.append([item, item.stages()])
+
+    def weight_grad(l, unit, piece, rhs, first):
+        index = open_set()
+        s = index % SETS
+        home = 0 if unit < 8 else 1
+
+        def do(off, size):
+            cols = pl.ds(off, size)
+            right = rhs[:, :, pl.ds(pl.multiple_of(first + off, LANES), size)].reshape(2 * flat, size)
+            left = piece[:, :, pl.ds(0, depth * LANES)].reshape(2 * flat, depth * LANES)
+            out = over_rows(left, right).astype(BF16)
+            for t in range(depth):
+                acc[s, t, :, cols] = out[t * LANES : (t + 1) * LANES]
+
+            @pl.when(core == home)
+            def _():
+                last = piece[:, :, pl.ds(depth * LANES, LANES)].reshape(2 * flat, LANES)
+                more = over_rows(last, right).astype(BF16)
+                for t in range(depth):
+                    rest_acc[t, pl.ds(16 * (unit - 8 * home), 16), cols] = more[t * 16 : (t + 1) * 16]
+
+        by_tiles(wide, 384, do)
+        launch(acc.at[s])
+
+    def rest_grad():
+        open_set()
+        launch(rest_acc)
+
+    def put_row(l, i, value):
+        sm[pl.ds(l * 16 + i, 1), pl.ds(0, width)] = value
+
+    def column_sums(l, i, src):
+        put_row(l, i, jnp.sum(src[0, :, pl.ds(0, width)].astype(F32), axis=0, keepdims=True))
+
+    def norm_back(l, i):
+        gain = vecs[l, pl.ds(i, 1), pl.ds(0, width)]
+
+        def do(step, carry):
+            gain_sum, shift_sum = carry
+            here = pl.ds(pl.multiple_of(step * 32, 32), 32)
+            unit, scale = row_norm(hx[here, :])
+            grad = dn[here, :]
+            inner = grad * gain
+            mean_inner = jnp.mean(inner, axis=-1, keepdims=True)
+            mean_unit = jnp.mean(inner * unit, axis=-1, keepdims=True)
+            g[here, :] = g[here, :] + scale * (inner - mean_inner - unit * mean_unit)
+            return (
+                gain_sum + jnp.sum(grad * unit, axis=0, keepdims=True),
+                shift_sum + jnp.sum(grad, axis=0, keepdims=True),
+            )
+
+        zero = jnp.zeros((1, width), F32)
+        gain_sum, shift_sum = lax.fori_loop(0, flat // 32, do, (zero, zero))
+        put_row(l, i, gain_sum)
+        put_row(l, 2 + i, shift_sum)
+
+    def load(l, name, dst, index):
+        return pltpu.make_async_copy(kept[l][name], dst, load_sem.at[index])
+
+    def low_copy(src, dst):
+        def do(first, size):
+            here = pl.ds(first, size)
+            dst[0, here, pl.ds(0, width)] = src[here, :].astype(BF16)
+
+        by_tiles(flat, 64, do)
+
+    def row_tile(whole, buf, slot, first, size, sem):
+        return pltpu.make_async_copy(
+            whole.at[pl.ds(first, size)], buf.at[slot, pl.ds(0, size)], sem.at[slot]
+        )
+
+    def ff_back(l):
+        w_up, w_down = wholes[l][2], wholes[l][3]
+        tile = 256
+        count = ff // tile
+
+        def copies(i, slot):
+            first = pl.multiple_of(i * tile, tile)
+            return (
+                pltpu.make_async_copy(w_down.at[pl.ds(first, tile)], wt_a.at[slot], w_sem.at[0, slot]),
+                pltpu.make_async_copy(w_up.at[:, pl.ds(first, tile)], wt_u.at[slot], w_sem.at[1, slot]),
+            )
+
+        dn[...] = jnp.zeros_like(dn)
+        for copy in copies(0, 0):
+            copy.start()
+
+        def step(i, carry):
+            slot = lax.rem(i, 2)
+            for copy in copies(i, slot):
+                copy.wait()
+
+            @pl.when(i + 1 < count)
+            def _():
+                for copy in copies(i + 1, 1 - slot):
+                    copy.start()
+
+            cols = pl.ds(pl.multiple_of(i * tile, tile), tile)
+            grad = across(gm[0, :, pl.ds(0, width)], wt_a[slot])
+            low = (grad * dg[:, cols].astype(F32)).astype(BF16)
+            gu[0, :, cols] = low
+            up_row[pl.ds(0, 1), cols] = jnp.sum(low.astype(F32), axis=0, keepdims=True)
+            dn[...] = dn[...] + across(low, wt_u[slot])
+            return carry
+
+        def part(first, size):
+            lax.fori_loop(first, first + size, step, 0)
+
+        half = count // 2
+        part(0, half)
+        pump()
+        part(half, count - half)
+
+    def tiles_back(whole, buf, sem, left, put):
+        tile = buf.shape[1]
+        spans = [(i, min(tile, width - i)) for i in range(0, width, tile)]
+        row_tile(whole, buf, 0, *spans[0], sem).start()
+        for n, (first, size) in enumerate(spans):
+            row_tile(whole, buf, n % 2, first, size, sem).wait()
+            if n + 1 < len(spans):
+                row_tile(whole, buf, (n + 1) % 2, *spans[n + 1], sem).start()
+            put(first, size, across(left(), buf[n % 2, pl.ds(0, size)]))
+
+    def kv_copy(l, it, slot):
+        s, j = it // pairs, lax.rem(it, pairs)
+        return [
+            pltpu.make_async_copy(
+                kept[l]["kv"].at[s, :, pl.ds(pl.multiple_of(i * wide + j * LANES, LANES), LANES)],
+                kvp.at[slot, i],
+                kvp_sem.at[slot, i],
+            )
+            for i in range(2)
+        ]
+
+    def attend_back(l, first, count):
+        def step(it, carry):
+            slot = lax.rem(it, 2)
+            for copy in kv_copy(l, it, slot):
+                copy.wait()
+
+            @pl.when(it + 1 < total)
+            def _():
+                for copy in kv_copy(l, it + 1, 1 - slot):
+                    copy.start()
+
+            s, j = it // pairs, lax.rem(it, pairs)
+            here = pl.ds(pl.multiple_of(s * rows, rows), rows)
+            col = pl.ds(pl.multiple_of(j * LANES, LANES), LANES)
+            col_v = pl.ds(pl.multiple_of(wide + j * LANES, LANES), LANES)
+            q2, go_block = two_heads(q[here, col]), go[here, col]
+            go2 = two_heads(go_block)
+            keys, values = kvp[slot, 0], kvp[slot, 1]
+            product = go_block.astype(F32) * o[here, col].astype(F32)
+            delta = jnp.sum(two_heads(product), axis=-1, keepdims=True)
+            lane = lax.broadcasted_iota(jnp.int32, (2 * rows, LANES), 1)
+            block = lse[pl.ds(pl.multiple_of(s * 2 * rows, rows), 2 * rows), :]
+            log_total = jnp.sum(jnp.where(lane == it, block, 0.0), axis=-1, keepdims=True)
+            seen = bias[s]
+            scores = across(q2, keys) * (HEAD_DIM ** (-0.5)) + jnp.concatenate([seen, seen], axis=0)
+            probs = jnp.exp(scores - log_total)
+            grads = across(go2, values)
+            low = (probs * (grads - delta)).astype(BF16)
+            dq = jnp.dot(low, keys, preferred_element_type=F32) * (HEAD_DIM ** (-0.5))
+            gq[0, here, col] = one_pair(dq, rows).astype(BF16)
+            dk = (over_rows(low, q2) * (HEAD_DIM ** (-0.5))).astype(BF16)
+            dv = over_rows(probs.astype(BF16), go2).astype(BF16)
+            for b in range(slots // rows):
+                mine = lax.rem(b + core, 2)
+                span = slice(b * rows, (b + 1) * rows)
+                parts[mine, b // 2, s, :, col] = dk[span]
+                parts[mine, b // 2, s, :, col_v] = dv[span]
+            return carry
+
+        lax.fori_loop(first, first + count, step, 0)
+
+    loads = {}
+
+    def early(l):
+        for i, (name, dst) in enumerate((("h1", hx), ("dg", dg), ("q", q), ("o", o), ("lse", lse))):
+            loads[name] = load(l, name, dst, i)
+            loads[name].start()
+        for kind in KINDS:
+            free_kind(kind, l)
+            name = exchange[kind][0][0]
+            piece_load(l, name).start()
+            pg_sent(name)
+            pg_post(name, kept[l][name].at[1 - core])
+
+    rest_acc[...] = jnp.zeros_like(rest_acc)
+    sm[...] = jnp.zeros_like(sm)
+    for buf in (gm, gu, ga, gq, gk, gv):
+        buf[0] = jnp.zeros(buf.shape[1:], BF16)
+    go[...] = jnp.zeros_like(go)
+    early(layers - 1)
+    for s in range(seqs):
+
+        def first_grad(first, size):
+            here = pl.ds(s * rows + first, size)
+            place = at.c8 * rows + first + lax.broadcasted_iota(jnp.int32, (size, width), 0)
+            g[here, :] = jnp.where(place < lengths[s], cot[here, :].astype(F32), 0.0)
+
+        by_tiles(rows, 32, first_grad)
+    key_bias(bias, seqs, rows, slots, lengths, at.c8)
+
+    for l in reversed(range(layers)):
+        keys = KeyGrads(
+            at, parts, kv_sib[l], kv_stage, kv_plane, kv_send.at[l], kv_recv.at[l], kv_local,
+            kv_credit, None if l == layers - 1 else l,
+        )
+        if l < layers - 1:
+            early(l)
+        pg_sent("gm")
+        low_copy(g, gm)
+        pg_post("gm", gm.at[0])
+        column_sums(l, 7, gm)
+        piece_load(l, "pz").wait()
+        pg_take("pz")
+        pg_take("gm")
+        for i in range(4):
+            weight_grad(l, i, pz.at[:, i], gm, 0)
+            pump()
+        done_kind("down", l)
+        loads["dg"].wait()
+        pg_sent("gu")
+        ff_back(l)
+        pg_post("gu", gu.at[0])
+        pump()
+        for r in range(4):
+            sm[pl.ds(l * 16 + 8 + r, 1), :] = up_row[pl.ds(0, 1), pl.ds(r * wide, wide)]
+        loads["h1"].wait()
+        norm_back(l, 1)
+        loads["h"] = load(l, "h", hx, 5)
+        loads["h"].start()
+        pg_sent("ga")
+        low_copy(g, ga)
+        pg_post("ga", ga.at[0])
+        column_sums(l, 6, ga)
+        pump()
+
+        def put_go(first, size, value):
+            go[:, pl.ds(first, size)] = value.astype(BF16)
+
+        tiles_back(wholes[l][1], wt_a, w_sem.at[0], lambda: ga[0, :, pl.ds(0, width)], put_go)
+        for copy in kv_copy(l, 0, 0):
+            copy.start()
+        pump()
+        piece_load(l, "pc").wait()
+        pg_take("pc")
+        pg_take("gu")
+        for i in range(4):
+            weight_grad(l, 4 + i, pc, gu, i * wide)
+            pump()
+        done_kind("up", l)
+        piece_load(l, "po").wait()
+        pg_take("po")
+        pg_take("ga")
+        weight_grad(l, 8, po, ga, 0)
+        done_kind("out", l)
+        pump()
+        for name in ("q", "o", "lse"):
+            loads[name].wait()
+        pg_sent("gq")
+        step = 3
+        for first in range(0, total, step):
+            attend_back(l, first, min(step, total - first))
+            pump()
+        keys.start()
+        pg_post("gq", gq.at[0])
+        column_sums(l, 4, gq)
+        keys.first()
+        pump()
+        keys.relay()
+        pump()
+        keys.combine(l > 0)
+        pg_sent("gk")
+        pg_sent("gv")
+        for s in range(seqs):
+            here = pl.ds(s * rows, rows)
+            gk[0, here, :] = parts[0, at.p, s, :, pl.ds(0, wide)]
+            gv[0, here, :] = parts[0, at.p, s, :, pl.ds(wide, wide)]
+        pg_post("gk", gk.at[0])
+        pg_post("gv", gv.at[0])
+        column_sums(l, 5, gv)
+        for i, src in enumerate((gq, gk, gv)):
+
+            def join(first, size):
+                here = pl.ds(first, size)
+                gm3[here, pl.ds(i * width, width)] = src[0, here, pl.ds(0, width)]
+
+            by_tiles(flat, 64, join)
+
+        def put_dn(first, size, value):
+            dn[:, pl.ds(first, size)] = value
+
+        piece_load(l, "pa").wait()
+        pg_take("pa")
+        pg_take("gq")
+        weight_grad(l, 9, pa, gq, 0)
+        pg_take("gk")
+        weight_grad(l, 10, pa, gk, 0)
+        pg_take("gv")
+        weight_grad(l, 11, pa, gv, 0)
+        done_kind("mix", l)
+        rest_grad()
+        rest_item = items[-1]
+        pump()
+        tiles_back(wholes[l][0], wt_q, w_sem.at[2], lambda: gm3[...], put_dn)
+        loads["h"].wait()
+        pump()
+        norm_back(l, 0)
+        keys.drain()
+        while l and any(entry[0] is rest_item and len(entry[1]) > 2 for entry in active):
+            pump()
+
+    def do_out(first, size):
+        here = pl.ds(first, size)
+        grad_in[here, :] = g[here, :]
+
+    by_tiles(flat, 64, do_out)
+
+    def sm_copy(i, src, dst, device):
+        return remote(src, dst, sm_send.at[i], sm_recv.at[i], device)
+
+    current = sm
+    for i, device in enumerate((at.sib, at.x_dev, at.y_dev)):
+        copy = sm_copy(i, current, sm_in.at[i], device)
+        copy.start()
+        pump()
+        copy.wait()
+        sm_sum[i] = current[...] + sm_in[i]
+        current = sm_sum.at[i]
+    hops = []
+    for i, device in enumerate(others):
+        copy = sm_copy(3 + i, current, sm_z.at[i], device)
+        copy.start()
+        hops.append(copy)
+    pump()
+    for copy in hops:
+        copy.wait()
+    small_total = jnp.zeros(sm.shape, F32)
+    for z in range(depth):
+        slot = lax.rem(at.z - z - 1 + 2 * depth, depth)
+        other = sm_z[jnp.minimum(slot, depth - 2)]
+        small_total = small_total + jnp.where(slot == depth - 1, current[...], other)
+    small_out[...] = small_total
+    while active:
+        pump()
+    for item in items:
+        item.drain()
+    for name in list(posted):
+        pg_sent(name)
+
+
+def backward(cotangent, lengths, vecs, kept, wholes, layers, ff):
+    seqs, rows, width = cotangent.shape
+    depth = lax.axis_size("fsdp")
+    slots = rows * lax.axis_size("ctx")
+    flat, wide = seqs * rows, pad_lanes(width)
+    per_layer = 13
+    count = layers * per_layer
+    dims = (layers, seqs, rows, slots, width, ff, depth, per_layer)
+    any_spec = pl.BlockSpec(memory_space=pl.ANY)
+    vmem = pl.BlockSpec(memory_space=pltpu.VMEM)
+    struct = lambda shape, kind: jax.ShapeDtypeStruct(shape, kind)
+    out_shape = [struct((flat, width), F32), struct((layers * 16, wide), F32)]
+    out_shape += [struct((2 * LANES, wide), BF16) for _ in range(count)]
+    out_shape += [struct((4, seqs, rows, 2 * wide), BF16) for _ in range(layers)]
+    dma, regular = pltpu.SemaphoreType.DMA, pltpu.SemaphoreType.REGULAR
+    low = lambda *shape: pltpu.VMEM(shape, BF16)
+    full = lambda *shape: pltpu.VMEM(shape, F32)
+    chunk = LANES // 4
+    scratch = [
+        dma((count, 24)), dma((count, 24)), dma((count,)), regular((count,)),
+        dma((layers, 8)), dma((layers, 8)), dma, regular,
+        dma((10,)), dma((10,)), dma((10,)), regular((4,)), dma((8,)), dma((8,)), dma((8,)), dma((3, 2)), dma((2, 2)),
+        low(SETS, depth, LANES, wide), low(SETS, 3, depth, chunk, wide), low(SETS, depth + 1, chunk, wide),
+        low(depth, LANES, wide), low(count, chunk, wide),
+        full(flat, width), full(flat, width), full(flat, width),
+        low(2, flat, wide), low(2, flat, 4 * wide), low(2, flat, wide),
+        low(2, flat, wide), low(2, flat, wide), low(2, flat, wide),
+        low(2, 4, flat, PIECE), low(2, flat, PIECE), low(2, flat, PIECE), low(2, flat, PIECE),
+        low(flat, ff), low(flat, wide), low(flat, wide), low(flat, wide), full(2 * flat, LANES),
+        full(seqs, rows, slots), low(2, 2, slots, LANES),
+        low(2, 4, seqs, rows, 2 * wide), low(seqs, rows, 2 * wide), low(3, seqs, rows, 2 * wide),
+        low(2, 256, width), low(2, width, 256), low(2, 256, 3 * width), low(flat, 3 * width),
+        full(layers * 16, wide), full(3, layers * 16, wide), full(3, layers * 16, wide),
+        full(depth - 1, layers * 16, wide), full(8, 4 * wide),
+    ]
+    flat_kept = [kept[l][name] for l in range(layers) for name in KEPT]
+    flat_wholes = [item for layer in wholes for item in layer]
+    outs = pl.pallas_call(
+        functools.partial(backward_kernel, dims),
+        out_shape=out_shape,
+        in_specs=[vmem, pl.BlockSpec(memory_space=pltpu.SMEM), vmem]
+        + [any_spec] * (len(flat_kept) + len(flat_wholes)),
+        out_specs=[vmem, vmem] + [any_spec] * (len(out_shape) - 2),
+        scratch_shapes=scratch,
+        compiler_params=pltpu.CompilerParams(
+            collective_id=1, has_side_effects=True, vmem_limit_bytes=63 * 1024 * 1024
+        ),
+    )(cotangent.reshape(flat, width), lengths, vecs, *flat_kept, *flat_wholes)
+    sums = outs[2 : 2 + count]
+    grads = [sums[(layers - 1 - l) * per_layer : (layers - l) * per_layer] for l in range(layers)]
+    return outs[0], outs[1].reshape(layers, 16, wide), grads
+
+
+def assemble(sums, width, ff):
+    rest = sums[12]
+    unit = lambda u: jnp.concatenate([sums[u], rest[16 * u : 16 * u + 16]], axis=0)
+    down = jnp.concatenate([unit(i)[:, :width] for i in range(4)], axis=0)
+    up = jnp.concatenate([unit(4 + i) for i in range(4)], axis=1)[:, :ff]
+    out = unit(8)[:, :width]
+    mix = jnp.concatenate([unit(9 + i)[:, :width] for i in range(3)], axis=1)
+    return [item.astype(F32) for item in (down, up, out, mix)]
 
 
 def normalize(values, scales, shifts):
@@ -1276,11 +1739,7 @@
     return [wholes[4 * i : 4 * i + 4] for i in range(layers)], [small_all[:, i] for i in range(layers)]
 
 
-def reduce_layer(grads, collective_id):
-    depth = lax.axis_size("fsdp")
-    if fast_mesh(grads[0].shape[0] // depth):
-        parts = [item.reshape(depth, item.shape[0] // depth, item.shape[1]) for item in grads]
-        return reduce_grads(parts, [0] * len(parts), collective_id, lag=1)
+def reduce_layer(grads):
     shards_now = [
         lax.psum_scatter(item, "fsdp", scatter_dimension=0, tiled=True) for item in grads
     ]
@@ -1317,107 +1776,96 @@
     small = pack_small(ln_gain, ln_bias, b_qv, b_out, b_up, b_down)
     if fast_mesh(w_qkv.shape[1]):
         part = small.shape[2]
+        ff = w_up.shape[2]
         padded = jnp.pad(small, ((0, 0), (0, 4), (0, pad_lanes(part) - part)))
         activations, vectors, weights, kept = forward(
             tokens, lengths, w_qkv, w_out, w_up, w_down, padded.reshape(layer_total * 16, -1)
         )
-        activations = activations.reshape(tokens.shape)
-        kept_layers = []
-        for layer_index in range(layer_total):
-            one = kept[layer_index]
-            wide = one["q"].shape[1]
-            cut = lambda array: array[..., :model_width]
-            heads = cut(one["q"]).reshape(split_shape)
-            kv_shape = (seq_count, -1, head_count, head_width)
-            attended = cut(one["o"])
-            lse = one["lse"].reshape(seq_count, 2, row_count, -1)
-            pairs = wide // LANES
-            log_total = jnp.stack(
-                [
-                    jnp.stack([lse[s, n % 2, :, s * pairs + n // 2] for n in range(head_count)])
-                    for s in range(seq_count)
-                ]
+        grad_in, small_sums, sums = backward(
+            cotangent, lengths, vectors, kept, weights, layer_total, ff
+        )
+        mine = lambda rows: lax.dynamic_slice_in_dim(
+            rows[..., :model_width], lax.axis_index("fsdp") * part, part, axis=rows.ndim - 1
+        )
+        up_bias = small_sums[:, 8:12].reshape(layer_total, -1)[:, :ff]
+        up_part = ff // depth
+        shard_grads = [assemble(item, model_width, ff) for item in sums]
+        whole = lambda member: jnp.stack([item[member] for item in shard_grads])
+        return (
+            activations.reshape(tokens.shape),
+            grad_in.reshape(tokens.shape),
+            mine(small_sums[:, 0:2]),
+            mine(small_sums[:, 2:4]),
+            whole(3),
+            mine(small_sums[:, 4:6]),
+            whole(2),
+            mine(small_sums[:, 6]),
+            whole(1),
+            lax.dynamic_slice_in_dim(up_bias, lax.axis_index("fsdp") * up_part, up_part, axis=1),
+            whole(0),
+            mine(small_sums[:, 7]),
+        )
+    weights, smalls = gather_all(
+        [(w_qkv[i], w_out[i], w_up[i], w_down[i]) for i in range(layer_total)], small
+    )
+    kept_layers = []
+    for layer_index in range(layer_total):
+        mix_weight, out_weight, up_weight, down_weight = weights[layer_index]
+        gain_rows, shift_rows, mix_bias, out_bias, down_bias, up_bias = unpack_small(
+            smalls[layer_index].astype(jnp.float32)
+        )
+        normed_first = normalize(hidden, gain_rows[0], shift_rows[0]).astype(jnp.bfloat16)
+        mixed_rows = jnp.dot(normed_first, mix_weight, preferred_element_type=jnp.float32)
+        queries = (
+            (mixed_rows[:, :model_width] + mix_bias[0]).astype(jnp.bfloat16).reshape(split_shape)
+        )
+        key_rows = (
+            mixed_rows[:, model_width : 2 * model_width].astype(jnp.bfloat16).reshape(split_shape)
+        )
+        value_rows = (
+            (mixed_rows[:, 2 * model_width :] + mix_bias[1])
+            .astype(jnp.bfloat16)
+            .reshape(split_shape)
+        )
+        key_part = lax.all_gather(key_rows, "ctx", axis=1, tiled=True)
+        value_part = lax.all_gather(value_rows, "ctx", axis=1, tiled=True)
+        output, log_total = attend_forward(
+            queries, key_part, value_part, positions, lengths, score_scale
+        )
+        output = output.reshape(flat_rows, model_width)
+        attended = output.astype(jnp.bfloat16)
+        middle = (
+            hidden + jnp.dot(attended, out_weight, preferred_element_type=jnp.float32) + out_bias
+        )
+        normed_second = normalize(middle, gain_rows[1], shift_rows[1]).astype(jnp.bfloat16)
+        upper_pre = (
+            jnp.dot(normed_second, up_weight, preferred_element_type=jnp.float32) + up_bias
+        )
+        active = jax.nn.gelu(upper_pre).astype(jnp.bfloat16)
+        kept_layers.append(
+            (
+                hidden,
+                normed_first,
+                queries,
+                key_part,
+                value_part,
+                output,
+                log_total,
+                attended,
+                middle,
+                normed_second,
+                upper_pre,
+                active,
+                gain_rows,
+                shift_rows,
             )
-            kept_layers.append(
-                (
-                    one["h"],
-                    one["a"],
-                    heads,
-                    cut(one["kv"]).reshape(kv_shape),
-                    cut(one["kv"][..., wide:]).reshape(kv_shape),
-                    attended.astype(jnp.float32),
-                    log_total,
-                    attended,
-                    one["h1"],
-                    one["c"],
-                    one["u"],
-                    jax.nn.gelu(one["u"]).astype(jnp.bfloat16),
-                    cut(vectors[layer_index, 0:2]),
-                    cut(vectors[layer_index, 2:4]),
-                )
-            )
-    else:
-        weights, smalls = gather_all(
-            [(w_qkv[i], w_out[i], w_up[i], w_down[i]) for i in range(layer_total)], small
-        )
-        kept_layers = []
-        for layer_index in range(layer_total):
-            mix_weight, out_weight, up_weight, down_weight = weights[layer_index]
-            gain_rows, shift_rows, mix_bias, out_bias, down_bias, up_bias = unpack_small(
-                smalls[layer_index].astype(jnp.float32)
-            )
-            normed_first = normalize(hidden, gain_rows[0], shift_rows[0]).astype(jnp.bfloat16)
-            mixed_rows = jnp.dot(normed_first, mix_weight, preferred_element_type=jnp.float32)
-            queries = (
-                (mixed_rows[:, :model_width] + mix_bias[0]).astype(jnp.bfloat16).reshape(split_shape)
-            )
-            key_rows = (
-                mixed_rows[:, model_width : 2 * model_width].astype(jnp.bfloat16).reshape(split_shape)
-            )
-            value_rows = (
-                (mixed_rows[:, 2 * model_width :] + mix_bias[1])
-                .astype(jnp.bfloat16)
-                .reshape(split_shape)
-            )
-            key_part = lax.all_gather(key_rows, "ctx", axis=1, tiled=True)
-            value_part = lax.all_gather(value_rows, "ctx", axis=1, tiled=True)
-            output, log_total = attend_forward(
-                queries, key_part, value_part, positions, lengths, score_scale
-            )
-            output = output.reshape(flat_rows, model_width)
-            attended = output.astype(jnp.bfloat16)
-            middle = (
-                hidden + jnp.dot(attended, out_weight, preferred_element_type=jnp.float32) + out_bias
-            )
-            normed_second = normalize(middle, gain_rows[1], shift_rows[1]).astype(jnp.bfloat16)
-            upper_pre = (
-                jnp.dot(normed_second, up_weight, preferred_element_type=jnp.float32) + up_bias
-            )
-            active = jax.nn.gelu(upper_pre).astype(jnp.bfloat16)
-            kept_layers.append(
-                (
-                    hidden,
-                    normed_first,
-                    queries,
-                    key_part,
-                    value_part,
-                    output,
-                    log_total,
-                    attended,
-                    middle,
-                    normed_second,
-                    upper_pre,
-                    active,
-                    gain_rows,
-                    shift_rows,
-                )
-            )
-            hidden = (
-                middle + jnp.dot(active, down_weight, preferred_element_type=jnp.float32) + down_bias
-            )
-        activations = (valid_rows * hidden.reshape(seq_count, row_count, model_width)).astype(
-            jnp.bfloat16
-        )
+        )
+        hidden = (
+            middle + jnp.dot(active, down_weight, preferred_element_type=jnp.float32) + down_bias
+        )
+    activations = (valid_rows * hidden.reshape(seq_count, row_count, model_width)).astype(
+        jnp.bfloat16
+    )
     grad_hidden = (cotangent.astype(jnp.float32) * valid_rows).reshape(flat_rows, model_width)
     big_grads = [None] * layer_total
     small_grads = [None] * layer_total
@@ -1492,8 +1940,7 @@
         grad_input, gain_first, shift_first = first_pull(grad_normed_first)
         grad_hidden = grad_input + grad_middle
         big_grads[layer_index] = reduce_layer(
-            [item.astype(jnp.bfloat16) for item in (up_grad, down_grad, mix_grad, out_grad)],
-            1 + layer_index,
+            [item.astype(jnp.bfloat16) for item in (up_grad, down_grad, mix_grad, out_grad)]
         )
         small_grads[layer_index] = small_rows(
             jnp.stack([gain_first, gain_second]),

time: 1400 us -> 1150 us (0.82)
  Pallas kernels: 759 us -> 1070 us
  local copies, waits for them, and re-layouts: 337 us -> 27.1 us
  matrix products: 181 us -> 0 us
  blocking collectives: 37.2 us -> 0 us
  other arithmetic: 51.2 us -> 33.2 us
  between operations: 15.4 us -> 1.21 us
    pallas_call x2 -> x1, Pallas kernels: 404 us -> 702 us  [backward(): pl.pallas_call(functools.partial(backward_kernel, dims), out_shape=out_sh...]
    unnamed x294 -> x66, local copies, waits for them, and re-layouts: 199 us -> 10.4 us
    dot_general x26 -> x0, matrix products: 181 us -> none  [the longest x8 50.7 us: outer_sum(): lax.dot_general(left_rows, right_rows, (((0,), (0,)), ((), ())), preferre...]
    slice x17 -> x5, local copies, waits for them, and re-layouts: 53.3 us -> 3.87 us  [the longest x1 1.44 us: shards(): small_sums[:, 7]]
    psum x1 -> x0, blocking collectives: 37.2 us -> none  [shards(): total = lax.psum(packed, ('fsdp', 'ctx'))]
    convert_element_type x6 -> x0, local copies, waits for them, and re-layouts: 32.6 us -> none  [the longest x2 28.5 us: shards(): item.astype(jnp.bfloat16)]
    reduce_sum x22 -> x0, other arithmetic: 26.6 us -> none  [the longest x4 7.91 us: normalize(): return centred * lax.rsqrt(variance + 1e-05) * scales + shifts]
    another operation x9 -> x6, other arithmetic: 17.1 us -> 28.3 us  [shards(): whole = lambda member: jnp.stack([item[member] for item in shard_grads])]
  transfers between devices with their start and end apart: 4 -> 0, of which waited for: 0 -> 0; matrix products, arithmetic and copies ran while one was open for 18% -> 0% of each run, Pallas kernels for 15% -> 0%
where the time goes in v3:
time: 1150 us; the launch traced here: 1130 us
  Pallas kernels  1070 us (93%)
  other arithmetic  33.2 us (3%)
  local copies, waits for them, and re-layouts  27.1 us (2%)
    pallas_call x1, Pallas kernels, backward(): pl.pallas_call(functools.partial(backward_kernel, dims), out_shape=out_sh...  702 us
    pallas_call x1, Pallas kernels, forward(): pl.pallas_call(functools.partial(forward_kernel, dims), out_shape=out_sha...  365 us
    another operation x6, other arithmetic, shards(): whole = lambda member: jnp.stack([item[member] for item in shard_grads])  28.3 us

profile of v3, /device:TPU:9, one launch (start us, length us, event | category | flops | bytes accessed | tf_op | source)
XLA Modules:
  0.0 1127.6 jit_solution(6109594066391453981)
XLA Ops:
  0.6 2.1 copy.25
  2.8 0.7 copy.26
  3.4 0.7 copy.27
  4.1 0.8 reshape.243
  4.9 0.8 concatenate.149
  6.3 364.6 %shard_map.220 = (bf16[256,1088]{1,0:T(8,128)(2,1)}, f32[2,8,1152]{2,1,0:T(8,128)}, bf16[1088,3264]{1,0:T(8,128)(2,1)}, bf16[1088,1088]{1,0:T(8,128)(2,1)}, bf16...) custom-call(bf16[256,1088]{1,0:T(8,128)(2,1)} %bitcast.55, ...), custom_call_target="tpu_custom_call" | custom-call | tf_op jit(solution)/shard_map/pallas_call | solution.py:837
  370.9 2.1 copy.31
  373.0 1.1 copy.28
  374.1 701.5 %shard_map.221 = (f32[256,1088]{1,0:T(8,128)}, f32[32,1152]{1,0:T(8,128)}, bf16[256,1152]{1,0:T(8,128)(2,1)}, bf16[256,1152]{1,0:T(8,128)(2,1)}, bf16[256,1152]{...) custom-call(bf16[256,1088]{1,0:T(8,128)(2,1)} %bitcast.56, ...), custom_call_target="tpu_custom_call" | custom-call | tf_op jit(solution)/shard_map/pallas_call | solution.py:1593
  1075.6 2.8 copy.32
  1078.4 1.1 fusion.27
  1082.2 1.2 fusion.20
  1083.4 1.1 fusion.18
  1084.5 2.9 concatenate.163
  1087.4 2.2 fusion.22
  1089.6 3.7 concatenate.156
  1093.3 5.1 maximum_convert_fusion.2
  1098.5 1.6 maximum_convert_fusion.3
  1100.2 1.4 fusion.26
  1102.4 13.0 %fusion.1 = (bf16[1,272,4352]{2,1,0:T(8,128)(2,1)S(1)}, bf16[1,272,4352]{2,1,0:T(8,128)(2,1)S(1)}) fusion(bf16[16,1152]{1,0:T(8,128)(2,1)S(1)} %get-tuple-element.160, bf16[256,1152]{1,0:T(8,128)(2,1)S(1)} %copy-done.3, bf16[16,1152]{1,0:T(8,128)(2,1)S(1)} %get-tuple-element.161, bf16[256,1152]{1,0:T(8,128)(2,1)S(1)} %copy-done.2, ...), kind=kLoop, calls=%fused_computation.5 | loop fusion | flops 37879808 | bytes 9748480 | tf_op jit(solution)/shard_map/stack | solution.py:1793
  1115.4 4.4 maximum_convert_fusion.1
  1119.8 1.0 slice_bitcast_fusion
  1121.8 0.8 copy-done.10
  1123.3 4.2 maximum_convert_fusion
  (73 shorter events, 5.8 us)
Async XLA Ops:
  6.3 366.7 %copy-start.21 = (bf16[2,128,1088]{1,2,0:T(8,128)(2,1)S(1)}, bf16[2,128,1088]{1,2,0:T(8,128)(2,1)}, u32[]{:S(2)}) copy-start(bf16[2,128,1088]{1,2,0:T(8,128)(2,1)} %param.15) | copy-start | bytes 1671172
  1075.6 5.2 copy-start.23
  1075.6 5.9 copy-start.22
  1075.6 6.6 copy-start.20
  1078.4 5.0 copy-start.18
  1078.4 5.0 copy-start.19
  1093.2 5.1 copy-start.16
  1093.3 5.1 copy-start.17
  1093.3 5.1 copy-start.27
  1093.3 5.1 copy-start.28
  1098.4 4.0 copy-start.6
  1098.4 4.0 copy-start.7
  1098.5 3.8 copy-start
  1098.5 3.8 copy-start.1
  1098.5 3.8 copy-start.2
  1098.5 3.8 copy-start.3
  1098.5 3.8 copy-start.4
  1098.5 3.8 copy-start.5
  1115.4 6.1 copy-start.14
  1115.4 6.1 copy-start.15
  1115.4 6.1 copy-start.25
  1115.4 6.1 copy-start.26
  1119.8 1.9 copy-start.12
  1119.8 1.9 copy-start.13
  (5 other events, 6.3 us)

commit v4 on v3

--- a/solution.py
+++ b/solution.py
@@ -61,14 +61,15 @@
 
 
 class Gather:
-    def __init__(self, at, own, whole, left_core, send, recv):
+    def __init__(self, at, own, whole, left_core, send, recv, line=0):
         self.at, self.own, self.whole = at, own, whole
         self.send, self.recv = send, recv
         rows = own.shape[0]
         self.rows = rows
         unit = rows // 17
-        self.t1 = 2 * unit
         self.block = 8 * unit
+        self.t1 = 2 * unit - line
+        self.line = pl.ds(pl.multiple_of(at.core * self.block + 4 * self.t1, 16), 4 * line) if line else None
         self.rest = pl.ds(16 * unit, unit)
         self.has_rest = at.core == left_core
 
@@ -98,6 +99,8 @@
         @pl.when(at.z < at.depth - 1)
         def _():
             self.copy(0, at.z, mine, at.up(), self.own.at[mine]).start()
+            if self.line:
+                self.copy(7, at.z, self.line, at.up(), self.own.at[self.line]).start()
 
             @pl.when(self.has_rest)
             def _():
@@ -106,6 +109,8 @@
         @pl.when(at.z > 0)
         def _():
             self.copy(0, at.z, mine, at.down(), self.own.at[mine], True).start()
+            if self.line:
+                self.copy(7, at.z, self.line, at.down(), self.own.at[self.line], True).start()
 
             @pl.when(self.has_rest)
             def _():
@@ -135,6 +140,12 @@
 
             self.copy(2, shard, mine, at.x_dev).start()
             self.copy(3, shard, mine, at.y_dev).start()
+            if self.line:
+                self.copy(7, shard, self.line, at.sib).wait_recv()
+
+                @pl.when(onward)
+                def _():
+                    self.copy(7, shard, self.line, device).start()
 
             @pl.when(self.has_rest)
             def _():
@@ -188,6 +199,8 @@
         @pl.when(at.z < at.depth - 1)
         def _():
             self.copy(0, at.z, mine, at.up(), self.own.at[mine]).wait_send()
+            if self.line:
+                self.copy(7, at.z, self.line, at.up(), self.own.at[self.line]).wait_send()
 
             @pl.when(self.has_rest)
             def _():
@@ -196,6 +209,8 @@
         @pl.when(at.z > 0)
         def _():
             self.copy(0, at.z, mine, at.down(), self.own.at[mine], True).wait_send()
+            if self.line:
+                self.copy(7, at.z, self.line, at.down(), self.own.at[self.line], True).wait_send()
 
             @pl.when(self.has_rest)
             def _():
@@ -205,6 +220,8 @@
             @pl.when(onward)
             def _():
                 self.copy(0, shard, mine, device).wait_send()
+                if self.line:
+                    self.copy(7, shard, self.line, device).wait_send()
 
                 @pl.when(self.has_rest)
                 def _():
@@ -380,6 +397,7 @@
 
 KEPT = ("h", "pa", "q", "kv", "o", "po", "lse", "h1", "pc", "pz", "dg")
 PIECE = 5 * LANES
+LINE_ROWS = (0, 0, 16, 16)
 
 
 def kept_shapes(seqs, slots, rows, width, ff):
@@ -472,7 +490,7 @@
     at.greet()
 
     owns = [ref.at[l] for l in range(layers) for ref in (w_qkv, w_out, w_up, w_down)]
-    items = [Gather(at, owns[k], wholes[k], k % 2, send.at[k], recv.at[k]) for k in range(4 * layers)]
+    items = [Gather(at, owns[k], wholes[k], k % 2, send.at[k], recv.at[k], LINE_ROWS[k % 4]) for k in range(4 * layers)]
     contexts = [
         Context(at, own_kv, kept[l]["kv"], rows, kv_send.at[l], kv_recv.at[l], keep_sem.at[l, len(KEPT)])
         for l in range(layers)
@@ -851,7 +869,11 @@
     return acts, vecs, [wholes[4 * l : 4 * l + 4] for l in range(layers)], kept
 
 
-SETS = 4
+SETS = 5
+FINS = 10
+LINE_FIRST = ()
+LINE_LAG = 0
+TILES = 3
 KINDS = ("down", "up", "out", "mix")
 
 
@@ -860,11 +882,13 @@
 
 
 class Granule:
-    def __init__(self, at, index, acc, plane_in, z_in, fin, out, send, recv, local, credit, wait_credit, give_credit):
-        self.at, self.index, self.acc, self.plane_in, self.z_in = at, index, acc, plane_in, z_in
+    def __init__(self, at, others, line_first, acc, plane_in, z_in, fin, out, send, recv, local, credit, wait_credit, give_credit, before):
+        self.before = before
+        self.line_first = line_first
+        self.at, self.others, self.acc, self.plane_in, self.z_in = at, others, acc, plane_in, z_in
         self.fin, self.out, self.send, self.recv, self.local = fin, out, send, recv, local
         self.credit, self.wait_credit, self.give_credit = credit, wait_credit, give_credit
-        self.t1 = acc.shape[1] // 4
+        self.t1 = acc.shape[2]
         self.names, self.posts = {}, []
         core, p = at.core, at.p
         self.direct_p = p + (1 - core) * (2 - 4 * at.py) + core * (1 - 2 * at.px)
@@ -874,93 +898,118 @@
         i = self.names.setdefault(name, len(self.names))
         return remote(src, dst, self.send.at[i], self.recv.at[i], device)
 
-    def post(self, name, src, dst, device, cond=None):
-        under(cond, lambda: self.make(name, src, dst, device).start())
-        self.posts.append((name, src, dst, device, cond))
+    def post(self, name, src, dst, device):
+        self.make(name, src, dst, device).start()
+        self.posts.append((name, src, dst, device))
 
     def take(self, name, dst):
         self.make(name, dst, dst, self.at.sib).wait_recv()
 
-    def chunk(self, p):
-        return pl.ds(pl.multiple_of(p * self.t1, 16), self.t1)
-
     def place(self, p, core):
-        return self.out.at[pl.ds(pl.multiple_of(core * 4 * self.t1 + p * self.t1, 16), self.t1)]
+        ref, first, col, cols = self.out
+        row = pl.multiple_of(first + core * 4 * self.t1 + p * self.t1, 16)
+        return ref.at[pl.ds(row, self.t1), pl.ds(col, cols)]
+
+    def line_out(self, part, landing):
+        for i, device in enumerate(self.others):
+            goal = lax.rem(self.at.z + 1 + i, self.at.depth)
+            self.post(f"z{i}", part(goal), landing.at[i], device)
+
+    def line_in(self, landing):
+        for i in range(len(self.others)):
+            self.take(f"z{i}", landing.at[i])
+
+    def plane_out(self, part, landing):
+        self.post("diag", part(self.at.p_d), landing.at[0], self.at.relay_dev)
+        self.post("near", part(self.direct_p), landing.at[1], self.at.relay_dev)
+
+    def plane_relay(self, part, landing, add):
+        self.take("diag", landing.at[0])
+        add(part(self.at.relay_from), landing.at[0])
+        self.post("relay", part(self.at.relay_from), landing.at[2], self.owner_dev)
+
+    def plane_in_all(self, landing):
+        self.take("near", landing.at[1])
+        self.take("relay", landing.at[2])
+
+    def over_shards(self, acc, extra):
+        for t in range(self.at.depth):
+            add_rows(acc.at[t], extra.at[t], self.t1)
+
+    def total(self, own, extra, out):
+        def step(i, carry):
+            piece = pl.ds(pl.multiple_of(i * 16, 16), 16)
+            value = own[piece, :].astype(F32)
+            for j in range(3):
+                value = value + extra(j)[piece, :].astype(F32)
+            out[piece, :] = value.astype(BF16)
+            return carry
+
+        lax.fori_loop(0, self.t1 // 16, step, 0)
+
+    def of_shard(self, p):
+        return self.acc.at[self.at.z, p]
+
+    def of_chip(self, p):
+        return self.acc.at[:, p]
 
     def begin(self):
+        if self.wait_credit is not None:
+            pl.semaphore_wait(self.wait_credit, 2 + len(self.others))
+        if self.line_first:
+            self.line_out(lambda t: self.acc.at[t], self.plane_in)
+        else:
+            self.plane_out(self.of_chip, self.plane_in)
+
+    def second(self):
         at = self.at
-        if self.wait_credit is not None:
-            below = jnp.where(at.z > 0, 1, 0)
-            above = jnp.where(at.z < at.depth - 1, 1, 0)
-            pl.semaphore_wait(self.wait_credit, 2 + below + above)
-        self.post("diag", self.acc.at[:, self.chunk(at.p_d)], self.plane_in.at[0], at.relay_dev)
-        self.post("near", self.acc.at[:, self.chunk(self.direct_p)], self.plane_in.at[1], at.relay_dev)
-
-    def relay(self):
+        if self.line_first:
+            self.line_in(self.plane_in)
+            for p in range(4):
+                own = self.of_shard(p)
+                self.total(own, lambda j: self.plane_in.at[j, p], own)
+            self.plane_out(self.of_shard, self.z_in)
+        else:
+            self.plane_relay(self.of_chip, self.plane_in, self.over_shards)
+
+    def third(self):
         at = self.at
-        self.take("diag", self.plane_in.at[0])
-        mine = self.chunk(at.relay_from)
-        for t in range(at.depth):
-            add_rows(self.acc.at[t, mine], self.plane_in.at[0, t], self.t1)
-        self.post("relay", self.acc.at[:, mine], self.plane_in.at[2], self.owner_dev)
-
-    def combine(self):
-        at = self.at
-        self.take("near", self.plane_in.at[1])
-        self.take("relay", self.plane_in.at[2])
-        mine = self.chunk(at.p)
-        for t in range(at.depth):
-            add_rows_two(self.acc.at[t, mine], self.plane_in.at[1, t], self.plane_in.at[2, t], self.t1)
-
-    def line(self, step):
-        at = self.at
-        last = at.depth - 1
-        right, left = last - step, step
-        mine = self.chunk(at.p)
-        acc = lambda t: self.acc.at[t, mine]
-
-        def go(t, here):
-            @pl.when(here)
-            def _():
-                self.take(f"z{t}", self.z_in.at[t])
-                add_rows(acc(t), self.z_in.at[t], self.t1)
-
-        is_right, is_left = at.z < right, at.z > left
-        under(is_right, lambda: go(right, at.z > 0))
-        self.post(f"z{right}", acc(right), self.z_in.at[right], at.up(), is_right)
-        under(is_left, lambda: go(left, at.z < last))
-        self.post(f"z{left}", acc(left), self.z_in.at[left], at.down(), at.z > left + 1)
-        self.post(f"e{left}", acc(left), self.z_in.at[at.depth], at.down(), at.z == left + 1)
+        if self.line_first:
+            self.plane_relay(self.of_shard, self.z_in, lambda a, b: add_rows(a, b, self.t1))
+        else:
+            self.plane_in_all(self.plane_in)
+            mine = self.of_chip(at.p)
+            for t in range(at.depth):
+                add_rows_two(mine.at[t], self.plane_in.at[1, t], self.plane_in.at[2, t], self.t1)
+            self.line_out(lambda t: self.acc.at[t, at.p], self.z_in)
+
+    def fin_sent(self):
+        for name, src, dst, device in self.posts:
+            if name in ("sx", "sy", "ss"):
+                self.make(name, src, dst, device).wait_send()
+        self.posts = [post for post in self.posts if post[0] not in ("sx", "sy", "ss")]
 
     def end(self):
         at = self.at
-        last = at.depth - 1
-        mine = self.chunk(at.p)
-        for t in range(at.depth):
-            def below():
-                self.take(f"z{t}", self.z_in.at[t])
-                add_rows(self.acc.at[t, mine], self.z_in.at[t], self.t1)
-
-            def above():
-                self.take(f"e{t}", self.z_in.at[at.depth])
-                add_rows(self.acc.at[t, mine], self.z_in.at[at.depth], self.t1)
-
-            if t > 0:
-                under(at.z == t, below)
-            if t < last:
-                under(at.z == t, above)
+        if self.before is not None:
+            self.before.fin_sent()
+        own = self.of_shard(at.p)
+        if self.line_first:
+            self.plane_in_all(self.z_in)
+
+            def step(i, carry):
+                piece = pl.ds(pl.multiple_of(i * 16, 16), 16)
+                value = own[piece, :].astype(F32) + self.z_in[1, piece, :].astype(F32)
+                self.fin[piece, :] = (value + self.z_in[2, piece, :].astype(F32)).astype(BF16)
+                return carry
+
+            lax.fori_loop(0, self.t1 // 16, step, 0)
+        else:
+            self.line_in(self.z_in)
+            self.total(own, lambda j: self.z_in.at[j], self.fin)
         if self.give_credit:
-            for device in (at.x_dev, at.y_dev):
+            for device in [at.x_dev, at.y_dev] + self.others:
                 pl.semaphore_signal(self.credit, inc=1, device_id=device, device_id_type=MESH)
-            under(
-                at.z > 0,
-                lambda: pl.semaphore_signal(self.credit, inc=1, device_id=at.down(), device_id_type=MESH),
-            )
-            under(
-                at.z < last,
-                lambda: pl.semaphore_signal(self.credit, inc=1, device_id=at.up(), device_id_type=MESH),
-            )
-        self.fin[...] = self.acc[at.z, mine]
         here = self.place(at.p, at.core)
         pltpu.make_async_copy(self.fin, here, self.local).start()
         self.post("sx", self.fin, here, at.x_dev)
@@ -969,11 +1018,11 @@
 
     def release(self):
         keep = []
-        for name, src, dst, device, cond in self.posts:
+        for name, src, dst, device in self.posts:
             if name[0] == "s":
-                keep.append((name, src, dst, device, cond))
+                keep.append((name, src, dst, device))
             else:
-                under(cond, lambda: self.make(name, src, dst, device).wait_send())
+                self.make(name, src, dst, device).wait_send()
         self.posts = keep
 
     def spread_relay(self):
@@ -998,15 +1047,15 @@
         pltpu.make_async_copy(self.fin, self.place(at.p, at.core), self.local).wait()
 
     def drain(self):
-        for name, src, dst, device, cond in self.posts:
-            under(cond, lambda: self.make(name, src, dst, device).wait_send())
+        for name, src, dst, device in self.posts:
+            self.make(name, src, dst, device).wait_send()
 
     def stages(self):
-        steps = range(self.at.depth - 1)
-        out = [[self.relay], [self.combine, functools.partial(self.line, 0)]]
-        out += [[functools.partial(self.line, i)] for i in steps[1:]]
-        out += [[self.end], [self.release, self.spread_relay], [self.spread_last], [self.finish]]
-        return out
+        wait = [[] for _ in range(LINE_LAG)] if self.line_first else []
+        return wait + [
+            [self.second], [self.third], [self.end], [self.release, self.spread_relay], [self.spread_last],
+            [self.finish],
+        ]
 
 
 class KeyGrads:
@@ -1049,10 +1098,11 @@
     def core_sum(self, i):
         p = self.order[i]
         self.take(f"s{i}", self.sib_in.at[p])
-        copy = pltpu.make_async_copy(self.sib_in.at[p], self.stage, self.local)
-        copy.start()
-        copy.wait()
-        self.add(p, self.stage)
+        for s in range(self.parts.shape[2]):
+            copy = pltpu.make_async_copy(self.sib_in.at[p, s], self.stage, self.local)
+            copy.start()
+            copy.wait()
+            add_rows(self.parts.at[0, p, s], self.stage, self.parts.shape[3])
 
     def first(self):
         at = self.at
@@ -1104,17 +1154,18 @@
     kept = [dict(zip(KEPT, grab(len(KEPT)))) for _ in range(layers)]
     wholes = [grab(4) for _ in range(layers)]
     grad_in, small_out = grab(2)
-    outs = grab(layers * per_layer)
+    outs = [grab(5) for _ in range(layers)]
     kv_sib = grab(layers)
     (g_send, g_recv, g_local, g_credit, kv_send, kv_recv, kv_local, kv_credit) = grab(8)
-    (pg_send, pg_recv, pg_local, pg_credit, sm_send, sm_recv, load_sem, w_sem, kvp_sem) = grab(9)
+    (pg_send, pg_recv, pg_local, pg_credit, sm_send, sm_recv, load_sem, w_sem, kvp_sem, rest_sem) = grab(10)
     acc, plane_in, z_in, rest_acc, fin = grab(5)
-    g, hx, dn = grab(3)
-    gm, gu, ga, gq, gk, gv = grab(6)
+    hx, dn = grab(2)
+    g = grad_in
+    gm, gu, ga, gx = grab(4)
     pz, pc, po, pa = grab(4)
     dg, q, go, o, lse, bias, kvp = grab(7)
     parts, kv_stage, kv_plane = grab(3)
-    wt_a, wt_u, wt_q, gm3 = grab(4)
+    wt_a, wt_u, wt_q, gq = grab(4)
     sm, sm_sum, sm_in, sm_z, up_row = grab(5)
 
     at = Place()
@@ -1129,7 +1180,7 @@
         "down": [("pz", pz), ("gm", gm)],
         "up": [("pc", pc), ("gu", gu)],
         "out": [("po", po), ("ga", ga)],
-        "mix": [("pa", pa), ("gq", gq), ("gk", gk), ("gv", gv)],
+        "mix": [("pa", pa), ("gx", gx)],
     }
     slot_of = {}
     for kind in KINDS:
@@ -1189,14 +1240,30 @@
                 pump()
         return index
 
-    def launch(source):
+    def goal(l, unit):
+        down, up, out, mix, rest = outs[l]
+        part = width // depth
+        if unit < 4:
+            return down, part * unit, 0, wide
+        if unit < 8:
+            return up, 0, (unit - 4) * wide, wide
+        if unit == 8:
+            return out, 0, 0, wide
+        if unit < 12:
+            return mix, 0, (unit - 9) * wide, wide
+        return rest, 0, 0, wide
+
+    def launch(l, unit, source):
         index = len(items)
         s = index % SETS
         item = Granule(
-            at, index, source, plane_in.at[s], z_in.at[s], fin.at[index], outs[index],
+            at, others, unit in LINE_FIRST, source, plane_in.at[s], z_in.at[s], fin.at[index % FINS], goal(l, unit),
             g_send.at[index], g_recv.at[index], g_local.at[index], g_credit.at[index],
             g_credit.at[index - SETS] if index >= SETS else None, index + SETS < line_up,
-        )
+            items[index - FINS] if index >= FINS else None,
+        )
+        if index >= FINS:
+            assert all(entry[0] is not items[index - FINS] for entry in active)
         item.begin()
         items.append(item)
         active.append([item, item.stages()])
@@ -1212,21 +1279,43 @@
             left = piece[:, :, pl.ds(0, depth * LANES)].reshape(2 * flat, depth * LANES)
             out = over_rows(left, right).astype(BF16)
             for t in range(depth):
-                acc[s, t, :, cols] = out[t * LANES : (t + 1) * LANES]
+                acc[s, t, :, :, cols] = out[t * LANES : (t + 1) * LANES].reshape(4, LANES // 4, size)
 
             @pl.when(core == home)
             def _():
                 last = piece[:, :, pl.ds(depth * LANES, LANES)].reshape(2 * flat, LANES)
                 more = over_rows(last, right).astype(BF16)
                 for t in range(depth):
-                    rest_acc[t, pl.ds(16 * (unit - 8 * home), 16), cols] = more[t * 16 : (t + 1) * 16]
+                    u = unit - 8 * home
+                    rest_acc[t, u // 2, pl.ds(16 * (u % 2), 16), cols] = more[t * 16 : (t + 1) * 16]
 
         by_tiles(wide, 384, do)
-        launch(acc.at[s])
-
-    def rest_grad():
+        launch(l, unit, acc.at[s])
+
+    def rest_grad(l):
         open_set()
-        launch(rest_acc)
+        launch(l, 12, rest_acc)
+
+    def rest_rows(l):
+        part = width // depth
+        rest_v = gq
+        copy = pltpu.make_async_copy(outs[l][4], rest_v, rest_sem.at[0])
+        copy.start()
+        copy.wait()
+        moves = []
+        for unit in range(12):
+            ref, first, col, cols = goal(l, unit)
+            moves.append(
+                pltpu.make_async_copy(
+                    rest_v.at[pl.ds(16 * unit, 16)],
+                    ref.at[pl.ds(first + 2 * LANES, part - 2 * LANES), pl.ds(col, cols)],
+                    rest_sem.at[1 + unit],
+                )
+            )
+        for move in moves:
+            move.start()
+        for move in moves:
+            move.wait()
 
     def put_row(l, i, value):
         sm[pl.ds(l * 16 + i, 1), pl.ds(0, width)] = value
@@ -1284,17 +1373,18 @@
             )
 
         dn[...] = jnp.zeros_like(dn)
-        for copy in copies(0, 0):
-            copy.start()
+        for i in range(TILES - 1):
+            for copy in copies(i, i):
+                copy.start()
 
         def step(i, carry):
-            slot = lax.rem(i, 2)
+            slot = lax.rem(i, TILES)
             for copy in copies(i, slot):
                 copy.wait()
 
-            @pl.when(i + 1 < count)
+            @pl.when(i + TILES - 1 < count)
             def _():
-                for copy in copies(i + 1, 1 - slot):
+                for copy in copies(i + TILES - 1, lax.rem(i + TILES - 1, TILES)):
                     copy.start()
 
             cols = pl.ds(pl.multiple_of(i * tile, tile), tile)
@@ -1363,7 +1453,7 @@
             grads = across(go2, values)
             low = (probs * (grads - delta)).astype(BF16)
             dq = jnp.dot(low, keys, preferred_element_type=F32) * (HEAD_DIM ** (-0.5))
-            gq[0, here, col] = one_pair(dq, rows).astype(BF16)
+            gq[here, col] = one_pair(dq, rows).astype(BF16)
             dk = (over_rows(low, q2) * (HEAD_DIM ** (-0.5))).astype(BF16)
             dv = over_rows(probs.astype(BF16), go2).astype(BF16)
             for b in range(slots // rows):
@@ -1390,7 +1480,7 @@
 
     rest_acc[...] = jnp.zeros_like(rest_acc)
     sm[...] = jnp.zeros_like(sm)
-    for buf in (gm, gu, ga, gq, gk, gv):
+    for buf in (gm, gu, ga, gx):
         buf[0] = jnp.zeros(buf.shape[1:], BF16)
     go[...] = jnp.zeros_like(go)
     early(layers - 1)
@@ -1461,52 +1551,44 @@
         pump()
         for name in ("q", "o", "lse"):
             loads[name].wait()
-        pg_sent("gq")
         step = 3
         for first in range(0, total, step):
             attend_back(l, first, min(step, total - first))
             pump()
         keys.start()
-        pg_post("gq", gq.at[0])
-        column_sums(l, 4, gq)
         keys.first()
         pump()
         keys.relay()
         pump()
         keys.combine(l > 0)
-        pg_sent("gk")
-        pg_sent("gv")
+        pg_sent("gx")
         for s in range(seqs):
-            here = pl.ds(s * rows, rows)
-            gk[0, here, :] = parts[0, at.p, s, :, pl.ds(0, wide)]
-            gv[0, here, :] = parts[0, at.p, s, :, pl.ds(wide, wide)]
-        pg_post("gk", gk.at[0])
-        pg_post("gv", gv.at[0])
-        column_sums(l, 5, gv)
-        for i, src in enumerate((gq, gk, gv)):
 
             def join(first, size):
-                here = pl.ds(first, size)
-                gm3[here, pl.ds(i * width, width)] = src[0, here, pl.ds(0, width)]
-
-            by_tiles(flat, 64, join)
+                here, there = pl.ds(s * rows + first, size), pl.ds(first, size)
+                gx[0, here, pl.ds(0, width)] = gq[here, pl.ds(0, width)]
+                gx[0, here, pl.ds(width, width)] = parts[0, at.p, s, there, pl.ds(0, width)]
+                gx[0, here, pl.ds(2 * width, width)] = parts[0, at.p, s, there, pl.ds(wide, width)]
+
+            by_tiles(rows, 64, join)
+        pg_post("gx", gx.at[0])
+        for i, col in ((4, 0), (5, 2 * width)):
+            put_row(l, i, jnp.sum(gx[0, :, pl.ds(col, width)].astype(F32), axis=0, keepdims=True))
 
         def put_dn(first, size, value):
             dn[:, pl.ds(first, size)] = value
 
         piece_load(l, "pa").wait()
         pg_take("pa")
-        pg_take("gq")
-        weight_grad(l, 9, pa, gq, 0)
-        pg_take("gk")
-        weight_grad(l, 10, pa, gk, 0)
-        pg_take("gv")
-        weight_grad(l, 11, pa, gv, 0)
+        pg_take("gx")
+        for i in range(3):
+            weight_grad(l, 9 + i, pa, gx, i * wide)
+            pump()
         done_kind("mix", l)
-        rest_grad()
+        rest_grad(l)
         rest_item = items[-1]
         pump()
-        tiles_back(wholes[l][0], wt_q, w_sem.at[2], lambda: gm3[...], put_dn)
+        tiles_back(wholes[l][0], wt_q, w_sem.at[2], lambda: gx[0, :, pl.ds(0, 3 * width)], put_dn)
         loads["h"].wait()
         pump()
         norm_back(l, 0)
@@ -1514,12 +1596,6 @@
         while l and any(entry[0] is rest_item and len(entry[1]) > 2 for entry in active):
             pump()
 
-    def do_out(first, size):
-        here = pl.ds(first, size)
-        grad_in[here, :] = g[here, :]
-
-    by_tiles(flat, 64, do_out)
-
     def sm_copy(i, src, dst, device):
         return remote(src, dst, sm_send.at[i], sm_recv.at[i], device)
 
@@ -1529,8 +1605,8 @@
         copy.start()
         pump()
         copy.wait()
-        sm_sum[i] = current[...] + sm_in[i]
-        current = sm_sum.at[i]
+        sm_sum[i % 2] = current[...] + sm_in[i]
+        current = sm_sum.at[i % 2]
     hops = []
     for i, device in enumerate(others):
         copy = sm_copy(3 + i, current, sm_z.at[i], device)
@@ -1545,6 +1621,10 @@
         other = sm_z[jnp.minimum(slot, depth - 2)]
         small_total = small_total + jnp.where(slot == depth - 1, current[...], other)
     small_out[...] = small_total
+    for l in range(layers):
+        while any(entry[0] is items[(layers - l) * per_layer - 1] for entry in active):
+            pump()
+        rest_rows(l)
     while active:
         pump()
     for item in items:
@@ -1565,7 +1645,15 @@
     vmem = pl.BlockSpec(memory_space=pltpu.VMEM)
     struct = lambda shape, kind: jax.ShapeDtypeStruct(shape, kind)
     out_shape = [struct((flat, width), F32), struct((layers * 16, wide), F32)]
-    out_shape += [struct((2 * LANES, wide), BF16) for _ in range(count)]
+    part = width // depth
+    for _ in range(layers):
+        out_shape += [
+            struct((4 * part, wide), BF16),
+            struct((part, 4 * wide), BF16),
+            struct((part, wide), BF16),
+            struct((part, 3 * wide), BF16),
+            struct((2 * LANES, wide), BF16),
+        ]
     out_shape += [struct((4, seqs, rows, 2 * wide), BF16) for _ in range(layers)]
     dma, regular = pltpu.SemaphoreType.DMA, pltpu.SemaphoreType.REGULAR
     low = lambda *shape: pltpu.VMEM(shape, BF16)
@@ -1574,18 +1662,17 @@
     scratch = [
         dma((count, 24)), dma((count, 24)), dma((count,)), regular((count,)),
         dma((layers, 8)), dma((layers, 8)), dma, regular,
-        dma((10,)), dma((10,)), dma((10,)), regular((4,)), dma((8,)), dma((8,)), dma((8,)), dma((3, 2)), dma((2, 2)),
-        low(SETS, depth, LANES, wide), low(SETS, 3, depth, chunk, wide), low(SETS, depth + 1, chunk, wide),
-        low(depth, LANES, wide), low(count, chunk, wide),
-        full(flat, width), full(flat, width), full(flat, width),
-        low(2, flat, wide), low(2, flat, 4 * wide), low(2, flat, wide),
-        low(2, flat, wide), low(2, flat, wide), low(2, flat, wide),
+        dma((10,)), dma((10,)), dma((10,)), regular((4,)), dma((8,)), dma((8,)), dma((8,)), dma((3, TILES)), dma((2, 2)), dma((13,)),
+        low(SETS, depth, 4, chunk, wide), low(SETS, 3, depth, chunk, wide), low(SETS, depth - 1, chunk, wide),
+        low(depth, 4, chunk, wide), low(FINS, chunk, wide),
+        full(flat, width), full(flat, width),
+        low(2, flat, wide), low(2, flat, 4 * wide), low(2, flat, wide), low(2, flat, 3 * wide),
         low(2, 4, flat, PIECE), low(2, flat, PIECE), low(2, flat, PIECE), low(2, flat, PIECE),
         low(flat, ff), low(flat, wide), low(flat, wide), low(flat, wide), full(2 * flat, LANES),
         full(seqs, rows, slots), low(2, 2, slots, LANES),
-        low(2, 4, seqs, rows, 2 * wide), low(seqs, rows, 2 * wide), low(3, seqs, rows, 2 * wide),
-        low(2, 256, width), low(2, width, 256), low(2, 256, 3 * width), low(flat, 3 * width),
-        full(layers * 16, wide), full(3, layers * 16, wide), full(3, layers * 16, wide),
+        low(2, 4, seqs, rows, 2 * wide), low(rows, 2 * wide), low(3, seqs, rows, 2 * wide),
+        low(TILES, 256, width), low(TILES, width, 256), low(2, 256, 3 * width), low(flat, wide),
+        full(layers * 16, wide), full(2, layers * 16, wide), full(3, layers * 16, wide),
         full(depth - 1, layers * 16, wide), full(8, 4 * wide),
     ]
     flat_kept = [kept[l][name] for l in range(layers) for name in KEPT]
@@ -1601,19 +1688,8 @@
             collective_id=1, has_side_effects=True, vmem_limit_bytes=63 * 1024 * 1024
         ),
     )(cotangent.reshape(flat, width), lengths, vecs, *flat_kept, *flat_wholes)
-    sums = outs[2 : 2 + count]
-    grads = [sums[(layers - 1 - l) * per_layer : (layers - l) * per_layer] for l in range(layers)]
+    grads = [outs[2 + 5 * l : 6 + 5 * l] for l in range(layers)]
     return outs[0], outs[1].reshape(layers, 16, wide), grads
-
-
-def assemble(sums, width, ff):
-    rest = sums[12]
-    unit = lambda u: jnp.concatenate([sums[u], rest[16 * u : 16 * u + 16]], axis=0)
-    down = jnp.concatenate([unit(i)[:, :width] for i in range(4)], axis=0)
-    up = jnp.concatenate([unit(4 + i) for i in range(4)], axis=1)[:, :ff]
-    out = unit(8)[:, :width]
-    mix = jnp.concatenate([unit(9 + i)[:, :width] for i in range(3)], axis=1)
-    return [item.astype(F32) for item in (down, up, out, mix)]
 
 
 def normalize(values, scales, shifts):
@@ -1789,20 +1865,21 @@
         )
         up_bias = small_sums[:, 8:12].reshape(layer_total, -1)[:, :ff]
         up_part = ff // depth
-        shard_grads = [assemble(item, model_width, ff) for item in sums]
-        whole = lambda member: jnp.stack([item[member] for item in shard_grads])
+        whole = lambda member, cols: jnp.stack(
+            [item[member][:, :cols].astype(jnp.float32) for item in sums]
+        )
         return (
             activations.reshape(tokens.shape),
             grad_in.reshape(tokens.shape),
             mine(small_sums[:, 0:2]),
             mine(small_sums[:, 2:4]),
-            whole(3),
+            whole(3, 3 * model_width),
             mine(small_sums[:, 4:6]),
-            whole(2),
+            whole(2, model_width),
             mine(small_sums[:, 6]),
-            whole(1),
+            whole(1, ff),
             lax.dynamic_slice_in_dim(up_bias, lax.axis_index("fsdp") * up_part, up_part, axis=1),
-            whole(0),
+            whole(0, model_width),
             mine(small_sums[:, 7]),
         )
     weights, smalls = gather_all(

time: 1150 us -> 947 us (0.82)
  Pallas kernels: 1070 us -> 896 us
  other arithmetic: 33.2 us -> 14.1 us
    pallas_call x1, Pallas kernels: 702 us -> 554 us  [backward(): pl.pallas_call(functools.partial(backward_kernel, dims), out_shape=out_sh...]
    pallas_call x1, Pallas kernels: 365 us -> 342 us  [forward(): pl.pallas_call(functools.partial(forward_kernel, dims), out_shape=out_sha...]
    another operation x6 -> x4, other arithmetic: 28.3 us -> 14.1 us  [shards(): jnp.stack([item[member][:, :cols].astype(jnp.float32) for item in sums])]
where the time goes in v4:
time: 947 us; the launch traced here: 933 us
  Pallas kernels  896 us (95%)
  local copies, waits for them, and re-layouts  22.1 us (2%)
  other arithmetic  14.1 us (1%)
    pallas_call x1, Pallas kernels, backward(): pl.pallas_call(functools.partial(backward_kernel, dims), out_shape=out_sh...  554 us
    pallas_call x1, Pallas kernels, forward(): pl.pallas_call(functools.partial(forward_kernel, dims), out_shape=out_sha...  342 us

profile of v4, /device:TPU:9, one launch (start us, length us, event | category | flops | bytes accessed | tf_op | source)
XLA Modules:
  0.0 933.0 jit_solution(696919570913931548)
XLA Ops:
  0.6 2.1 copy.25
  2.8 0.7 copy.26
  3.4 0.7 copy.27
  4.1 0.8 reshape.49
  4.9 0.8 concatenate.3
  5.7 0.6 pad.4
  6.3 341.9 %shard_map.220 = (bf16[256,1088]{1,0:T(8,128)(2,1)}, f32[2,8,1152]{2,1,0:T(8,128)}, bf16[1088,3264]{1,0:T(8,128)(2,1)}, bf16[1088,1088]{1,0:T(8,128)(2,1)}, bf16...) custom-call(bf16[256,1088]{1,0:T(8,128)(2,1)} %bitcast.35, ...), custom_call_target="tpu_custom_call" | custom-call | tf_op jit(solution)/shard_map/pallas_call | solution.py:855
  348.2 2.1 copy.31
  350.3 1.1 copy.28
  351.4 554.0 %shard_map.221 = (f32[256,1088]{1,0:T(8,128)}, f32[32,1152]{1,0:T(8,128)}, bf16[1088,1152]{1,0:T(8,128)(2,1)}, bf16[272,4608]{1,0:T(8,128)(2,1)}, bf16[272,1152]...) custom-call(bf16[256,1088]{1,0:T(8,128)(2,1)} %bitcast.36, ...), custom_call_target="tpu_custom_call" | custom-call | tf_op jit(solution)/shard_map/pallas_call | solution.py:1680
  905.4 2.8 copy.32
  908.1 1.0 fusion.1
  909.2 0.7 constant_dynamic-slice_fusion.5
  909.8 0.7 constant_dynamic-slice_fusion.3
  910.5 1.7 slice_bitcast_fusion.4
  912.3 3.5 maximum_convert_fusion.2
  915.9 1.6 maximum_convert_fusion.3
  917.5 1.6 fusion
  919.1 0.7 constant_dynamic-slice_fusion
  920.1 4.4 maximum_convert_fusion.1
  924.5 0.9 slice_bitcast_fusion.8
  925.4 0.7 constant_dynamic-slice_fusion.1
  926.1 2.1 slice_bitcast_fusion
  928.2 4.6 maximum_convert_fusion
  (20 shorter events, 0.5 us)
Async XLA Ops:
  6.3 344.0 %copy-start.6 = (bf16[2,128,1088]{1,2,0:T(8,128)(2,1)S(1)}, bf16[2,128,1088]{1,2,0:T(8,128)(2,1)}, u32[]{:S(2)}) copy-start(bf16[2,128,1088]{1,2,0:T(8,128)(2,1)} %param.15) | copy-start | bytes 1671172
  905.4 5.2 copy-start.3
  912.3 3.5 copy-start.4
  912.3 3.5 copy-start.5
  915.8 4.0 copy-start.2
  915.9 3.9 copy-start.1
  920.1 6.0 copy-start

commit v5 on v4

--- a/solution.py
+++ b/solution.py
@@ -178,9 +178,8 @@
 
         self.cases(step, do)
 
-    def finish(self):
+    def finish(self, step, then):
         at = self.at
-        mine = self.t1_rows(at.p)
 
         def do(shard, onward, device):
             self.copy(6, shard, self.block_rows(1 - at.core), at.sib).wait_recv()
@@ -189,8 +188,9 @@
             def _():
                 self.copy(5, shard, self.rest, at.sib).wait_recv()
 
-        for step in range(at.depth - 1):
-            self.cases(step, do)
+            then(shard)
+
+        self.cases(step, do)
 
     def drain(self):
         at = self.at
@@ -345,7 +345,7 @@
         self.names, self.posts = {}, []
 
     def place(self, p, core):
-        return self.whole.at[:, pl.ds(pl.multiple_of((2 * p + core) * self.rows, 16), self.rows)]
+        return self.whole.at[pl.ds(pl.multiple_of((2 * p + core) * self.rows, 16), self.rows)]
 
     def make(self, name, src, dst, device):
         i = self.names.setdefault(name, len(self.names))
@@ -398,6 +398,8 @@
 KEPT = ("h", "pa", "q", "kv", "o", "po", "lse", "h1", "pc", "pz", "dg")
 PIECE = 5 * LANES
 LINE_ROWS = (0, 0, 16, 16)
+SHARE_LAG, FINISH_LAG = 0, 1
+TICKS = (2, 2, 2, 2)
 
 
 def kept_shapes(seqs, slots, rows, width, ff):
@@ -492,7 +494,13 @@
     owns = [ref.at[l] for l in range(layers) for ref in (w_qkv, w_out, w_up, w_down)]
     items = [Gather(at, owns[k], wholes[k], k % 2, send.at[k], recv.at[k], LINE_ROWS[k % 4]) for k in range(4 * layers)]
     contexts = [
-        Context(at, own_kv, kept[l]["kv"], rows, kv_send.at[l], kv_recv.at[l], keep_sem.at[l, len(KEPT)])
+        [
+            Context(
+                at, own_kv.at[s], kept[l]["kv"].at[s], rows, kv_send.at[l, s], kv_recv.at[l, s],
+                keep_sem.at[l, len(KEPT) + s],
+            )
+            for s in range(seqs)
+        ]
         for l in range(layers)
     ]
     pending = {}
@@ -528,11 +536,17 @@
     def own_done(k):
         own_copy(k, False).wait()
 
-    def fetch(k):
-        pltpu.make_async_copy(wholes[k], buffer(k), load_sem.at[k]).start()
+    def fetch_copy(k, shard):
+        r = owns[k].shape[0]
+        here = pl.ds(pl.multiple_of(shard * r, 16), r)
+        return pltpu.make_async_copy(wholes[k].at[here], buffer(k).at[here], load_sem.at[k, shard])
+
+    def fetch(k, shard):
+        fetch_copy(k, shard).start()
 
     def ready(k):
-        pltpu.make_async_copy(wholes[k], buffer(k), load_sem.at[k]).wait()
+        for shard in range(depth):
+            fetch_copy(k, shard).wait()
 
     def small_copy(shard, device, src=None, second=False):
         return remote(
@@ -681,18 +695,24 @@
             by_tiles(rows, 32, do)
 
     steps = depth - 1
-    ticks = []
-    for k in range(4 * layers):
-        if k == 0:
-            ticks += [functools.partial(items[0].arrive, i) for i in range(steps)]
-        if k + 2 < 4 * layers:
-            ticks.append(items[k + 2].start)
-        for i in range(steps):
+    ticks = [functools.partial(items[0].arrive, i) for i in range(steps)]
+    last = 4 * layers * steps
+    for n in range(last + FINISH_LAG):
+        k, i = divmod(n, steps)
+        if n < last:
+            if i == 0 and k + 2 < 4 * layers:
+                ticks.append(items[k + 2].start)
             ticks.append(functools.partial(items[k].plane, i))
             if k + 1 < 4 * layers:
                 ticks.append(functools.partial(items[k + 1].arrive, i))
+        if 0 <= n - SHARE_LAG < last:
+            k, i = divmod(n - SHARE_LAG, steps)
             ticks.append(functools.partial(items[k].share, i))
-        ticks.append(("end", k))
+        if n >= FINISH_LAG:
+            k, i = divmod(n - FINISH_LAG, steps)
+            ticks.append(("shard", k, i))
+            if i == steps - 1:
+                ticks.append(("end", k))
 
     def tick(n):
         for _ in range(n):
@@ -700,7 +720,9 @@
                 return
             item = ticks.pop(0)
             if isinstance(item, tuple) and item[0] == "end":
-                items[item[1]].finish()
+                fetch(item[1], at.z)
+            elif isinstance(item, tuple):
+                items[item[1]].finish(item[2], functools.partial(fetch, item[1]))
             else:
                 item()
 
@@ -734,33 +756,33 @@
         cut_pieces(a, pa, part, 0)
         keep(l, "pa", pa)
         reach(k)
-        fetch(k)
         free(l - 1, "q")
         if l:
-            contexts[l - 1].drain(True)
+            for context in contexts[l - 1]:
+                context.drain(True)
         ready(k)
         mix(l)
-        contexts[l].start()
+        for context in contexts[l]:
+            context.start()
         keep(l, "q", q)
-        tick(8)
-        contexts[l].relay()
-        reach(k + 1)
-        fetch(k + 1)
-        tick(4)
-        contexts[l].last()
-        tick(3)
-        contexts[l].finish()
-        seen = pltpu.make_async_copy(kept[l]["kv"], kv, load_sem.at[4 * layers])
-        seen.start()
         free(l - 1, "o")
         free(l - 1, "lse")
-        seen.wait()
-        half = pairs // 2
-        for s in range(seqs):
-            attend(s, 0, half, q, kv, bias, o, lse, rows, pairs, wide)
-            tick(2)
-            attend(s, half, pairs - half, q, kv, bias, o, lse, rows, pairs, wide)
-            tick(2)
+        for context in contexts[l]:
+            tick(TICKS[0])
+            context.relay()
+        for s, context in enumerate(contexts[l]):
+            tick(TICKS[1])
+            context.last()
+            tick(TICKS[2])
+            context.finish()
+            seen = pltpu.make_async_copy(kept[l]["kv"].at[s], kv.at[s], load_sem.at[4 * layers, s])
+            seen.start()
+            seen.wait()
+            first = 0
+            for count in (pairs // 3, pairs // 3, pairs - 2 * (pairs // 3)):
+                attend(s, first, count, q, kv, bias, o, lse, rows, pairs, wide)
+                first += count
+                tick(TICKS[3])
         keep(l, "o", o)
         keep(l, "lse", lse)
         free(l - 1, "po")
@@ -775,7 +797,6 @@
         cut_pieces(c, pc, part, 0)
         keep(l, "pc", pc)
         reach(k + 2)
-        fetch(k + 2)
         ready(k + 2)
         free(l - 1, "dg")
         rise(l)
@@ -785,7 +806,6 @@
             cut_pieces(z, pz.at[:, i], part, i)
         keep(l, "pz", pz)
         reach(k + 3)
-        fetch(k + 3)
         free(l, "h")
         ready(k + 3)
         fall(l)
@@ -796,9 +816,11 @@
     small_drain()
     for item in items:
         item.drain()
-    contexts[-1].drain(True)
-    for context in contexts:
-        context.drain(False)
+    for context in contexts[-1]:
+        context.drain(True)
+    for of_layer in contexts:
+        for context in of_layer:
+            context.drain(False)
 
 
 def forward(tokens, lengths, w_qkv, w_out, w_up, w_down, small):
@@ -826,10 +848,10 @@
         dma((count, 8 * depth)),
         dma((depth + 1,)),
         dma((depth,)),
-        dma((layers, 8)),
-        dma((layers, 8)),
-        dma((count + 1,)),
-        dma((layers, len(KEPT) + 1)),
+        dma((layers, seqs, 8)),
+        dma((layers, seqs, 8)),
+        dma((count + 1, depth)),
+        dma((layers, len(KEPT) + seqs)),
         dma((3, count)),
         pltpu.VMEM((depth,) + small.shape, BF16),
         pltpu.VMEM((layers, 8, wide), F32),
@@ -1091,18 +1113,15 @@
         return [at.p_d, direct, relay, at.p]
 
     def add(self, p, extra):
-        seqs, rows = self.parts.shape[2], self.parts.shape[3]
-        for s in range(seqs):
-            add_rows(self.parts.at[0, p, s], extra.at[s], rows)
+        add_rows(self.parts.at[0, p], extra, self.parts.shape[2])
 
     def core_sum(self, i):
         p = self.order[i]
         self.take(f"s{i}", self.sib_in.at[p])
-        for s in range(self.parts.shape[2]):
-            copy = pltpu.make_async_copy(self.sib_in.at[p, s], self.stage, self.local)
-            copy.start()
-            copy.wait()
-            add_rows(self.parts.at[0, p, s], self.stage, self.parts.shape[3])
+        copy = pltpu.make_async_copy(self.sib_in.at[p], self.stage, self.local)
+        copy.start()
+        copy.wait()
+        self.add(p, self.stage)
 
     def first(self):
         at = self.at
@@ -1123,11 +1142,9 @@
 
     def combine(self, give_credit):
         at = self.at
-        seqs, rows = self.parts.shape[2], self.parts.shape[3]
         self.take("near", self.plane_in.at[1])
         self.take("relay", self.plane_in.at[2])
-        for s in range(seqs):
-            add_rows_two(self.parts.at[0, at.p, s], self.plane_in.at[1, s], self.plane_in.at[2, s], rows)
+        add_rows_two(self.parts.at[0, at.p], self.plane_in.at[1], self.plane_in.at[2], self.parts.shape[2])
         if give_credit:
             for device in (at.x_dev, at.y_dev):
                 pl.semaphore_signal(self.credit, inc=1, device_id=device, device_id_type=MESH)
@@ -1221,7 +1238,7 @@
                 pg_credit.at[KINDS.index(kind)], inc=1, device_id=at.sib, device_id_type=MESH
             )
 
-    active, items = [], []
+    active, items, rest_done = [], [], []
     line_up = layers * per_layer
 
     def pump(times=1):
@@ -1246,18 +1263,20 @@
         if unit < 4:
             return down, part * unit, 0, wide
         if unit < 8:
-            return up, 0, (unit - 4) * wide, wide
+            return up, 0, (unit - 4) * wide, min(wide, ff - (unit - 4) * wide)
         if unit == 8:
             return out, 0, 0, wide
         if unit < 12:
-            return mix, 0, (unit - 9) * wide, wide
+            return mix, 0, (unit - 9) * wide, min(wide, pad_lanes(3 * width) - (unit - 9) * wide)
         return rest, 0, 0, wide
 
     def launch(l, unit, source):
         index = len(items)
         s = index % SETS
+        cols = pl.ds(0, goal(l, unit)[3])
         item = Granule(
-            at, others, unit in LINE_FIRST, source, plane_in.at[s], z_in.at[s], fin.at[index % FINS], goal(l, unit),
+            at, others, unit in LINE_FIRST, source.at[:, :, :, cols], plane_in.at[s, :, :, :, cols],
+            z_in.at[s, :, :, cols], fin.at[index % FINS, :, cols], goal(l, unit),
             g_send.at[index], g_recv.at[index], g_local.at[index], g_credit.at[index],
             g_credit.at[index - SETS] if index >= SETS else None, index + SETS < line_up,
             items[index - FINS] if index >= FINS else None,
@@ -1307,7 +1326,7 @@
             ref, first, col, cols = goal(l, unit)
             moves.append(
                 pltpu.make_async_copy(
-                    rest_v.at[pl.ds(16 * unit, 16)],
+                    rest_v.at[pl.ds(16 * unit, 16), pl.ds(0, cols)],
                     ref.at[pl.ds(first + 2 * LANES, part - 2 * LANES), pl.ds(col, cols)],
                     rest_sem.at[1 + unit],
                 )
@@ -1459,8 +1478,8 @@
             for b in range(slots // rows):
                 mine = lax.rem(b + core, 2)
                 span = slice(b * rows, (b + 1) * rows)
-                parts[mine, b // 2, s, :, col] = dk[span]
-                parts[mine, b // 2, s, :, col_v] = dv[span]
+                parts[s, mine, b // 2, :, col] = dk[span]
+                parts[s, mine, b // 2, :, col_v] = dv[span]
             return carry
 
         lax.fori_loop(first, first + count, step, 0)
@@ -1480,9 +1499,10 @@
 
     rest_acc[...] = jnp.zeros_like(rest_acc)
     sm[...] = jnp.zeros_like(sm)
-    for buf in (gm, gu, ga, gx):
-        buf[0] = jnp.zeros(buf.shape[1:], BF16)
-    go[...] = jnp.zeros_like(go)
+    for buf, used in ((gm, width), (gu, ff), (ga, width), (gx, 3 * width)):
+        first = used // LANES * LANES
+        buf[0, :, pl.ds(first, buf.shape[2] - first)] = jnp.zeros((flat, buf.shape[2] - first), BF16)
+    go[:, pl.ds(wide - LANES, LANES)] = jnp.zeros((flat, LANES), BF16)
     early(layers - 1)
     for s in range(seqs):
 
@@ -1495,10 +1515,13 @@
     key_bias(bias, seqs, rows, slots, lengths, at.c8)
 
     for l in reversed(range(layers)):
-        keys = KeyGrads(
-            at, parts, kv_sib[l], kv_stage, kv_plane, kv_send.at[l], kv_recv.at[l], kv_local,
-            kv_credit, None if l == layers - 1 else l,
-        )
+        keys = [
+            KeyGrads(
+                at, parts.at[s], kv_sib[l].at[s], kv_stage, kv_plane.at[s], kv_send.at[l, s], kv_recv.at[l, s],
+                kv_local, kv_credit.at[s], None if l == layers - 1 else l,
+            )
+            for s in range(seqs)
+        ]
         if l < layers - 1:
             early(l)
         pg_sent("gm")
@@ -1549,26 +1572,34 @@
         weight_grad(l, 8, po, ga, 0)
         done_kind("out", l)
         pump()
+        if l < layers - 1 and all(entry[0] is not items[per_layer * (layers - 1 - l) - 1] for entry in active):
+            rest_rows(l + 1)
+            rest_done.append(l + 1)
         for name in ("q", "o", "lse"):
             loads[name].wait()
-        step = 3
-        for first in range(0, total, step):
-            attend_back(l, first, min(step, total - first))
-            pump()
-        keys.start()
-        keys.first()
-        pump()
-        keys.relay()
-        pump()
-        keys.combine(l > 0)
+        steps = []
+        for s in range(seqs):
+            third = pairs // 3
+            pieces = [(s * pairs, third), (s * pairs + third, third), (s * pairs + 2 * third, pairs - 2 * third)]
+            for piece in pieces:
+                attend_back(l, *piece)
+                pump()
+                if steps:
+                    steps.pop(0)()
+            steps += [keys[s].start, keys[s].first, keys[s].relay, functools.partial(keys[s].combine, l > 0)]
+            steps.pop(0)()
+        while steps:
+            steps.pop(0)()
+            if steps:
+                pump()
         pg_sent("gx")
         for s in range(seqs):
 
             def join(first, size):
                 here, there = pl.ds(s * rows + first, size), pl.ds(first, size)
                 gx[0, here, pl.ds(0, width)] = gq[here, pl.ds(0, width)]
-                gx[0, here, pl.ds(width, width)] = parts[0, at.p, s, there, pl.ds(0, width)]
-                gx[0, here, pl.ds(2 * width, width)] = parts[0, at.p, s, there, pl.ds(wide, width)]
+                gx[0, here, pl.ds(width, width)] = parts[s, 0, at.p, there, pl.ds(0, width)]
+                gx[0, here, pl.ds(2 * width, width)] = parts[s, 0, at.p, there, pl.ds(wide, width)]
 
             by_tiles(rows, 64, join)
         pg_post("gx", gx.at[0])
@@ -1592,7 +1623,8 @@
         loads["h"].wait()
         pump()
         norm_back(l, 0)
-        keys.drain()
+        for item in keys:
+            item.drain()
         while l and any(entry[0] is rest_item and len(entry[1]) > 2 for entry in active):
             pump()
 
@@ -1624,7 +1656,8 @@
     for l in range(layers):
         while any(entry[0] is items[(layers - l) * per_layer - 1] for entry in active):
             pump()
-        rest_rows(l)
+        if l not in rest_done:
+            rest_rows(l)
     while active:
         pump()
     for item in items:
@@ -1654,14 +1687,14 @@
             struct((part, 3 * wide), BF16),
             struct((2 * LANES, wide), BF16),
         ]
-    out_shape += [struct((4, seqs, rows, 2 * wide), BF16) for _ in range(layers)]
+    out_shape += [struct((seqs, 4, rows, 2 * wide), BF16) for _ in range(layers)]
     dma, regular = pltpu.SemaphoreType.DMA, pltpu.SemaphoreType.REGULAR
     low = lambda *shape: pltpu.VMEM(shape, BF16)
     full = lambda *shape: pltpu.VMEM(shape, F32)
     chunk = LANES // 4
     scratch = [
         dma((count, 24)), dma((count, 24)), dma((count,)), regular((count,)),
-        dma((layers, 8)), dma((layers, 8)), dma, regular,
+        dma((layers, seqs, 8)), dma((layers, seqs, 8)), dma, regular((seqs,)),
         dma((10,)), dma((10,)), dma((10,)), regular((4,)), dma((8,)), dma((8,)), dma((8,)), dma((3, TILES)), dma((2, 2)), dma((13,)),
         low(SETS, depth, 4, chunk, wide), low(SETS, 3, depth, chunk, wide), low(SETS, depth - 1, chunk, wide),
         low(depth, 4, chunk, wide), low(FINS, chunk, wide),
@@ -1670,7 +1703,7 @@
         low(2, 4, flat, PIECE), low(2, flat, PIECE), low(2, flat, PIECE), low(2, flat, PIECE),
         low(flat, ff), low(flat, wide), low(flat, wide), low(flat, wide), full(2 * flat, LANES),
         full(seqs, rows, slots), low(2, 2, slots, LANES),
-        low(2, 4, seqs, rows, 2 * wide), low(rows, 2 * wide), low(3, seqs, rows, 2 * wide),
+        low(seqs, 2, 4, rows, 2 * wide), low(rows, 2 * wide), low(seqs, 3, rows, 2 * wide),
         low(TILES, 256, width), low(TILES, width, 256), low(2, 256, 3 * width), low(flat, wide),
         full(layers * 16, wide), full(2, layers * 16, wide), full(3, layers * 16, wide),
         full(depth - 1, layers * 16, wide), full(8, 4 * wide),

time: 947 us -> 924 us (0.976)
  Pallas kernels: 896 us -> 873 us
    pallas_call x1, Pallas kernels: 342 us -> 318 us  [forward(): pl.pallas_call(functools.partial(forward_kernel, dims), out_shape=out_sha...]
where the time goes in v5:
time: 924 us; the launch traced here: 910 us
  Pallas kernels  873 us (94%)
  local copies, waits for them, and re-layouts  22.1 us (2%)
  other arithmetic  14.1 us (2%)
    pallas_call x1, Pallas kernels, backward(): pl.pallas_call(functools.partial(backward_kernel, dims), out_shape=out_sh...  555 us
    pallas_call x1, Pallas kernels, forward(): pl.pallas_call(functools.partial(forward_kernel, dims), out_shape=out_sha...  318 us

profile of v5, /device:TPU:9, one launch (start us, length us, event | category | flops | bytes accessed | tf_op | source)
XLA Modules:
  0.0 910.3 jit_solution(11226869756231974646)
XLA Ops:
  0.6 2.1 copy.25
  2.8 0.7 copy.26
  3.4 0.7 copy.27
  4.1 0.8 reshape.49
  4.9 0.8 concatenate.3
  5.7 0.6 pad.4
  6.3 317.7 %shard_map.220 = (bf16[256,1088]{1,0:T(8,128)(2,1)}, f32[2,8,1152]{2,1,0:T(8,128)}, bf16[1088,3264]{1,0:T(8,128)(2,1)}, bf16[1088,1088]{1,0:T(8,128)(2,1)}, bf16...) custom-call(bf16[256,1088]{1,0:T(8,128)(2,1)} %bitcast.35, ...), custom_call_target="tpu_custom_call" | custom-call | tf_op jit(solution)/shard_map/pallas_call | solution.py:877
  324.0 2.1 copy.31
  326.1 1.1 copy.28
  327.2 555.2 %shard_map.221 = (f32[256,1088]{1,0:T(8,128)}, f32[32,1152]{1,0:T(8,128)}, bf16[1088,1152]{1,0:T(8,128)(2,1)}, bf16[272,4608]{1,0:T(8,128)(2,1)}, bf16[272,1152]...) custom-call(bf16[256,1088]{1,0:T(8,128)(2,1)} %bitcast.36, ...), custom_call_target="tpu_custom_call" | custom-call | tf_op jit(solution)/shard_map/pallas_call | solution.py:1713
  882.4 2.8 copy.32
  885.2 1.0 fusion.1
  886.2 0.7 constant_dynamic-slice_fusion.5
  886.9 0.7 constant_dynamic-slice_fusion.3
  887.6 1.7 slice_bitcast_fusion.4
  889.3 3.5 maximum_convert_fusion.2
  892.9 1.6 maximum_convert_fusion.3
  894.6 1.6 fusion
  896.2 0.7 constant_dynamic-slice_fusion
  897.2 4.4 maximum_convert_fusion.1
  901.6 0.9 slice_bitcast_fusion.8
  902.5 0.7 constant_dynamic-slice_fusion.1
  903.2 2.1 slice_bitcast_fusion
  905.3 4.6 maximum_convert_fusion
  (20 shorter events, 0.5 us)
Async XLA Ops:
  6.3 319.8 %copy-start.6 = (bf16[2,128,1088]{1,2,0:T(8,128)(2,1)S(1)}, bf16[2,128,1088]{1,2,0:T(8,128)(2,1)}, u32[]{:S(2)}) copy-start(bf16[2,128,1088]{1,2,0:T(8,128)(2,1)} %param.15) | copy-start | bytes 1671172
  882.4 5.2 copy-start.3
  889.3 3.5 copy-start.4
  889.3 3.5 copy-start.5
  892.8 4.0 copy-start.2
  892.9 3.9 copy-start.1
  897.2 6.0 copy-start

commit v6 on v5

--- a/solution.py
+++ b/solution.py
@@ -397,7 +397,7 @@
 
 KEPT = ("h", "pa", "q", "kv", "o", "po", "lse", "h1", "pc", "pz", "dg")
 PIECE = 5 * LANES
-LINE_ROWS = (0, 0, 16, 16)
+LINE_ROWS = (0, 0, 16, 0)
 SHARE_LAG, FINISH_LAG = 0, 1
 TICKS = (2, 2, 2, 2)
 

time: 924 us -> 931 us (level)
  no operation moved by 1% of the time
where the time goes in v6:
time: 931 us; the launch traced here: 916 us
  Pallas kernels  878 us (94%)
  local copies, waits for them, and re-layouts  22.1 us (2%)
  other arithmetic  14.1 us (2%)
    pallas_call x1, Pallas kernels, backward(): pl.pallas_call(functools.partial(backward_kernel, dims), out_shape=out_sh...  554 us
    pallas_call x1, Pallas kernels, forward(): pl.pallas_call(functools.partial(forward_kernel, dims), out_shape=out_sha...  324 us

profile of v6, /device:TPU:9, one launch (start us, length us, event | category | flops | bytes accessed | tf_op | source)
XLA Modules:
  0.0 915.7 jit_solution(7768075719971230025)
XLA Ops:
  0.6 2.1 copy.25
  2.8 0.7 copy.26
  3.4 0.7 copy.27
  4.1 0.8 reshape.49
  4.9 0.8 concatenate.3
  5.7 0.6 pad.4
  6.3 324.4 %shard_map.220 = (bf16[256,1088]{1,0:T(8,128)(2,1)}, f32[2,8,1152]{2,1,0:T(8,128)}, bf16[1088,3264]{1,0:T(8,128)(2,1)}, bf16[1088,1088]{1,0:T(8,128)(2,1)}, bf16...) custom-call(bf16[256,1088]{1,0:T(8,128)(2,1)} %bitcast.35, ...), custom_call_target="tpu_custom_call" | custom-call | tf_op jit(solution)/shard_map/pallas_call | solution.py:877
  330.7 2.1 copy.31
  332.8 1.1 copy.28
  333.9 553.9 %shard_map.221 = (f32[256,1088]{1,0:T(8,128)}, f32[32,1152]{1,0:T(8,128)}, bf16[1088,1152]{1,0:T(8,128)(2,1)}, bf16[272,4608]{1,0:T(8,128)(2,1)}, bf16[272,1152]...) custom-call(bf16[256,1088]{1,0:T(8,128)(2,1)} %bitcast.36, ...), custom_call_target="tpu_custom_call" | custom-call | tf_op jit(solution)/shard_map/pallas_call | solution.py:1713
  887.8 2.8 copy.32
  890.5 1.0 fusion.1
  891.6 0.7 constant_dynamic-slice_fusion.5
  892.2 0.7 constant_dynamic-slice_fusion.3
  892.9 1.7 slice_bitcast_fusion.4
  894.7 3.5 maximum_convert_fusion.2
  898.3 1.6 maximum_convert_fusion.3
  899.9 1.6 fusion
  901.5 0.7 constant_dynamic-slice_fusion
  902.5 4.4 maximum_convert_fusion.1
  906.9 0.9 slice_bitcast_fusion.8
  907.8 0.7 constant_dynamic-slice_fusion.1
  908.5 2.1 slice_bitcast_fusion
  910.6 4.6 maximum_convert_fusion
  (20 shorter events, 0.5 us)
Async XLA Ops:
  6.3 326.5 %copy-start.6 = (bf16[2,128,1088]{1,2,0:T(8,128)(2,1)S(1)}, bf16[2,128,1088]{1,2,0:T(8,128)(2,1)}, u32[]{:S(2)}) copy-start(bf16[2,128,1088]{1,2,0:T(8,128)(2,1)} %param.15) | copy-start | bytes 1671172
  887.8 5.2 copy-start.3
  894.6 3.5 copy-start.4
  894.7 3.5 copy-start.5
  898.2 4.0 copy-start.2
  898.3 3.9 copy-start.1
  902.5 6.0 copy-start
